TPU v7x, 256 devices: a whole 4x4x8 slice. The times are simulated.
256 devices in a mesh: dp: 16 (over z_lo, x, core), expert: 16 (over z_hi, y).
Axes of the slice: x: 4, y: 4, z: 8 (z_hi: 4, z_lo: 2; z = z_hi * 2 + z_lo), core: 2. Of those that a mesh axis runs over, the one named last changes fastest.
Arguments:
- tokens: bfloat16 [32768, 3584], P(('dp', 'expert')), may hold values from -6 to 6
- out_grad: bfloat16 [32768, 3584], P(('dp', 'expert')), may hold values from -6 to 6
- routes: int32 [32768, 2], P(('dp', 'expert')), may hold values from 0 to 15, all different within a row; in each aligned block of 128 rows (0 to 127, 128 to 255, ...) at most 20 rows name the same one
- probs: bfloat16 [32768, 2], P(('dp', 'expert')), may hold values from 0.099609375 to 1
- swap_flags: int32 [16], replicated, may hold values from 0 to 1, as said below
- up_weight: bfloat16 [16, 1024, 3584], P('expert', 'dp'), may hold values from -4 to 4
- down_weight: bfloat16 [16, 1024, 3584], P('expert', 'dp'), may hold values from -4 to 4
- up_first: float32 [16, 1024, 3584], P('expert', 'dp'), may hold values from -3 to 3
- up_second: float32 [16, 1024, 3584], P('expert', 'dp'), may hold values from 0.02 to 0.3
- down_first: float32 [16, 1024, 3584], P('expert', 'dp'), may hold values from -3 to 3
- down_second: float32 [16, 1024, 3584], P('expert', 'dp'), may hold values from 0.02 to 0.3
Outputs:
- token_grad: bfloat16 [32768, 3584], P(('dp', 'expert'))
- new_up_weight: bfloat16 [16, 1024, 3584], P('expert', 'dp')
- new_down_weight: bfloat16 [16, 1024, 3584], P('expert', 'dp')
- new_up_first: float32 [16, 1024, 3584], P('expert', 'dp')
- new_up_second: float32 [16, 1024, 3584], P('expert', 'dp')
- new_down_first: float32 [16, 1024, 3584], P('expert', 'dp')
- new_down_second: float32 [16, 1024, 3584], P('expert', 'dp')
Inputs may be any that keep to these rules, and one draw needn't show every extreme that they name: `routes`: each row names 2 different experts. Within the 128 rows of one device no expert is named by more than 20 rows, a bound that some block reaches. swap_flags[s] equals swap_flags[s XOR (8)]; the slots 16 // 2 - 1 and 15 always trade places.
All inputs are finite; a program needn't handle non-finite values.
Results may differ from a plain program's by a relative error of at most 0.022.
Values may be sent and summed in bfloat16 or wider, within the bound.
No kernel may reach another device: no remote copies, remote signals or barrier semaphores. Data moves between devices by JAX's collectives and lax.ppermute only.
A program may use at most 128 MiB of HBM per device.

v0:
```python
import functools

import jax
import jax.numpy as jnp
from jax import lax
from jax.experimental import pallas as pl
from jax.experimental.pallas import tpu as pltpu
from jax.sharding import Mesh
from jax.sharding import PartitionSpec as P

ADAM_STEP = 20


beta_first = 0.9
beta_second = 0.95
step_size = 0.05
adam_epsilon = 1e-08

NEAR = "near"
RING = "ring"
CORE = "core"
HIGH = "high"
SIDE = "side"
HIGHS = 4


def partner(array, axis, flip):
    return lax.ppermute(array, axis, [(i, i ^ flip) for i in range(lax.axis_size(axis))])


def z_routes():
    routes = []
    for step, crosses in ((1, False), (-1, True), (2, True)):
        pairs = []
        for near in range(2):
            sign = 1 if near == 0 else -1
            for high in range(HIGHS):
                other = (1 - near) if crosses else near
                pairs.append((near * HIGHS + high, other * HIGHS + (high + sign * step) % HIGHS))
        routes.append(pairs)
    return routes


def adam_update(weight, first, second, gradient):
    first_new = beta_first * first + (1.0 - beta_first) * gradient
    second_new = beta_second * second + (1.0 - beta_second) * gradient * gradient
    corr_first = 1.0 - beta_first**ADAM_STEP
    corr_second = 1.0 - beta_second**ADAM_STEP
    stepped = weight.astype(jnp.float32) - step_size * (first_new / corr_first) / (
        jnp.sqrt(second_new / corr_second) + adam_epsilon
    )
    return (stepped.astype(jnp.bfloat16), first_new, second_new)


def dispatch_kernel(
    capacity,
    flags_ref,
    routes_ref,
    probs_ref,
    tokens_ref,
    out_grad_ref,
    token_rows_ref,
    scaled_rows_ref,
    select_ref,
):
    count, tops = routes_ref.shape
    experts = flags_ref.shape[1]
    rows, width = token_rows_ref.shape
    side = experts // HIGHS
    half_axis = experts // 2
    my_high = lax.axis_index(HIGH)
    my_near = lax.axis_index(NEAR)
    ids = lax.broadcasted_iota(jnp.int32, (1, experts), 1)
    slot = jnp.where(flags_ref[...] == 1, jnp.bitwise_xor(ids, half_axis), ids)
    away = lax.shift_right_logical(slot, side.bit_length() - 1) - my_high
    away = jnp.bitwise_and(jnp.where(my_near == 0, away, -away), HIGHS - 1)
    block = jnp.where(away >= 2, 5 - away, away)
    base = jnp.bitwise_and(slot, side - 1) * (HIGHS * capacity) + block * capacity
    base = base.astype(jnp.float32)
    expert_ids = lax.broadcasted_iota(jnp.int32, (count, experts), 1)
    below = (
        lax.broadcasted_iota(jnp.int32, (count, count), 0)
        > lax.broadcasted_iota(jnp.int32, (count, count), 1)
    )
    below = jnp.where(below, 1.0, 0.0).astype(jnp.bfloat16)
    padded = -(-rows // 128) * 128
    row_ids = lax.broadcasted_iota(jnp.int32, (count, padded), 1)
    token_select = jnp.zeros((count, padded), jnp.float32)
    prob_select = jnp.zeros((count, padded), jnp.float32)
    for k in range(tops):
        onehot = jnp.where(routes_ref[:, k : k + 1] == expert_ids, 1.0, 0.0)
        earlier = jnp.dot(below, onehot.astype(jnp.bfloat16), preferred_element_type=jnp.float32)
        row = jnp.sum(onehot * (base + earlier), axis=1, keepdims=True).astype(jnp.int32)
        hit = row_ids == row
        token_select = token_select + jnp.where(hit, 1.0, 0.0)
        prob = probs_ref[:, k : k + 1].astype(jnp.float32)
        prob_select = prob_select + jnp.where(hit, prob, 0.0)
        base = base + jnp.sum(onehot, axis=0, keepdims=True)
    select_ref[...] = token_select[:, :rows].astype(jnp.bfloat16)
    token_pick = token_select.T[:rows].astype(jnp.bfloat16)
    prob_pick = prob_select.T[:rows].astype(jnp.bfloat16)
    piece = 512
    for at in range(0, width, piece):
        cut = slice(at, min(at + piece, width))
        for pick, source, target in (
            (token_pick, tokens_ref, token_rows_ref),
            (prob_pick, out_grad_ref, scaled_rows_ref),
        ):
            target[:, cut] = jnp.dot(
                pick, source[:, cut], preferred_element_type=jnp.float32
            ).astype(jnp.bfloat16)


def dispatch(swap_flags, routes, probs, tokens, out_grad, capacity):
    count, width = tokens.shape
    rows = swap_flags.shape[0] * capacity
    whole = pl.BlockSpec(memory_space=pltpu.VMEM)
    return pl.pallas_call(
        functools.partial(dispatch_kernel, capacity),
        in_specs=[whole] * 5,
        out_specs=[whole] * 3,
        out_shape=[
            jax.ShapeDtypeStruct((rows, width), jnp.bfloat16),
            jax.ShapeDtypeStruct((rows, width), jnp.bfloat16),
            jax.ShapeDtypeStruct((count, rows), jnp.bfloat16),
        ],
        compiler_params=pltpu.CompilerParams(vmem_limit_bytes=24 * 1024 * 1024),
        cost_estimate=pl.CostEstimate(flops=0, bytes_accessed=1024, transcendentals=0),
    )(swap_flags.reshape(1, -1), routes, probs, tokens, out_grad)


def expert_kernel(
    steps,
    inv_model,
    inv_hidden,
    mine_ref,
    other_ref,
    mine_scaled_ref,
    other_scaled_ref,
    weight_ref,
    part_ref,
    pair_ref,
    pair_other_ref,
    pre_ref,
    back_ref,
    delta_ref,
    delta_turned_ref,
    activ_turned_ref,
):
    step = pl.program_id(0)
    chips, both, _ = weight_ref.shape
    local = both // 2
    rows = mine_ref.shape[0]
    contract_last = (((1,), (1,)), ((), ()))
    up = jnp.concatenate([weight_ref[i, :local] for i in range(chips)], axis=0)

    @pl.when(step == 0)
    def _():
        pre_ref[...] = jnp.zeros_like(pre_ref)
        back_ref[...] = jnp.zeros_like(back_ref)

    @pl.when(step < steps)
    def _():
        down = jnp.concatenate([weight_ref[i, local:] for i in range(chips)], axis=0)
        for at, token, scaled in (
            (0, mine_ref, mine_scaled_ref),
            (rows, other_ref, other_scaled_ref),
        ):
            pre_ref[at : at + rows] += lax.dot_general(
                token[...], up, contract_last, preferred_element_type=jnp.float32
            )
            back_ref[at : at + rows] += lax.dot_general(
                scaled[...], down, contract_last, preferred_element_type=jnp.float32
            )

    @pl.when(step == steps - 1)
    def _():
        pre_act = pre_ref[...] * inv_model
        sigmoid_act = 1.0 / (1.0 + jnp.exp(-pre_act))
        delta = (
            back_ref[...] * inv_hidden * sigmoid_act * (1.0 + pre_act * (1.0 - sigmoid_act))
        )
        delta_ref[...] = delta.astype(jnp.bfloat16)
        delta_turned_ref[...] = delta.T.astype(jnp.bfloat16)
        activ_turned_ref[...] = (pre_act * sigmoid_act).T.astype(jnp.bfloat16)

    @pl.when(step >= steps)
    def _():
        for at, turned, mine, other, scale in (
            (0, delta_turned_ref, mine_ref, other_ref, inv_model),
            (local, activ_turned_ref, mine_scaled_ref, other_scaled_ref, inv_hidden),
        ):
            right = jnp.concatenate((mine[...], other[...]), axis=0)
            part = jnp.dot(turned[...], right, preferred_element_type=jnp.float32) * scale
            part = part.astype(jnp.bfloat16)
            for i in range(chips):
                part_ref[i, at : at + local] = part[i * local : (i + 1) * local]
        pair = jnp.dot(delta_ref[...], up, preferred_element_type=jnp.float32) * inv_model
        pair_ref[...] = pair[:rows]
        pair_other_ref[...] = pair[rows:].astype(jnp.bfloat16)


def expert_stage(mine, other, mine_scaled, other_scaled, weights, inv_model, inv_hidden):
    rows, width = mine.shape
    chips, both, _ = weights.shape
    hidden = chips * both // 2
    block = 512
    steps = width // block

    def late(i):
        return jnp.maximum(i - steps, 0)

    row_spec = pl.BlockSpec((rows, block), lambda i: (0, i % steps))
    late_spec = pl.BlockSpec((rows, block), lambda i: (0, late(i)))
    return pl.pallas_call(
        functools.partial(expert_kernel, steps, inv_model, inv_hidden),
        grid=(2 * steps,),
        in_specs=[row_spec] * 4 + [pl.BlockSpec((chips, both, block), lambda i: (0, 0, i % steps))],
        out_specs=[
            pl.BlockSpec((chips, both, block), lambda i: (0, 0, late(i))),
            late_spec,
            late_spec,
        ],
        out_shape=[
            jax.ShapeDtypeStruct(weights.shape, jnp.bfloat16),
            jax.ShapeDtypeStruct((rows, width), jnp.float32),
            jax.ShapeDtypeStruct((rows, width), jnp.bfloat16),
        ],
        scratch_shapes=[
            pltpu.VMEM((2 * rows, hidden), jnp.float32),
            pltpu.VMEM((2 * rows, hidden), jnp.float32),
            pltpu.VMEM((2 * rows, hidden), jnp.bfloat16),
            pltpu.VMEM((hidden, 2 * rows), jnp.bfloat16),
            pltpu.VMEM((hidden, 2 * rows), jnp.bfloat16),
        ],
        compiler_params=pltpu.CompilerParams(
            dimension_semantics=("arbitrary",), vmem_limit_bytes=40 * 1024 * 1024
        ),
        cost_estimate=pl.CostEstimate(flops=0, bytes_accessed=1024, transcendentals=0),
    )(mine, other, mine_scaled, other_scaled, weights)


def on_device(
    tokens,
    out_grad,
    routes,
    probs,
    swap_flags,
    up_weight,
    down_weight,
    up_first,
    up_second,
    down_first,
    down_second,
):
    model_width = tokens.shape[1]
    high = lax.axis_size(HIGH)
    side = lax.axis_size(SIDE)
    experts = high * side
    ring = lax.axis_size(RING)
    near = lax.axis_size(NEAR)
    chips = ring * near
    half_axis = experts // 2
    swap_flip = half_axis // side
    capacity = max(2, routes.size * 5 // (4 * experts))
    side_rows = high * capacity
    high_rows = side * capacity
    buffer_rows = experts * capacity
    local_hidden = up_weight.shape[1]
    hidden_units = local_hidden * chips * lax.axis_size(CORE)
    inv_model = model_width ** (-0.5)
    inv_hidden = hidden_units ** (-0.5)
    my_high = lax.axis_index(HIGH)
    my_index = my_high * side + lax.axis_index(SIDE)
    expert_ids = jnp.arange(experts, dtype=jnp.int32)
    flag_mine = jnp.sum(jnp.where(expert_ids == my_index, swap_flags, 0))
    swapped = flag_mine == 1

    weights = jnp.concatenate((up_weight[0], down_weight[0]), axis=0)
    weights_partner = partner(weights, HIGH, swap_flip)

    send_tokens, send_scaled, token_select = dispatch(
        swap_flags, routes, probs, tokens, out_grad, capacity
    )
    buffer_ids = jnp.arange(buffer_rows, dtype=jnp.int32)
    other_order = (
        (buffer_ids // capacity % high) * side_rows
        + (buffer_ids // side_rows) * capacity
        + buffer_ids % capacity
    )
    regroup = (buffer_ids[None, :] == other_order[:, None]).astype(jnp.bfloat16)

    def along_side(rows):
        return lax.all_to_all(
            rows.reshape(side, side_rows, model_width),
            SIDE,
            split_axis=0,
            concat_axis=0,
            tiled=True,
        ).reshape(buffer_rows, model_width)

    def pick(matrix, rows):
        return jnp.dot(matrix, rows, preferred_element_type=jnp.float32).astype(jnp.bfloat16)

    ways = z_routes()

    def along_high(rows, back):
        blocks = [rows[i * high_rows : (i + 1) * high_rows] for i in range(high)]
        moved = [
            lax.ppermute(
                array, (NEAR, HIGH), [(b, a) for a, b in way] if back else way
            )
            for array, way in zip(blocks[1:], ways)
        ]
        return jnp.concatenate(blocks[:1] + moved, axis=0)

    token_rows = pick(regroup, along_side(send_tokens))
    scaled_rows = pick(regroup, along_side(send_scaled))

    weights = jnp.where(swapped, weights_partner, weights)
    weights, token_rows, scaled_rows = lax.optimization_barrier(
        (weights, token_rows, scaled_rows)
    )
    both = jnp.stack((weights, partner(weights, NEAR, 1)), axis=0)
    gathered = lax.all_gather(both, RING, axis=0).reshape(
        chips, 2 * local_hidden, model_width
    )

    rows_mine = along_high(token_rows, False)
    scaled_mine = along_high(scaled_rows, False)
    rows_other = partner(rows_mine, CORE, 1)
    scaled_other = partner(scaled_mine, CORE, 1)
    moments = (up_first[0], up_second[0], down_first[0], down_second[0])
    held, rows_mine, scaled_mine = lax.optimization_barrier(
        (tuple(array.astype(jnp.bfloat16) for array in moments), rows_mine, scaled_mine)
    )
    arrived = tuple(partner(array, HIGH, swap_flip) for array in held)

    parts, pair_mine, for_other = expert_stage(
        rows_mine, rows_other, scaled_mine, scaled_other, gathered, inv_model, inv_hidden
    )
    from_other = partner(for_other, CORE, 1)
    pair_grad = (pair_mine + from_other.astype(jnp.float32)).astype(jnp.bfloat16)
    arrived, pair_grad = lax.optimization_barrier((arrived, pair_grad))
    returned = along_side(pick(regroup, along_high(pair_grad, True)))
    token_grad = pick(token_select, returned)

    own, beside = lax.psum_scatter(
        parts.reshape(ring, near, 2 * local_hidden, model_width),
        RING,
        scatter_dimension=0,
        tiled=False,
    )
    summed = own.astype(jnp.float32) + partner(beside, NEAR, 1).astype(jnp.float32)
    moments = tuple(
        jnp.where(swapped, new.astype(jnp.float32), old) for new, old in zip(arrived, moments)
    )
    new_up, up_first_new, up_second_new = adam_update(
        weights[:local_hidden], moments[0], moments[1], summed[:local_hidden]
    )
    new_down, down_first_new, down_second_new = adam_update(
        weights[local_hidden:], moments[2], moments[3], summed[local_hidden:]
    )
    return (
        token_grad,
        new_up[None],
        new_down[None],
        up_first_new[None],
        up_second_new[None],
        down_first_new[None],
        down_second_new[None],
    )


def solution(mesh):
    dp, expert = (mesh.shape[name] for name in ("dp", "expert"))
    fine = Mesh(
        mesh.devices.reshape(2, dp // 4, 2, HIGHS, expert // HIGHS),
        (NEAR, RING, CORE, HIGH, SIDE),
    )
    rows = P((NEAR, RING, CORE, HIGH, SIDE), None)
    slots = P((HIGH, SIDE), (NEAR, RING, CORE), None)
    return jax.shard_map(
        on_device,
        mesh=fine,
        in_specs=(rows, rows, rows, rows, P()) + (slots,) * 6,
        out_specs=(rows,) + (slots,) * 6,
        check_vma=False,
    )
```

profile of v0, /device:TPU:8, one launch (start us, length us, event | category | flops | bytes accessed | tf_op | source)
XLA Modules:
  0.0 439.2 jit_solution(12388309208875946645)
XLA Ops:
  11.8 3.8 shard_map.162
  15.6 5.9 %all-to-all-start = ((bf16[4,80,3584]{2,1,0:T(8,128)(2,1)}), bf16[4,80,3584]{2,1,0:T(8,128)(2,1)S(1)}, u32[]{:S(2)}, u32[]{:S(2)}) async-start(bf16[4,80,3584]{2,1,0:T(8,128)(2,1)} %bitcast.7), calls=%async_computation | async-start | bytes 4587520 | tf_op jit(solution)/shard_map/all_to_all | solution.py:294
  22.5 6.3 %collective-permute-start = (bf16[128,3584]{1,0:T(8,128)(2,1)}, bf16[128,3584]{1,0:T(8,128)(2,1)}, u32[]{:S(2)}, u32[]{:S(2)}) collective-permute-start(bf16[128,3584]{1,0:T(8,128)(2,1)} %pad_maximum_fusion.3), channel_id=1, source_target_pairs={{0,8},{4,12},{8,0},{12,4},{1,9},{5,13},{9,1},{13,5},{2,10},{6,14},... | collective-permute-start | bytes 2752520 | tf_op jit(solution)/shard_map/ppermute | solution.py:28
  28.8 18.8 %all-to-all-done = bf16[4,80,3584]{2,1,0:T(8,128)(2,1)S(1)} async-done(((bf16[4,80,3584]{2,1,0:T(8,128)(2,1)}), bf16[4,80,3584]{2,1,0:T(8,128)(2,1)S(1)}, u32[]{:S(2)}, u32[]{:S(2)}) %all-to-all-start) | async-done | bytes 2293792 | tf_op jit(solution)/shard_map/all_to_all | solution.py:294
  47.6 6.0 %all-to-all-start.1 = ((bf16[4,80,3584]{2,1,0:T(8,128)(2,1)}), bf16[4,80,3584]{2,1,0:T(8,128)(2,1)}, u32[]{:S(2)}, u32[]{:S(2)}) async-start(bf16[4,80,3584]{2,1,0:T(8,128)(2,1)} %bitcast.9), calls=%async_computation.1 | async-start | bytes 4587520 | tf_op jit(solution)/shard_map/all_to_all | solution.py:294
  55.0 12.3 %collective-permute-done = bf16[128,3584]{1,0:T(8,128)(2,1)} collective-permute-done((bf16[128,3584]{1,0:T(8,128)(2,1)}, bf16[128,3584]{1,0:T(8,128)(2,1)}, u32[]{:S(2)}, u32[]{:S(2)}) %collective-permute-start) | collective-permute-done | bytes 917536 | tf_op jit(solution)/shard_map/ppermute | solution.py:28
  68.7 2.9 convolution_convert_fusion.2
  71.5 7.5 %all-to-all-done.1 = bf16[4,80,3584]{2,1,0:T(8,128)(2,1)} async-done(((bf16[4,80,3584]{2,1,0:T(8,128)(2,1)}), bf16[4,80,3584]{2,1,0:T(8,128)(2,1)}, u32[]{:S(2)}, u32[]{:S(2)}) %all-to-all-start.1) | async-done | bytes 2293792 | tf_op jit(solution)/shard_map/all_to_all | solution.py:294
  79.0 4.5 %convolution_convert_fusion.1 = bf16[320,3584]{1,0:T(8,128)(2,1)} fusion(bf16[320,3584]{1,0:T(8,128)(2,1)} %bitcast.10, s32[320]{0:T(512)S(1)} %fusion.26), kind=kOutput, calls=%fused_computation.1 | convolution fusion | flops 735252480 | bytes 4588800 | tf_op jit(solution)/shard_map/dot_general | solution.py:303
  86.3 18.3 %collective-permute-done.13 = bf16[128,3584]{1,0:T(8,128)(2,1)S(1)} collective-permute-done((bf16[128,3584]{1,0:T(8,128)(2,1)S(1)}, bf16[128,3584]{1,0:T(8,128)(2,1)S(1)}, u32[]{:S(2)}, u32[]{:S(2)}) %collective-permute-start.13) | collective-permute-done | bytes 917536 | tf_op jit(solution)/shard_map/ppermute | solution.py:28
  108.0 6.7 %collective-permute-start.6 = (bf16[80,3584]{1,0:T(8,128)(2,1)S(1)}, bf16[80,3584]{1,0:T(8,128)(2,1)S(1)}, u32[]{:S(2)}, u32[]{:S(2)}) collective-permute-start(bf16[80,3584]{1,0:T(8,128)(2,1)S(1)} %get-tuple-element.61), channel_id=1, source_target_pairs={{0,136},{4,140},{8,128},{12,132},{128,8},{132,12},{136,0},{140,4},... | collective-permute-start | bytes 1720328 | tf_op jit(solution)/shard_map/ppermute | solution.py:310
  119.5 3.2 collective-permute-start.2
  122.7 30.4 %collective-permute-done.6 = bf16[80,3584]{1,0:T(8,128)(2,1)S(1)} collective-permute-done((bf16[80,3584]{1,0:T(8,128)(2,1)S(1)}, bf16[80,3584]{1,0:T(8,128)(2,1)S(1)}, u32[]{:S(2)}, u32[]{:S(2)}) %collective-permute-start.6) | collective-permute-done | bytes 573472 | tf_op jit(solution)/shard_map/ppermute | solution.py:310
  153.1 3.9 collective-permute-start.1
  157.0 20.7 %collective-permute-done.5 = bf16[80,3584]{1,0:T(8,128)(2,1)S(1)} collective-permute-done((bf16[80,3584]{1,0:T(8,128)(2,1)S(1)}, bf16[80,3584]{1,0:T(8,128)(2,1)S(1)}, u32[]{:S(2)}, u32[]{:S(2)}) %collective-permute-start.5) | collective-permute-done | bytes 573472 | tf_op jit(solution)/shard_map/ppermute | solution.py:310
  177.9 24.2 %collective-permute-done.3 = bf16[80,3584]{1,0:T(8,128)(2,1)S(1)} collective-permute-done((bf16[80,3584]{1,0:T(8,128)(2,1)S(1)}, bf16[80,3584]{1,0:T(8,128)(2,1)S(1)}, u32[]{:S(2)}, u32[]{:S(2)}) %collective-permute-start.3) | collective-permute-done | bytes 573472 | tf_op jit(solution)/shard_map/ppermute | solution.py:310
  202.2 7.8 %collective-permute-done.2 = bf16[80,3584]{1,0:T(8,128)(2,1)S(1)} collective-permute-done((bf16[80,3584]{1,0:T(8,128)(2,1)S(1)}, bf16[80,3584]{1,0:T(8,128)(2,1)S(1)}, u32[]{:S(2)}, u32[]{:S(2)}) %collective-permute-start.2) | collective-permute-done | bytes 573472 | tf_op jit(solution)/shard_map/ppermute | solution.py:310
  222.1 22.7 %shard_map.163 = (bf16[8,128,3584]{2,1,0:T(8,128)(2,1)}, f32[320,3584]{1,0:T(8,128)}, bf16[320,3584]{1,0:T(8,128)(2,1)S(1)}) custom-call(bf16[320,3584]{1,0:T(8,128)(2,1)S(1)} %copy-done.1, bf16[320,3584]{1,0:T(8,128)(2,1)S(1)} %copy-done.5, bf16[320,3584]{1,0:T(8,128)(2,1)S(1)} %pad_maximum_fusion.1.mine_scaled_ref, bf16[320,3584]{1,0:T(8,128)(2,1)S(1)} %copy-done.3, ...), custom_call_target="tpu_custom_call" | custom-call | bytes 1024 | tf_op jit(solution)/shard_map/pallas_call | solution.py:215
  247.7 5.0 %collective-permute-start.7 = (bf16[64,3584]{1,0:T(8,128)(2,1)}, bf16[64,3584]{1,0:T(8,128)(2,1)S(1)}, u32[]{:S(2)}, u32[]{:S(2)}) collective-permute-start(bf16[64,3584]{1,0:T(8,128)(2,1)} %get-tuple-element.32), channel_id=1, source_target_pairs={{0,8},{4,12},{8,0},{12,4},{1,9},{5,13},{9,1},{13,5},{2,10},{6,14},... | collective-permute-start | bytes 1376264 | tf_op jit(solution)/shard_map/ppermute | solution.py:28
  253.7 5.0 %collective-permute-start.9 = (bf16[64,3584]{1,0:T(8,128)(2,1)}, bf16[64,3584]{1,0:T(8,128)(2,1)S(1)}, u32[]{:S(2)}, u32[]{:S(2)}) collective-permute-start(bf16[64,3584]{1,0:T(8,128)(2,1)} %get-tuple-element.34), channel_id=1, source_target_pairs={{0,8},{4,12},{8,0},{12,4},{1,9},{5,13},{9,1},{13,5},{2,10},{6,14},... | collective-permute-start | bytes 1376264 | tf_op jit(solution)/shard_map/ppermute | solution.py:28
  259.6 2.9 add_convert_fusion
  262.6 29.9 %collective-permute-done.7 = bf16[64,3584]{1,0:T(8,128)(2,1)S(1)} collective-permute-done((bf16[64,3584]{1,0:T(8,128)(2,1)}, bf16[64,3584]{1,0:T(8,128)(2,1)S(1)}, u32[]{:S(2)}, u32[]{:S(2)}) %collective-permute-start.7) | collective-permute-done | bytes 458784 | tf_op jit(solution)/shard_map/ppermute | solution.py:28
  292.4 22.4 %collective-permute-done.8 = bf16[64,3584]{1,0:T(8,128)(2,1)S(1)} collective-permute-done((bf16[64,3584]{1,0:T(8,128)(2,1)}, bf16[64,3584]{1,0:T(8,128)(2,1)S(1)}, u32[]{:S(2)}, u32[]{:S(2)}) %collective-permute-start.8) | collective-permute-done | bytes 458784 | tf_op jit(solution)/shard_map/ppermute | solution.py:28
  314.8 9.8 %collective-permute-done.9 = bf16[64,3584]{1,0:T(8,128)(2,1)S(1)} collective-permute-done((bf16[64,3584]{1,0:T(8,128)(2,1)}, bf16[64,3584]{1,0:T(8,128)(2,1)S(1)}, u32[]{:S(2)}, u32[]{:S(2)}) %collective-permute-start.9) | collective-permute-done | bytes 458784 | tf_op jit(solution)/shard_map/ppermute | solution.py:28
  324.6 9.4 %collective-permute-done.10 = bf16[64,3584]{1,0:T(8,128)(2,1)S(1)} collective-permute-done((bf16[64,3584]{1,0:T(8,128)(2,1)}, bf16[64,3584]{1,0:T(8,128)(2,1)S(1)}, u32[]{:S(2)}, u32[]{:S(2)}) %collective-permute-start.10) | collective-permute-done | bytes 458784 | tf_op jit(solution)/shard_map/ppermute | solution.py:28
  334.9 3.5 collective-permute-start.16
  340.5 23.5 %collective-permute-done.17 = bf16[80,3584]{1,0:T(8,128)(2,1)S(1)} collective-permute-done((bf16[80,3584]{1,0:T(8,128)(2,1)S(1)}, bf16[80,3584]{1,0:T(8,128)(2,1)S(1)}, u32[]{:S(2)}, u32[]{:S(2)}) %collective-permute-start.17) | collective-permute-done | bytes 573472 | tf_op jit(solution)/shard_map/ppermute | solution.py:310
  364.0 12.7 %collective-permute-done.16 = bf16[80,3584]{1,0:T(8,128)(2,1)S(1)} collective-permute-done((bf16[80,3584]{1,0:T(8,128)(2,1)S(1)}, bf16[80,3584]{1,0:T(8,128)(2,1)S(1)}, u32[]{:S(2)}, u32[]{:S(2)}) %collective-permute-start.16) | collective-permute-done | bytes 573472 | tf_op jit(solution)/shard_map/ppermute | solution.py:310
  376.7 12.6 %collective-permute-done.15 = bf16[80,3584]{1,0:T(8,128)(2,1)S(1)} collective-permute-done((bf16[80,3584]{1,0:T(8,128)(2,1)S(1)}, bf16[80,3584]{1,0:T(8,128)(2,1)S(1)}, u32[]{:S(2)}, u32[]{:S(2)}) %collective-permute-start.15) | collective-permute-done | bytes 573472 | tf_op jit(solution)/shard_map/ppermute | solution.py:310
  392.0 5.1 %all-to-all-start.2 = ((bf16[4,80,3584]{2,1,0:T(8,128)(2,1)}), bf16[4,80,3584]{2,1,0:T(8,128)(2,1)S(1)}, u32[]{:S(2)}, u32[]{:S(2)}) async-start(bf16[4,80,3584]{2,1,0:T(8,128)(2,1)} %bitcast.84), calls=%async_computation.2 | async-start | bytes 4587520 | tf_op jit(solution)/shard_map/all_to_all | solution.py:294
  399.4 25.0 %all-to-all-done.2 = bf16[4,80,3584]{2,1,0:T(8,128)(2,1)S(1)} async-done(((bf16[4,80,3584]{2,1,0:T(8,128)(2,1)}), bf16[4,80,3584]{2,1,0:T(8,128)(2,1)S(1)}, u32[]{:S(2)}, u32[]{:S(2)}) %all-to-all-start.2) | async-done | bytes 2293792 | tf_op jit(solution)/shard_map/all_to_all | solution.py:294
  428.4 3.9 fusion.38
  (104 shorter events, 47.5 us)
Async XLA Ops:
  15.6 5.9 %copy-start.22 = (bf16[1,64,3584]{2,1,0:T(8,128)(2,1)S(1)}, bf16[1,64,3584]{2,1,0:T(8,128)(2,1)}, u32[]{:S(2)}) copy-start(bf16[1,64,3584]{2,1,0:T(8,128)(2,1)} %param.17) | copy-start | bytes 1376260
  15.6 5.9 %copy-start.23 = (bf16[1,64,3584]{2,1,0:T(8,128)(2,1)S(1)}, bf16[1,64,3584]{2,1,0:T(8,128)(2,1)}, u32[]{:S(2)}) copy-start(bf16[1,64,3584]{2,1,0:T(8,128)(2,1)} %param.16) | copy-start | bytes 1376260
  15.6 32.0 %all-to-all-start = ((bf16[4,80,3584]{2,1,0:T(8,128)(2,1)}), bf16[4,80,3584]{2,1,0:T(8,128)(2,1)S(1)}, u32[]{:S(2)}, u32[]{:S(2)}) async-start(bf16[4,80,3584]{2,1,0:T(8,128)(2,1)} %bitcast.7), calls=%async_computation | async-start | bytes 4587520 | tf_op jit(solution)/shard_map/all_to_all | solution.py:294
  22.5 44.8 %collective-permute-start = (bf16[128,3584]{1,0:T(8,128)(2,1)}, bf16[128,3584]{1,0:T(8,128)(2,1)}, u32[]{:S(2)}, u32[]{:S(2)}) collective-permute-start(bf16[128,3584]{1,0:T(8,128)(2,1)} %pad_maximum_fusion.3), channel_id=1, source_target_pairs={{0,8},{4,12},{8,0},{12,4},{1,9},{5,13},{9,1},{13,5},{2,10},{6,14},... | collective-permute-start | bytes 2752520 | tf_op jit(solution)/shard_map/ppermute | solution.py:28
  47.6 6.0 %copy-start.9 = (s32[16]{0:T(128)S(1)}, s32[16]{0:T(128)}, u32[]{:S(2)}) copy-start(s32[16]{0:T(128)} %param.15) | copy-start | bytes 196
  47.6 31.4 %all-to-all-start.1 = ((bf16[4,80,3584]{2,1,0:T(8,128)(2,1)}), bf16[4,80,3584]{2,1,0:T(8,128)(2,1)}, u32[]{:S(2)}, u32[]{:S(2)}) async-start(bf16[4,80,3584]{2,1,0:T(8,128)(2,1)} %bitcast.9), calls=%async_computation.1 | async-start | bytes 4587520 | tf_op jit(solution)/shard_map/all_to_all | solution.py:294
  53.6 163.5 %all-gather.3.cloned.1.call-start = ((), (), s32[]{:S(2)}) async-start(), calls=%async_computation.5 | async-start | bytes 9175040 | tf_op jit(solution)/shard_map/all_gather | solution.py:325
  83.5 21.1 %collective-permute-start.13 = (bf16[128,3584]{1,0:T(8,128)(2,1)S(1)}, bf16[128,3584]{1,0:T(8,128)(2,1)S(1)}, u32[]{:S(2)}, u32[]{:S(2)}) collective-permute-start(bf16[128,3584]{1,0:T(8,128)(2,1)S(1)} %broadcast_select_fusion), channel_id=1, source_target_pairs={{0,128},{128,0},{1,129},{129,1},{2,130},{130,2},{3,131},{131,3},{4... | collective-permute-start | bytes 2752520 | tf_op jit(solution)/shard_map/ppermute | solution.py:28
  106.0 11.1 %copy-start.20 = (bf16[320,3584]{1,0:T(8,128)(2,1)S(1)}, bf16[320,3584]{1,0:T(8,128)(2,1)}, u32[]{:S(2)}) copy-start(bf16[320,3584]{1,0:T(8,128)(2,1)} %convolution_convert_fusion.2) | copy-start | bytes 6881284
  106.0 291.0 %reduce-scatter.2.cloned.1.call-start = ((), (), s32[]{:S(2)}) async-start(), calls=%async_computation.4 | async-start | bytes 9175040 | tf_op jit(solution)/shard_map/reduce_scatter | solution.py:348
  108.0 45.1 %collective-permute-start.6 = (bf16[80,3584]{1,0:T(8,128)(2,1)S(1)}, bf16[80,3584]{1,0:T(8,128)(2,1)S(1)}, u32[]{:S(2)}, u32[]{:S(2)}) collective-permute-start(bf16[80,3584]{1,0:T(8,128)(2,1)S(1)} %get-tuple-element.61), channel_id=1, source_target_pairs={{0,136},{4,140},{8,128},{12,132},{128,8},{132,12},{136,0},{140,4},... | collective-permute-start | bytes 1720328 | tf_op jit(solution)/shard_map/ppermute | solution.py:310
  114.6 63.0 %collective-permute-start.5 = (bf16[80,3584]{1,0:T(8,128)(2,1)S(1)}, bf16[80,3584]{1,0:T(8,128)(2,1)S(1)}, u32[]{:S(2)}, u32[]{:S(2)}) collective-permute-start(bf16[80,3584]{1,0:T(8,128)(2,1)S(1)} %get-tuple-element.62), channel_id=1, source_target_pairs={{0,140},{4,128},{8,132},{12,136},{128,4},{132,8},{136,12},{140,0},... | collective-permute-start | bytes 1720328 | tf_op jit(solution)/shard_map/ppermute | solution.py:310
  114.7 63.0 %collective-permute-start.4 = (bf16[80,3584]{1,0:T(8,128)(2,1)S(1)}, bf16[80,3584]{1,0:T(8,128)(2,1)S(1)}, u32[]{:S(2)}, u32[]{:S(2)}) collective-permute-start(bf16[80,3584]{1,0:T(8,128)(2,1)S(1)} %get-tuple-element.63), channel_id=1, source_target_pairs={{0,4},{4,8},{8,12},{12,0},{128,140},{132,128},{136,132},{140,136},... | collective-permute-start | bytes 1720328 | tf_op jit(solution)/shard_map/ppermute | solution.py:310
  117.3 84.9 %collective-permute-start.3 = (bf16[80,3584]{1,0:T(8,128)(2,1)S(1)}, bf16[80,3584]{1,0:T(8,128)(2,1)S(1)}, u32[]{:S(2)}, u32[]{:S(2)}) collective-permute-start(bf16[80,3584]{1,0:T(8,128)(2,1)S(1)} %get-tuple-element.65), channel_id=1, source_target_pairs={{0,136},{4,140},{8,128},{12,132},{128,8},{132,12},{136,0},{140,4},... | collective-permute-start | bytes 1720328 | tf_op jit(solution)/shard_map/ppermute | solution.py:310
  119.5 90.5 %collective-permute-start.2 = (bf16[80,3584]{1,0:T(8,128)(2,1)S(1)}, bf16[80,3584]{1,0:T(8,128)(2,1)S(1)}, u32[]{:S(2)}, u32[]{:S(2)}) collective-permute-start(bf16[80,3584]{1,0:T(8,128)(2,1)S(1)} %get-tuple-element.66), channel_id=1, source_target_pairs={{0,140},{4,128},{8,132},{12,136},{128,4},{132,8},{136,12},{140,0},... | collective-permute-start | bytes 1720328 | tf_op jit(solution)/shard_map/ppermute | solution.py:310
  153.1 56.9 %collective-permute-start.1 = (bf16[80,3584]{1,0:T(8,128)(2,1)S(1)}, bf16[80,3584]{1,0:T(8,128)(2,1)S(1)}, u32[]{:S(2)}, u32[]{:S(2)}) collective-permute-start(bf16[80,3584]{1,0:T(8,128)(2,1)S(1)} %get-tuple-element.67), channel_id=1, source_target_pairs={{0,4},{4,8},{8,12},{12,0},{128,140},{132,128},{136,132},{140,136},... | collective-permute-start | bytes 1720328 | tf_op jit(solution)/shard_map/ppermute | solution.py:310
  177.8 36.5 %collective-permute-start.12 = (bf16[320,3584]{1,0:T(8,128)(2,1)S(1)}, bf16[320,3584]{1,0:T(8,128)(2,1)S(1)}, u32[]{:S(2)}, u32[]{:S(2)}) collective-permute-start(bf16[320,3584]{1,0:T(8,128)(2,1)S(1)} %pad_maximum_fusion.1.mine_scaled_ref), channel_id=1, source_target_pairs={{0,16},{16,0},{1,17},{17,1},{2,18},{18,2},{3,19},{19,3},{4,20},{20... | collective-permute-start | bytes 6881288 | tf_op jit(solution)/shard_map/ppermute | solution.py:28
  210.2 4.2 copy-start
  210.2 5.5 %collective-permute-start.11 = (bf16[320,3584]{1,0:T(8,128)(2,1)S(1)}, bf16[320,3584]{1,0:T(8,128)(2,1)S(1)}, u32[]{:S(2)}, u32[]{:S(2)}) collective-permute-start(bf16[320,3584]{1,0:T(8,128)(2,1)S(1)} %pad_maximum_fusion.mine_ref), channel_id=1, source_target_pairs={{0,16},{16,0},{1,17},{17,1},{2,18},{18,2},{3,19},{19,3},{4,20},{20... | collective-permute-start | bytes 6881288 | tf_op jit(solution)/shard_map/ppermute | solution.py:28
  247.7 11.9 %collective-permute-start.14 = (bf16[320,3584]{1,0:T(8,128)(2,1)S(1)}, bf16[320,3584]{1,0:T(8,128)(2,1)S(1)}, u32[]{:S(2)}, u32[]{:S(2)}) collective-permute-start(bf16[320,3584]{1,0:T(8,128)(2,1)S(1)} %copy-done.11), channel_id=1, source_target_pairs={{0,16},{16,0},{1,17},{17,1},{2,18},{18,2},{3,19},{19,3},{4,20},{20... | collective-permute-start | bytes 6881288 | tf_op jit(solution)/shard_map/ppermute | solution.py:28
  247.7 44.7 %collective-permute-start.7 = (bf16[64,3584]{1,0:T(8,128)(2,1)}, bf16[64,3584]{1,0:T(8,128)(2,1)S(1)}, u32[]{:S(2)}, u32[]{:S(2)}) collective-permute-start(bf16[64,3584]{1,0:T(8,128)(2,1)} %get-tuple-element.32), channel_id=1, source_target_pairs={{0,8},{4,12},{8,0},{12,4},{1,9},{5,13},{9,1},{13,5},{2,10},{6,14},... | collective-permute-start | bytes 1376264 | tf_op jit(solution)/shard_map/ppermute | solution.py:28
  252.7 62.0 %collective-permute-start.8 = (bf16[64,3584]{1,0:T(8,128)(2,1)}, bf16[64,3584]{1,0:T(8,128)(2,1)S(1)}, u32[]{:S(2)}, u32[]{:S(2)}) collective-permute-start(bf16[64,3584]{1,0:T(8,128)(2,1)} %get-tuple-element.33), channel_id=1, source_target_pairs={{0,8},{4,12},{8,0},{12,4},{1,9},{5,13},{9,1},{13,5},{2,10},{6,14},... | collective-permute-start | bytes 1376264 | tf_op jit(solution)/shard_map/ppermute | solution.py:28
  253.7 70.9 %collective-permute-start.9 = (bf16[64,3584]{1,0:T(8,128)(2,1)}, bf16[64,3584]{1,0:T(8,128)(2,1)S(1)}, u32[]{:S(2)}, u32[]{:S(2)}) collective-permute-start(bf16[64,3584]{1,0:T(8,128)(2,1)} %get-tuple-element.34), channel_id=1, source_target_pairs={{0,8},{4,12},{8,0},{12,4},{1,9},{5,13},{9,1},{13,5},{2,10},{6,14},... | collective-permute-start | bytes 1376264 | tf_op jit(solution)/shard_map/ppermute | solution.py:28
  258.7 75.4 %collective-permute-start.10 = (bf16[64,3584]{1,0:T(8,128)(2,1)}, bf16[64,3584]{1,0:T(8,128)(2,1)S(1)}, u32[]{:S(2)}, u32[]{:S(2)}) collective-permute-start(bf16[64,3584]{1,0:T(8,128)(2,1)} %get-tuple-element.35), channel_id=1, source_target_pairs={{0,8},{4,12},{8,0},{12,4},{1,9},{5,13},{9,1},{13,5},{2,10},{6,14},... | collective-permute-start | bytes 1376264 | tf_op jit(solution)/shard_map/ppermute | solution.py:28
  292.4 41.8 %copy-start.24 = (bf16[64,3584]{1,0:T(8,128)(2,1)}, bf16[64,3584]{1,0:T(8,128)(2,1)S(1)}, u32[]{:S(2)}) copy-start(bf16[64,3584]{1,0:T(8,128)(2,1)S(1)} %collective-permute-done.7) | copy-start | bytes 1376260
  314.8 19.4 %copy-start.26 = (bf16[64,3584]{1,0:T(8,128)(2,1)}, bf16[64,3584]{1,0:T(8,128)(2,1)S(1)}, u32[]{:S(2)}) copy-start(bf16[64,3584]{1,0:T(8,128)(2,1)S(1)} %collective-permute-done.8) | copy-start | bytes 1376260
  324.6 9.6 %copy-start.28 = (bf16[64,3584]{1,0:T(8,128)(2,1)}, bf16[64,3584]{1,0:T(8,128)(2,1)S(1)}, u32[]{:S(2)}) copy-start(bf16[64,3584]{1,0:T(8,128)(2,1)S(1)} %collective-permute-done.9) | copy-start | bytes 1376260
  334.9 29.1 %collective-permute-start.17 = (bf16[80,3584]{1,0:T(8,128)(2,1)S(1)}, bf16[80,3584]{1,0:T(8,128)(2,1)S(1)}, u32[]{:S(2)}, u32[]{:S(2)}) collective-permute-start(bf16[80,3584]{1,0:T(8,128)(2,1)S(1)} %get-tuple-element.57), channel_id=1, source_target_pairs={{136,0},{140,4},{128,8},{132,12},{8,128},{12,132},{0,136},{4,140},... | collective-permute-start | bytes 1720328 | tf_op jit(solution)/shard_map/ppermute | solution.py:310
  334.9 41.9 %collective-permute-start.16 = (bf16[80,3584]{1,0:T(8,128)(2,1)S(1)}, bf16[80,3584]{1,0:T(8,128)(2,1)S(1)}, u32[]{:S(2)}, u32[]{:S(2)}) collective-permute-start(bf16[80,3584]{1,0:T(8,128)(2,1)S(1)} %get-tuple-element.58), channel_id=1, source_target_pairs={{140,0},{128,4},{132,8},{136,12},{4,128},{8,132},{12,136},{0,140},... | collective-permute-start | bytes 1720328 | tf_op jit(solution)/shard_map/ppermute | solution.py:310
  338.3 51.0 %collective-permute-start.15 = (bf16[80,3584]{1,0:T(8,128)(2,1)S(1)}, bf16[80,3584]{1,0:T(8,128)(2,1)S(1)}, u32[]{:S(2)}, u32[]{:S(2)}) collective-permute-start(bf16[80,3584]{1,0:T(8,128)(2,1)S(1)} %get-tuple-element.59), channel_id=1, source_target_pairs={{4,0},{8,4},{12,8},{0,12},{140,128},{128,132},{132,136},{136,140},... | collective-permute-start | bytes 1720328 | tf_op jit(solution)/shard_map/ppermute | solution.py:310
  392.0 32.5 %all-to-all-start.2 = ((bf16[4,80,3584]{2,1,0:T(8,128)(2,1)}), bf16[4,80,3584]{2,1,0:T(8,128)(2,1)S(1)}, u32[]{:S(2)}, u32[]{:S(2)}) async-start(bf16[4,80,3584]{2,1,0:T(8,128)(2,1)} %bitcast.84), calls=%async_computation.2 | async-start | bytes 4587520 | tf_op jit(solution)/shard_map/all_to_all | solution.py:294
  399.2 26.9 %collective-permute-start.18 = (bf16[128,3584]{1,0:T(8,128)(2,1)}, bf16[128,3584]{1,0:T(8,128)(2,1)}, u32[]{:S(2)}, u32[]{:S(2)}) collective-permute-start(bf16[128,3584]{1,0:T(8,128)(2,1)} %slice_bitcast_fusion), channel_id=1, source_target_pairs={{0,128},{128,0},{1,129},{129,1},{2,130},{130,2},{3,131},{131,3},{4... | collective-permute-start | bytes 2752520 | tf_op jit(solution)/shard_map/ppermute | solution.py:28
  (23 other events, 43.6 us)
Sparse Core Ops, SparseCore 0:
  106.2 78.6 all-gather.2
  246.2 74.7 reduce-scatter.1
where the time goes:
time: 442 us; the launch traced here: 439 us
  waiting for transfers between devices  286 us (65%)
  starting transfers between devices  62.7 us (14%)
  Pallas kernels  26.5 us (6%)
  local copies, waits for them, and re-layouts  22.9 us (5%)
  other arithmetic  15.2 us (3%)
  between operations  14.9 us (3%)
  matrix products  11.6 us (3%)
    ppermute x9, waiting for transfers between devices, along_high(): lax.ppermute(array, (NEAR, HIGH), [(b, a) for a, b in way] if back else way)  132 us
    ppermute x10, waiting for transfers between devices, partner(): lax.ppermute(array, axis, [(i, i ^ flip) for i in range(lax.axis_size(axi...  102 us
    all_to_all x3, waiting for transfers between devices, along_side(): lax.all_to_all(rows.reshape(side, side_rows, model_width), SIDE, split_ax...  51.4 us
    ppermute x9, starting transfers between devices, along_high(): lax.ppermute(array, (NEAR, HIGH), [(b, a) for a, b in way] if back else way)  24 us
    pallas_call x1, Pallas kernels, expert_stage(): pl.pallas_call(functools.partial(expert_kernel, steps, inv_model, inv_hid...  22.7 us
    ppermute x10, starting transfers between devices, partner(): lax.ppermute(array, axis, [(i, i ^ flip) for i in range(lax.axis_size(axi...  21.6 us
    unnamed x64, local copies, waits for them, and re-layouts  18.5 us
    all_to_all x3, starting transfers between devices, along_side(): lax.all_to_all(rows.reshape(side, side_rows, model_width), SIDE, split_ax...  17 us
  transfers between devices with their start and end apart: 24, of which 16 were waited for; matrix products, arithmetic and copies ran while one was open for 4% of the time, Pallas kernels for 0%

commit v1 on v0

--- a/solution.py
+++ b/solution.py
@@ -19,7 +19,9 @@
 NEAR = "near"
 RING = "ring"
 CORE = "core"
-HIGH = "high"
+FAR = "far"
+STEP = "step"
+HIGH = (FAR, STEP)
 SIDE = "side"
 HIGHS = 4
 
@@ -138,14 +140,12 @@
     mine_scaled_ref,
     other_scaled_ref,
     weight_ref,
-    part_ref,
     pair_ref,
     pair_other_ref,
+    left_ref,
     pre_ref,
     back_ref,
     delta_ref,
-    delta_turned_ref,
-    activ_turned_ref,
 ):
     step = pl.program_id(0)
     chips, both, _ = weight_ref.shape
@@ -162,16 +162,14 @@
     @pl.when(step < steps)
     def _():
         down = jnp.concatenate([weight_ref[i, local:] for i in range(chips)], axis=0)
-        for at, token, scaled in (
-            (0, mine_ref, mine_scaled_ref),
-            (rows, other_ref, other_scaled_ref),
-        ):
-            pre_ref[at : at + rows] += lax.dot_general(
-                token[...], up, contract_last, preferred_element_type=jnp.float32
-            )
-            back_ref[at : at + rows] += lax.dot_general(
-                scaled[...], down, contract_last, preferred_element_type=jnp.float32
-            )
+        token = jnp.concatenate((mine_ref[...], other_ref[...]), axis=0)
+        pre_ref[...] += lax.dot_general(
+            up, token, contract_last, preferred_element_type=jnp.float32
+        )
+        scaled = jnp.concatenate((mine_scaled_ref[...], other_scaled_ref[...]), axis=0)
+        back_ref[...] += lax.dot_general(
+            down, scaled, contract_last, preferred_element_type=jnp.float32
+        )
 
     @pl.when(step == steps - 1)
     def _():
@@ -179,22 +177,13 @@
         sigmoid_act = 1.0 / (1.0 + jnp.exp(-pre_act))
         delta = (
             back_ref[...] * inv_hidden * sigmoid_act * (1.0 + pre_act * (1.0 - sigmoid_act))
-        )
-        delta_ref[...] = delta.astype(jnp.bfloat16)
-        delta_turned_ref[...] = delta.T.astype(jnp.bfloat16)
-        activ_turned_ref[...] = (pre_act * sigmoid_act).T.astype(jnp.bfloat16)
+        ).astype(jnp.bfloat16)
+        left_ref[0] = delta
+        left_ref[1] = (pre_act * sigmoid_act).astype(jnp.bfloat16)
+        delta_ref[...] = delta.T
 
     @pl.when(step >= steps)
     def _():
-        for at, turned, mine, other, scale in (
-            (0, delta_turned_ref, mine_ref, other_ref, inv_model),
-            (local, activ_turned_ref, mine_scaled_ref, other_scaled_ref, inv_hidden),
-        ):
-            right = jnp.concatenate((mine[...], other[...]), axis=0)
-            part = jnp.dot(turned[...], right, preferred_element_type=jnp.float32) * scale
-            part = part.astype(jnp.bfloat16)
-            for i in range(chips):
-                part_ref[i, at : at + local] = part[i * local : (i + 1) * local]
         pair = jnp.dot(delta_ref[...], up, preferred_element_type=jnp.float32) * inv_model
         pair_ref[...] = pair[:rows]
         pair_other_ref[...] = pair[rows:].astype(jnp.bfloat16)
@@ -207,37 +196,85 @@
     block = 512
     steps = width // block
 
+    def early(i):
+        return jnp.minimum(i, steps - 1)
+
     def late(i):
         return jnp.maximum(i - steps, 0)
 
-    row_spec = pl.BlockSpec((rows, block), lambda i: (0, i % steps))
+    row_spec = pl.BlockSpec((rows, block), lambda i: (0, early(i)))
     late_spec = pl.BlockSpec((rows, block), lambda i: (0, late(i)))
     return pl.pallas_call(
         functools.partial(expert_kernel, steps, inv_model, inv_hidden),
         grid=(2 * steps,),
         in_specs=[row_spec] * 4 + [pl.BlockSpec((chips, both, block), lambda i: (0, 0, i % steps))],
         out_specs=[
-            pl.BlockSpec((chips, both, block), lambda i: (0, 0, late(i))),
             late_spec,
             late_spec,
+            pl.BlockSpec((2, hidden, 2 * rows), lambda i: (0, 0, 0)),
         ],
         out_shape=[
-            jax.ShapeDtypeStruct(weights.shape, jnp.bfloat16),
             jax.ShapeDtypeStruct((rows, width), jnp.float32),
             jax.ShapeDtypeStruct((rows, width), jnp.bfloat16),
+            jax.ShapeDtypeStruct((2, hidden, 2 * rows), jnp.bfloat16),
         ],
         scratch_shapes=[
-            pltpu.VMEM((2 * rows, hidden), jnp.float32),
-            pltpu.VMEM((2 * rows, hidden), jnp.float32),
+            pltpu.VMEM((hidden, 2 * rows), jnp.float32),
+            pltpu.VMEM((hidden, 2 * rows), jnp.float32),
             pltpu.VMEM((2 * rows, hidden), jnp.bfloat16),
-            pltpu.VMEM((hidden, 2 * rows), jnp.bfloat16),
-            pltpu.VMEM((hidden, 2 * rows), jnp.bfloat16),
         ],
         compiler_params=pltpu.CompilerParams(
             dimension_semantics=("arbitrary",), vmem_limit_bytes=40 * 1024 * 1024
         ),
-        cost_estimate=pl.CostEstimate(flops=0, bytes_accessed=1024, transcendentals=0),
+        cost_estimate=pl.CostEstimate(
+            flops=12 * rows * hidden * width, bytes_accessed=32 * rows * width, transcendentals=0
+        ),
     )(mine, other, mine_scaled, other_scaled, weights)
+
+
+def weight_kernel(
+    inv_model,
+    inv_hidden,
+    left_ref,
+    mine_ref,
+    other_ref,
+    mine_scaled_ref,
+    other_scaled_ref,
+    part_ref,
+):
+    chips, both, _ = part_ref.shape
+    local = both // 2
+    for kind, mine, other, scale in (
+        (0, mine_ref, other_ref, inv_model),
+        (1, mine_scaled_ref, other_scaled_ref, inv_hidden),
+    ):
+        right = jnp.concatenate((mine[...], other[...]), axis=0)
+        part = jnp.dot(left_ref[kind], right, preferred_element_type=jnp.float32) * scale
+        part = part.astype(jnp.bfloat16)
+        for i in range(chips):
+            part_ref[i, kind * local : (kind + 1) * local] = part[i * local : (i + 1) * local]
+
+
+def weight_stage(left, mine, other, mine_scaled, other_scaled, chips, inv_model, inv_hidden):
+    rows, width = mine.shape
+    both = 2 * left.shape[1] // chips
+    block = 512
+    row_spec = pl.BlockSpec((rows, block), lambda i: (0, i))
+    return pl.pallas_call(
+        functools.partial(weight_kernel, inv_model, inv_hidden),
+        grid=(width // block,),
+        in_specs=[pl.BlockSpec(left.shape, lambda i: (0, 0, 0))] + [row_spec] * 4,
+        out_specs=pl.BlockSpec((chips, both, block), lambda i: (0, 0, i)),
+        out_shape=jax.ShapeDtypeStruct((chips, both, width), jnp.bfloat16),
+        compiler_params=pltpu.CompilerParams(
+            dimension_semantics=("arbitrary",), vmem_limit_bytes=40 * 1024 * 1024
+        ),
+        cost_estimate=pl.CostEstimate(
+            flops=8 * rows * left.shape[1] * width,
+            bytes_accessed=32 * rows * width,
+            transcendentals=0,
+        ),
+    )(left, mine, other, mine_scaled, other_scaled)
 
 
 def on_device(
@@ -261,7 +298,6 @@
     near = lax.axis_size(NEAR)
     chips = ring * near
     half_axis = experts // 2
-    swap_flip = half_axis // side
     capacity = max(2, routes.size * 5 // (4 * experts))
     side_rows = high * capacity
     high_rows = side * capacity
@@ -277,7 +313,7 @@
     swapped = flag_mine == 1
 
     weights = jnp.concatenate((up_weight[0], down_weight[0]), axis=0)
-    weights_partner = partner(weights, HIGH, swap_flip)
+    weights_partner = partner(weights, FAR, 1)
 
     send_tokens, send_scaled, token_select = dispatch(
         swap_flags, routes, probs, tokens, out_grad, capacity
@@ -308,20 +344,20 @@
         blocks = [rows[i * high_rows : (i + 1) * high_rows] for i in range(high)]
         moved = [
             lax.ppermute(
-                array, (NEAR, HIGH), [(b, a) for a, b in way] if back else way
+                array, (NEAR, *HIGH), [(b, a) for a, b in way] if back else way
             )
             for array, way in zip(blocks[1:], ways)
         ]
         return jnp.concatenate(blocks[:1] + moved, axis=0)
 
     token_rows = pick(regroup, along_side(send_tokens))
-    scaled_rows = pick(regroup, along_side(send_scaled))
+    side_scaled = along_side(send_scaled)
+    scaled_rows = pick(regroup, side_scaled)
 
     weights = jnp.where(swapped, weights_partner, weights)
-    weights, token_rows, scaled_rows = lax.optimization_barrier(
-        (weights, token_rows, scaled_rows)
-    )
+    weights, _ = lax.optimization_barrier((weights, token_rows))
     both = jnp.stack((weights, partner(weights, NEAR, 1)), axis=0)
+    both, _ = lax.optimization_barrier((both, side_scaled))
     gathered = lax.all_gather(both, RING, axis=0).reshape(
         chips, 2 * local_hidden, model_width
     )
@@ -331,18 +367,24 @@
     rows_other = partner(rows_mine, CORE, 1)
     scaled_other = partner(scaled_mine, CORE, 1)
     moments = (up_first[0], up_second[0], down_first[0], down_second[0])
-    held, rows_mine, scaled_mine = lax.optimization_barrier(
-        (tuple(array.astype(jnp.bfloat16) for array in moments), rows_mine, scaled_mine)
-    )
-    arrived = tuple(partner(array, HIGH, swap_flip) for array in held)
-
-    parts, pair_mine, for_other = expert_stage(
+
+    rounded = tuple(array.astype(jnp.bfloat16) for array in moments)
+    up_held, _ = lax.optimization_barrier((jnp.stack(rounded[:2]), scaled_mine))
+    up_pair = lax.all_gather(up_held, FAR, axis=0)
+    pair_mine, for_other, left = expert_stage(
         rows_mine, rows_other, scaled_mine, scaled_other, gathered, inv_model, inv_hidden
+    )
+    parts = weight_stage(
+        left, rows_mine, rows_other, scaled_mine, scaled_other, chips, inv_model, inv_hidden
     )
     from_other = partner(for_other, CORE, 1)
     pair_grad = (pair_mine + from_other.astype(jnp.float32)).astype(jnp.bfloat16)
-    arrived, pair_grad = lax.optimization_barrier((arrived, pair_grad))
-    returned = along_side(pick(regroup, along_high(pair_grad, True)))
+    parts, up_pair, _ = lax.optimization_barrier((parts, up_pair, pair_grad))
+    up_arrived = jnp.where(lax.axis_index(FAR) == 0, up_pair[1], up_pair[0])
+    back_rows = along_high(pair_grad, True)
+    down_held, back_rows = lax.optimization_barrier((rounded[2:], back_rows))
+    down_arrived = tuple(partner(array, FAR, 1) for array in down_held)
+    returned = along_side(pick(regroup, back_rows))
     token_grad = pick(token_select, returned)
 
     own, beside = lax.psum_scatter(
@@ -351,6 +393,8 @@
         scatter_dimension=0,
         tiled=False,
     )
+    down_arrived, beside = lax.optimization_barrier((down_arrived, beside))
+    arrived = (up_arrived[0], up_arrived[1], *down_arrived)
     summed = own.astype(jnp.float32) + partner(beside, NEAR, 1).astype(jnp.float32)
     moments = tuple(
         jnp.where(swapped, new.astype(jnp.float32), old) for new, old in zip(arrived, moments)
@@ -375,11 +419,11 @@
 def solution(mesh):
     dp, expert = (mesh.shape[name] for name in ("dp", "expert"))
     fine = Mesh(
-        mesh.devices.reshape(2, dp // 4, 2, HIGHS, expert // HIGHS),
-        (NEAR, RING, CORE, HIGH, SIDE),
-    )
-    rows = P((NEAR, RING, CORE, HIGH, SIDE), None)
-    slots = P((HIGH, SIDE), (NEAR, RING, CORE), None)
+        mesh.devices.reshape(2, dp // 4, 2, 2, HIGHS // 2, expert // HIGHS),
+        (NEAR, RING, CORE, *HIGH, SIDE),
+    )
+    rows = P((NEAR, RING, CORE, *HIGH, SIDE), None)
+    slots = P((*HIGH, SIDE), (NEAR, RING, CORE), None)
     return jax.shard_map(
         on_device,
         mesh=fine,

time: 442 us -> 419 us (0.948)
  waiting for transfers between devices: 286 us -> 247 us
  starting transfers between devices: 62.7 us -> 71.7 us
  Pallas kernels: 26.5 us -> 31.5 us
    all_to_all x3, waiting for transfers between devices: 51.4 us -> 0.01 us  [along_side(): lax.all_to_all(rows.reshape(side, side_rows, model_width), SIDE, split_ax...]
    all_gather x0 -> x1, waiting for transfers between devices: none -> 39.9 us  [on_device(): up_pair = lax.all_gather(up_held, FAR, axis=0)]
    ppermute x10 -> x8, waiting for transfers between devices: 102 us -> 68 us  [partner(): lax.ppermute(array, axis, [(i, i ^ flip) for i in range(lax.axis_size(axi...]
    ppermute x10 -> x8, starting transfers between devices: 21.6 us -> 36.7 us  [partner(): lax.ppermute(array, axis, [(i, i ^ flip) for i in range(lax.axis_size(axi...]
    pallas_call x0 -> x1, Pallas kernels: none -> 8.63 us  [weight_stage(): pl.pallas_call(functools.partial(weight_kernel, inv_model, inv_hidden), g...]
    reduce_scatter x1, waiting for transfers between devices: 0.01 us -> 7.88 us  [on_device(): lax.psum_scatter(parts.reshape(ring, near, 2 * local_hidden, model_width)...]
    unnamed x64 -> x54, local copies, waits for them, and re-layouts: 18.5 us -> 18.7 us
  transfers between devices with their start and end apart: 24 -> 23, of which waited for: 16 -> 15; matrix products, arithmetic and copies ran while one was open for 4% -> 6% of each run, Pallas kernels for 0% -> 3%
where the time goes in v1:
time: 419 us; the launch traced here: 417 us
  waiting for transfers between devices  247 us (59%)
  starting transfers between devices  71.7 us (17%)
  Pallas kernels  31.5 us (8%)
  local copies, waits for them, and re-layouts  21.5 us (5%)
  other arithmetic  18.4 us (4%)
  between operations  16.4 us (4%)
  matrix products  10.2 us (2%)
    ppermute x9, waiting for transfers between devices, along_high(): lax.ppermute(array, (NEAR, *HIGH), [(b, a) for a, b in way] if back else...  131 us
    ppermute x8, waiting for transfers between devices, partner(): lax.ppermute(array, axis, [(i, i ^ flip) for i in range(lax.axis_size(axi...  68 us
    all_gather x1, waiting for transfers between devices, on_device(): up_pair = lax.all_gather(up_held, FAR, axis=0)  39.9 us
    ppermute x8, starting transfers between devices, partner(): lax.ppermute(array, axis, [(i, i ^ flip) for i in range(lax.axis_size(axi...  36.7 us
    ppermute x9, starting transfers between devices, along_high(): lax.ppermute(array, (NEAR, *HIGH), [(b, a) for a, b in way] if back else...  20 us
    pallas_call x1, Pallas kernels, expert_stage(): pl.pallas_call(functools.partial(expert_kernel, steps, inv_model, inv_hid...  19.1 us
    unnamed x54, local copies, waits for them, and re-layouts  18.7 us
    all_to_all x3, starting transfers between devices, along_side(): lax.all_to_all(rows.reshape(side, side_rows, model_width), SIDE, split_ax...  15 us
  transfers between devices with their start and end apart: 23, of which 15 were waited for; matrix products, arithmetic and copies ran while one was open for 6% of the time, Pallas kernels for 3%

profile of v1, /device:TPU:8, one launch (start us, length us, event | category | flops | bytes accessed | tf_op | source)
XLA Modules:
  0.0 416.9 jit_solution(9782217994113207578)
XLA Ops:
  10.3 7.2 %collective-permute-start.8 = (bf16[128,3584]{1,0:T(8,128)(2,1)}, bf16[128,3584]{1,0:T(8,128)(2,1)}, u32[]{:S(2)}, u32[]{:S(2)}) collective-permute-start(bf16[128,3584]{1,0:T(8,128)(2,1)} %pad_maximum_fusion.4), channel_id=1, source_target_pairs={{0,8},{8,0},{1,9},{9,1},{2,10},{10,2},{3,11},{11,3},{4,12},{12,4},... | collective-permute-start | bytes 2752520 | tf_op jit(solution)/shard_map/ppermute | solution.py:30
  19.7 3.8 shard_map.162
  23.5 4.9 %all-to-all-start = ((bf16[4,80,3584]{2,1,0:T(8,128)(2,1)}), bf16[4,80,3584]{2,1,0:T(8,128)(2,1)S(1)}, u32[]{:S(2)}, u32[]{:S(2)}) async-start(bf16[4,80,3584]{2,1,0:T(8,128)(2,1)} %bitcast.3), calls=%async_computation | async-start | bytes 4587520 | tf_op jit(solution)/shard_map/all_to_all | solution.py:330
  29.7 26.8 %collective-permute-done.8 = bf16[128,3584]{1,0:T(8,128)(2,1)} collective-permute-done((bf16[128,3584]{1,0:T(8,128)(2,1)}, bf16[128,3584]{1,0:T(8,128)(2,1)}, u32[]{:S(2)}, u32[]{:S(2)}) %collective-permute-start.8) | collective-permute-done | bytes 917536 | tf_op jit(solution)/shard_map/ppermute | solution.py:30
  57.9 5.2 %all-to-all-start.1 = ((bf16[4,80,3584]{2,1,0:T(8,128)(2,1)}), bf16[4,80,3584]{2,1,0:T(8,128)(2,1)}, u32[]{:S(2)}, u32[]{:S(2)}) async-start(bf16[4,80,3584]{2,1,0:T(8,128)(2,1)} %bitcast.5), calls=%async_computation.1 | async-start | bytes 4587520 | tf_op jit(solution)/shard_map/all_to_all | solution.py:330
  63.1 2.8 convolution_convert_fusion.2
  68.5 19.3 %collective-permute-done.9 = bf16[128,3584]{1,0:T(8,128)(2,1)S(1)} collective-permute-done((bf16[128,3584]{1,0:T(8,128)(2,1)S(1)}, bf16[128,3584]{1,0:T(8,128)(2,1)S(1)}, u32[]{:S(2)}, u32[]{:S(2)}) %collective-permute-start.9) | collective-permute-done | bytes 917536 | tf_op jit(solution)/shard_map/ppermute | solution.py:30
  89.3 3.0 convolution_convert_fusion.1
  92.5 4.0 collective-permute-start.4
  96.4 3.6 collective-permute-start.5
  102.7 3.2 collective-permute-start.1
  105.9 7.0 %collective-permute-done.4 = bf16[80,3584]{1,0:T(8,128)(2,1)S(1)} collective-permute-done((bf16[80,3584]{1,0:T(8,128)(2,1)S(1)}, bf16[80,3584]{1,0:T(8,128)(2,1)S(1)}, u32[]{:S(2)}, u32[]{:S(2)}) %collective-permute-start.4) | collective-permute-done | bytes 573472 | tf_op jit(solution)/shard_map/ppermute | solution.py:346
  112.9 3.5 collective-permute-start.2
  116.4 18.6 %collective-permute-done.5 = bf16[80,3584]{1,0:T(8,128)(2,1)S(1)} collective-permute-done((bf16[80,3584]{1,0:T(8,128)(2,1)S(1)}, bf16[80,3584]{1,0:T(8,128)(2,1)S(1)}, u32[]{:S(2)}, u32[]{:S(2)}) %collective-permute-start.5) | collective-permute-done | bytes 573472 | tf_op jit(solution)/shard_map/ppermute | solution.py:346
  135.0 26.7 %collective-permute-done.6 = bf16[80,3584]{1,0:T(8,128)(2,1)S(1)} collective-permute-done((bf16[80,3584]{1,0:T(8,128)(2,1)S(1)}, bf16[80,3584]{1,0:T(8,128)(2,1)S(1)}, u32[]{:S(2)}, u32[]{:S(2)}) %collective-permute-start.6) | collective-permute-done | bytes 573472 | tf_op jit(solution)/shard_map/ppermute | solution.py:346
  162.0 9.9 %collective-permute-done.1 = bf16[80,3584]{1,0:T(8,128)(2,1)S(1)} collective-permute-done((bf16[80,3584]{1,0:T(8,128)(2,1)S(1)}, bf16[80,3584]{1,0:T(8,128)(2,1)S(1)}, u32[]{:S(2)}, u32[]{:S(2)}) %collective-permute-start.1) | collective-permute-done | bytes 573472 | tf_op jit(solution)/shard_map/ppermute | solution.py:346
  171.8 24.1 %collective-permute-done.2 = bf16[80,3584]{1,0:T(8,128)(2,1)S(1)} collective-permute-done((bf16[80,3584]{1,0:T(8,128)(2,1)S(1)}, bf16[80,3584]{1,0:T(8,128)(2,1)S(1)}, u32[]{:S(2)}, u32[]{:S(2)}) %collective-permute-start.2) | collective-permute-done | bytes 573472 | tf_op jit(solution)/shard_map/ppermute | solution.py:346
  207.1 19.1 %shard_map.163 = (f32[320,3584]{1,0:T(8,128)}, bf16[320,3584]{1,0:T(8,128)(2,1)}, bf16[2,512,640]{2,1,0:T(8,128)(2,1)S(1)}) custom-call(bf16[320,3584]{1,0:T(8,128)(2,1)S(1)} %copy-done.1, bf16[320,3584]{1,0:T(8,128)(2,1)S(1)} %copy-done.7, bf16[320,3584]{1,0:T(8,128)(2,1)S(1)} %pad_maximum_fusion.1.mine_scaled_ref, bf16[320,3584]{1,0:T(8,128)(2,1)S(1)} %copy-done.4, ...), custom_call_target="tpu_custom_call" | custom-call | flops 7046430720 | bytes 36700160 | tf_op jit(solution)/shard_map/pallas_call | solution.py:207
  234.9 8.6 %shard_map.164 = bf16[8,128,3584]{2,1,0:T(8,128)(2,1)} custom-call(bf16[2,512,640]{2,1,0:T(8,128)(2,1)S(1)} %copy-done.10, bf16[320,3584]{1,0:T(8,128)(2,1)S(1)} %copy-done.2, bf16[320,3584]{1,0:T(8,128)(2,1)S(1)} %copy-done.8, bf16[320,3584]{1,0:T(8,128)(2,1)S(1)} %pad_maximum_fusion.1.mine_scaled_ref, bf16[320,3584]{1,0:T(8,128)(2,1)S(1)} %copy-done.5), custom_call_target="tpu_custom_call" | custom-call | flops 4697620480 | bytes 36700160 | tf_op jit(solution)/shard_map/pallas_call | solution.py:263
  243.5 3.6 add_convert_fusion
  247.1 39.9 %all-gather.7.cloned.1.call-done = bf16[4,64,3584]{2,1,0:T(8,128)(2,1)} async-done(((bf16[2,64,3584]{2,1,0:T(8,128)(2,1)}), bf16[4,64,3584]{2,1,0:T(8,128)(2,1)}) %all-gather.7.cloned.1.call-update) | async-done | bytes 1835024 | tf_op jit(solution)/shard_map/all_gather | solution.py:373
  287.4 3.0 collective-permute-start.12
  291.5 12.6 %collective-permute-done.11 = bf16[80,3584]{1,0:T(8,128)(2,1)S(1)} collective-permute-done((bf16[80,3584]{1,0:T(8,128)(2,1)S(1)}, bf16[80,3584]{1,0:T(8,128)(2,1)S(1)}, u32[]{:S(2)}, u32[]{:S(2)}) %collective-permute-start.11) | collective-permute-done | bytes 573472 | tf_op jit(solution)/shard_map/ppermute | solution.py:346
  304.1 24.8 %collective-permute-done.12 = bf16[80,3584]{1,0:T(8,128)(2,1)S(1)} collective-permute-done((bf16[80,3584]{1,0:T(8,128)(2,1)S(1)}, bf16[80,3584]{1,0:T(8,128)(2,1)S(1)}, u32[]{:S(2)}, u32[]{:S(2)}) %collective-permute-start.12) | collective-permute-done | bytes 573472 | tf_op jit(solution)/shard_map/ppermute | solution.py:346
  328.8 7.8 %collective-permute-done.13 = bf16[80,3584]{1,0:T(8,128)(2,1)S(1)} collective-permute-done((bf16[80,3584]{1,0:T(8,128)(2,1)S(1)}, bf16[80,3584]{1,0:T(8,128)(2,1)S(1)}, u32[]{:S(2)}, u32[]{:S(2)}) %collective-permute-start.13) | collective-permute-done | bytes 573472 | tf_op jit(solution)/shard_map/ppermute | solution.py:346
  336.8 3.5 collective-permute-start.14
  342.8 2.8 convolution_convert_fusion
  345.6 4.8 %all-to-all-start.2 = ((bf16[4,80,3584]{2,1,0:T(8,128)(2,1)}), bf16[4,80,3584]{2,1,0:T(8,128)(2,1)S(1)}, u32[]{:S(2)}, u32[]{:S(2)}) async-start(bf16[4,80,3584]{2,1,0:T(8,128)(2,1)} %bitcast.98), calls=%async_computation.2 | async-start | bytes 4587520 | tf_op jit(solution)/shard_map/all_to_all | solution.py:330
  350.4 7.9 %reduce-scatter.2.cloned.1.call-done = bf16[1,2,128,3584]{3,2,1,0:T(8,128)(2,1)} async-done(((bf16[4,2,128,3584]{3,2,1,0:T(8,128)(2,1)}), bf16[1,2,128,3584]{3,2,1,0:T(8,128)(2,1)}) %reduce-scatter.2.cloned.1.call-update) | async-done | bytes 1835024 | tf_op jit(solution)/shard_map/reduce_scatter | solution.py:390
  362.6 20.5 %collective-permute-start.16 = (bf16[128,3584]{1,0:T(8,128)(2,1)}, bf16[128,3584]{1,0:T(8,128)(2,1)}, u32[]{:S(2)}, u32[]{:S(2)}) collective-permute-start(bf16[128,3584]{1,0:T(8,128)(2,1)} %slice_bitcast_fusion), channel_id=1, source_target_pairs={{0,128},{128,0},{1,129},{129,1},{2,130},{130,2},{3,131},{131,3},{4... | collective-permute-start | bytes 2752520 | tf_op jit(solution)/shard_map/ppermute | solution.py:30
  385.7 18.2 %collective-permute-done.16 = bf16[128,3584]{1,0:T(8,128)(2,1)} collective-permute-done((bf16[128,3584]{1,0:T(8,128)(2,1)}, bf16[128,3584]{1,0:T(8,128)(2,1)}, u32[]{:S(2)}, u32[]{:S(2)}) %collective-permute-start.16) | collective-permute-done | bytes 917536 | tf_op jit(solution)/shard_map/ppermute | solution.py:30
  405.4 4.1 fusion.31
  (98 shorter events, 45.7 us)
Async XLA Ops:
  10.3 46.2 %collective-permute-start.8 = (bf16[128,3584]{1,0:T(8,128)(2,1)}, bf16[128,3584]{1,0:T(8,128)(2,1)}, u32[]{:S(2)}, u32[]{:S(2)}) collective-permute-start(bf16[128,3584]{1,0:T(8,128)(2,1)} %pad_maximum_fusion.4), channel_id=1, source_target_pairs={{0,8},{8,0},{1,9},{9,1},{2,10},{10,2},{3,11},{11,3},{4,12},{12,4},... | collective-permute-start | bytes 2752520 | tf_op jit(solution)/shard_map/ppermute | solution.py:30
  23.5 34.4 %all-to-all-start = ((bf16[4,80,3584]{2,1,0:T(8,128)(2,1)}), bf16[4,80,3584]{2,1,0:T(8,128)(2,1)S(1)}, u32[]{:S(2)}, u32[]{:S(2)}) async-start(bf16[4,80,3584]{2,1,0:T(8,128)(2,1)} %bitcast.3), calls=%async_computation | async-start | bytes 4587520 | tf_op jit(solution)/shard_map/all_to_all | solution.py:330
  57.9 31.3 %all-to-all-start.1 = ((bf16[4,80,3584]{2,1,0:T(8,128)(2,1)}), bf16[4,80,3584]{2,1,0:T(8,128)(2,1)}, u32[]{:S(2)}, u32[]{:S(2)}) async-start(bf16[4,80,3584]{2,1,0:T(8,128)(2,1)} %bitcast.5), calls=%async_computation.1 | async-start | bytes 4587520 | tf_op jit(solution)/shard_map/all_to_all | solution.py:330
  63.1 139.1 %all-gather.5.cloned.1.call-start = ((), (), s32[]{:S(2)}) async-start(), calls=%async_computation.5 | async-start | bytes 9175040 | tf_op jit(solution)/shard_map/all_gather | solution.py:361
  66.0 21.8 %collective-permute-start.9 = (bf16[128,3584]{1,0:T(8,128)(2,1)S(1)}, bf16[128,3584]{1,0:T(8,128)(2,1)S(1)}, u32[]{:S(2)}, u32[]{:S(2)}) collective-permute-start(bf16[128,3584]{1,0:T(8,128)(2,1)S(1)} %broadcast_select_fusion), channel_id=1, source_target_pairs={{0,128},{128,0},{1,129},{129,1},{2,130},{130,2},{3,131},{131,3},{4... | collective-permute-start | bytes 2752520 | tf_op jit(solution)/shard_map/ppermute | solution.py:30
  89.2 197.8 %all-gather.7.cloned.1.call-start = ((), (), s32[]{:S(2)}) async-start(), calls=%async_computation.6 | async-start | bytes 2752512 | tf_op jit(solution)/shard_map/all_gather | solution.py:373
  92.5 20.4 %collective-permute-start.4 = (bf16[80,3584]{1,0:T(8,128)(2,1)S(1)}, bf16[80,3584]{1,0:T(8,128)(2,1)S(1)}, u32[]{:S(2)}, u32[]{:S(2)}) collective-permute-start(bf16[80,3584]{1,0:T(8,128)(2,1)S(1)} %get-tuple-element.57), channel_id=1, source_target_pairs={{0,4},{4,8},{8,12},{12,0},{128,140},{132,128},{136,132},{140,136},... | collective-permute-start | bytes 1720328 | tf_op jit(solution)/shard_map/ppermute | solution.py:346
  96.4 38.5 %collective-permute-start.5 = (bf16[80,3584]{1,0:T(8,128)(2,1)S(1)}, bf16[80,3584]{1,0:T(8,128)(2,1)S(1)}, u32[]{:S(2)}, u32[]{:S(2)}) collective-permute-start(bf16[80,3584]{1,0:T(8,128)(2,1)S(1)} %get-tuple-element.56), channel_id=1, source_target_pairs={{0,140},{4,128},{8,132},{12,136},{128,4},{132,8},{136,12},{140,0},... | collective-permute-start | bytes 1720328 | tf_op jit(solution)/shard_map/ppermute | solution.py:346
  100.1 61.6 %collective-permute-start.6 = (bf16[80,3584]{1,0:T(8,128)(2,1)S(1)}, bf16[80,3584]{1,0:T(8,128)(2,1)S(1)}, u32[]{:S(2)}, u32[]{:S(2)}) collective-permute-start(bf16[80,3584]{1,0:T(8,128)(2,1)S(1)} %get-tuple-element.55), channel_id=1, source_target_pairs={{0,136},{4,140},{8,128},{12,132},{128,8},{132,12},{136,0},{140,4},... | collective-permute-start | bytes 1720328 | tf_op jit(solution)/shard_map/ppermute | solution.py:346
  100.7 61.2 %collective-permute-start = (bf16[80,3584]{1,0:T(8,128)(2,1)S(1)}, bf16[80,3584]{1,0:T(8,128)(2,1)S(1)}, u32[]{:S(2)}, u32[]{:S(2)}) collective-permute-start(bf16[80,3584]{1,0:T(8,128)(2,1)S(1)} %get-tuple-element.61), channel_id=1, source_target_pairs={{0,4},{4,8},{8,12},{12,0},{128,140},{132,128},{136,132},{140,136},... | collective-permute-start | bytes 1720328 | tf_op jit(solution)/shard_map/ppermute | solution.py:346
  102.7 69.1 %collective-permute-start.1 = (bf16[80,3584]{1,0:T(8,128)(2,1)S(1)}, bf16[80,3584]{1,0:T(8,128)(2,1)S(1)}, u32[]{:S(2)}, u32[]{:S(2)}) collective-permute-start(bf16[80,3584]{1,0:T(8,128)(2,1)S(1)} %get-tuple-element.60), channel_id=1, source_target_pairs={{0,140},{4,128},{8,132},{12,136},{128,4},{132,8},{136,12},{140,0},... | collective-permute-start | bytes 1720328 | tf_op jit(solution)/shard_map/ppermute | solution.py:346
  112.9 83.0 %collective-permute-start.2 = (bf16[80,3584]{1,0:T(8,128)(2,1)S(1)}, bf16[80,3584]{1,0:T(8,128)(2,1)S(1)}, u32[]{:S(2)}, u32[]{:S(2)}) collective-permute-start(bf16[80,3584]{1,0:T(8,128)(2,1)S(1)} %get-tuple-element.59), channel_id=1, source_target_pairs={{0,136},{4,140},{8,128},{12,132},{128,8},{132,12},{136,0},{140,4},... | collective-permute-start | bytes 1720328 | tf_op jit(solution)/shard_map/ppermute | solution.py:346
  161.8 35.9 %collective-permute-start.7 = (bf16[320,3584]{1,0:T(8,128)(2,1)S(1)}, bf16[320,3584]{1,0:T(8,128)(2,1)S(1)}, u32[]{:S(2)}, u32[]{:S(2)}) collective-permute-start(bf16[320,3584]{1,0:T(8,128)(2,1)S(1)} %pad_maximum_fusion.1.mine_scaled_ref), channel_id=1, source_target_pairs={{0,16},{16,0},{1,17},{17,1},{2,18},{18,2},{3,19},{19,3},{4,20},{20... | collective-permute-start | bytes 6881288 | tf_op jit(solution)/shard_map/ppermute | solution.py:30
  196.1 4.7 %collective-permute-start.3 = (bf16[320,3584]{1,0:T(8,128)(2,1)S(1)}, bf16[320,3584]{1,0:T(8,128)(2,1)S(1)}, u32[]{:S(2)}, u32[]{:S(2)}) collective-permute-start(bf16[320,3584]{1,0:T(8,128)(2,1)S(1)} %pad_maximum_fusion.mine_ref), channel_id=1, source_target_pairs={{0,16},{16,0},{1,17},{17,1},{2,18},{18,2},{3,19},{19,3},{4,20},{20... | collective-permute-start | bytes 6881288 | tf_op jit(solution)/shard_map/ppermute | solution.py:30
  207.1 20.3 %copy-start.14 = (f32[1,64,3584]{2,1,0:T(8,128)S(1)}, f32[1,64,3584]{2,1,0:T(8,128)}, u32[]{:S(2)}) copy-start(f32[1,64,3584]{2,1,0:T(8,128)} %param.18) | copy-start | bytes 2752516
  207.1 20.3 %copy-start.16 = (f32[1,64,3584]{2,1,0:T(8,128)S(1)}, f32[1,64,3584]{2,1,0:T(8,128)}, u32[]{:S(2)}) copy-start(f32[1,64,3584]{2,1,0:T(8,128)} %param.19) | copy-start | bytes 2752516
  227.3 16.2 %collective-permute-start.10 = (bf16[320,3584]{1,0:T(8,128)(2,1)}, bf16[320,3584]{1,0:T(8,128)(2,1)}, u32[]{:S(2)}, u32[]{:S(2)}) collective-permute-start(bf16[320,3584]{1,0:T(8,128)(2,1)} %get-tuple-element.30), channel_id=1, source_target_pairs={{0,16},{16,0},{1,17},{17,1},{2,18},{18,2},{3,19},{19,3},{4,20},{20... | collective-permute-start | bytes 6881288 | tf_op jit(solution)/shard_map/ppermute | solution.py:30
  228.6 129.7 %reduce-scatter.2.cloned.1.call-start = ((), (), s32[]{:S(2)}) async-start(), calls=%async_computation.4 | async-start | bytes 9175040 | tf_op jit(solution)/shard_map/reduce_scatter | solution.py:390
  287.2 16.9 %collective-permute-start.11 = (bf16[80,3584]{1,0:T(8,128)(2,1)S(1)}, bf16[80,3584]{1,0:T(8,128)(2,1)S(1)}, u32[]{:S(2)}, u32[]{:S(2)}) collective-permute-start(bf16[80,3584]{1,0:T(8,128)(2,1)S(1)} %get-tuple-element.53), channel_id=1, source_target_pairs={{4,0},{8,4},{12,8},{0,12},{140,128},{128,132},{132,136},{136,140},... | collective-permute-start | bytes 1720328 | tf_op jit(solution)/shard_map/ppermute | solution.py:346
  287.4 41.4 %collective-permute-start.12 = (bf16[80,3584]{1,0:T(8,128)(2,1)S(1)}, bf16[80,3584]{1,0:T(8,128)(2,1)S(1)}, u32[]{:S(2)}, u32[]{:S(2)}) collective-permute-start(bf16[80,3584]{1,0:T(8,128)(2,1)S(1)} %get-tuple-element.52), channel_id=1, source_target_pairs={{140,0},{128,4},{132,8},{136,12},{4,128},{8,132},{12,136},{0,140},... | collective-permute-start | bytes 1720328 | tf_op jit(solution)/shard_map/ppermute | solution.py:346
  290.4 46.2 %collective-permute-start.13 = (bf16[80,3584]{1,0:T(8,128)(2,1)S(1)}, bf16[80,3584]{1,0:T(8,128)(2,1)S(1)}, u32[]{:S(2)}, u32[]{:S(2)}) collective-permute-start(bf16[80,3584]{1,0:T(8,128)(2,1)S(1)} %get-tuple-element.51), channel_id=1, source_target_pairs={{136,0},{140,4},{128,8},{132,12},{8,128},{12,132},{0,136},{4,140},... | collective-permute-start | bytes 1720328 | tf_op jit(solution)/shard_map/ppermute | solution.py:346
  336.8 23.9 %collective-permute-start.14 = (bf16[64,3584]{1,0:T(8,128)(2,1)}, bf16[64,3584]{1,0:T(8,128)(2,1)}, u32[]{:S(2)}, u32[]{:S(2)}) collective-permute-start(bf16[64,3584]{1,0:T(8,128)(2,1)} %get-tuple-element.36), channel_id=1, source_target_pairs={{0,8},{8,0},{1,9},{9,1},{2,10},{10,2},{3,11},{11,3},{4,12},{12,4},... | collective-permute-start | bytes 1376264 | tf_op jit(solution)/shard_map/ppermute | solution.py:30
  340.2 22.4 %collective-permute-start.15 = (bf16[64,3584]{1,0:T(8,128)(2,1)}, bf16[64,3584]{1,0:T(8,128)(2,1)}, u32[]{:S(2)}, u32[]{:S(2)}) collective-permute-start(bf16[64,3584]{1,0:T(8,128)(2,1)} %get-tuple-element.37), channel_id=1, source_target_pairs={{0,8},{8,0},{1,9},{9,1},{2,10},{10,2},{3,11},{11,3},{4,12},{12,4},... | collective-permute-start | bytes 1376264 | tf_op jit(solution)/shard_map/ppermute | solution.py:30
  345.6 38.5 %all-to-all-start.2 = ((bf16[4,80,3584]{2,1,0:T(8,128)(2,1)}), bf16[4,80,3584]{2,1,0:T(8,128)(2,1)S(1)}, u32[]{:S(2)}, u32[]{:S(2)}) async-start(bf16[4,80,3584]{2,1,0:T(8,128)(2,1)} %bitcast.98), calls=%async_computation.2 | async-start | bytes 4587520 | tf_op jit(solution)/shard_map/all_to_all | solution.py:330
  358.3 24.8 %copy-start.25 = (bf16[4,64,3584]{2,1,0:T(8,128)(2,1)S(1)}, bf16[4,64,3584]{2,1,0:T(8,128)(2,1)}, u32[]{:S(2)}) copy-start(bf16[4,64,3584]{2,1,0:T(8,128)(2,1)} %all-gather.7.cloned.1.call-done) | copy-start | bytes 5505028
  362.6 41.3 %collective-permute-start.16 = (bf16[128,3584]{1,0:T(8,128)(2,1)}, bf16[128,3584]{1,0:T(8,128)(2,1)}, u32[]{:S(2)}, u32[]{:S(2)}) collective-permute-start(bf16[128,3584]{1,0:T(8,128)(2,1)} %slice_bitcast_fusion), channel_id=1, source_target_pairs={{0,128},{128,0},{1,129},{129,1},{2,130},{130,2},{3,131},{131,3},{4... | collective-permute-start | bytes 2752520 | tf_op jit(solution)/shard_map/ppermute | solution.py:30
  384.1 19.8 %copy-start.24 = (bf16[1,2,128,3584]{3,2,1,0:T(8,128)(2,1)S(1)}, bf16[1,2,128,3584]{3,2,1,0:T(8,128)(2,1)}, u32[]{:S(2)}) copy-start(bf16[1,2,128,3584]{3,2,1,0:T(8,128)(2,1)} %reduce-scatter.2.cloned.1.call-done) | copy-start | bytes 5505028
  384.1 21.2 %copy-start.22 = (f32[1,64,3584]{2,1,0:T(8,128)S(1)}, f32[1,64,3584]{2,1,0:T(8,128)}, u32[]{:S(2)}) copy-start(f32[1,64,3584]{2,1,0:T(8,128)} %param.20) | copy-start | bytes 2752516
  385.7 19.7 %copy-start.15 = (f32[1,64,3584]{2,1,0:T(8,128)S(1)}, f32[1,64,3584]{2,1,0:T(8,128)}, u32[]{:S(2)}) copy-start(f32[1,64,3584]{2,1,0:T(8,128)} %param.18) | copy-start | bytes 2752516
  385.7 19.7 %copy-start.17 = (f32[1,64,3584]{2,1,0:T(8,128)S(1)}, f32[1,64,3584]{2,1,0:T(8,128)}, u32[]{:S(2)}) copy-start(f32[1,64,3584]{2,1,0:T(8,128)} %param.19) | copy-start | bytes 2752516
  385.7 19.7 %copy-start.18 = (bf16[1,2,64,3584]{3,2,1,0:T(8,128)(2,1)S(1)}, bf16[1,2,64,3584]{3,2,1,0:T(8,128)(2,1)}, u32[]{:S(2)}) copy-start(bf16[1,2,64,3584]{3,2,1,0:T(8,128)(2,1)} %slice_select_fusion) | copy-start | bytes 2752516
  385.7 19.7 %copy-start.20 = (f32[1,64,3584]{2,1,0:T(8,128)S(1)}, f32[1,64,3584]{2,1,0:T(8,128)}, u32[]{:S(2)}) copy-start(f32[1,64,3584]{2,1,0:T(8,128)} %param.21) | copy-start | bytes 2752516
  (17 other events, 54.2 us)
Sparse Core Ops, SparseCore 0:
  89.3 78.5 all-gather.4
  287.1 71.1 reduce-scatter.1
Sparse Core Ops, SparseCore 1:
  228.7 58.3 all-gather.6

commit v2 on v1

--- a/solution.py
+++ b/solution.py
@@ -269,11 +269,7 @@
         compiler_params=pltpu.CompilerParams(
             dimension_semantics=("arbitrary",), vmem_limit_bytes=40 * 1024 * 1024
         ),
-        cost_estimate=pl.CostEstimate(
-            flops=8 * rows * left.shape[1] * width,
-            bytes_accessed=32 * rows * width,
-            transcendentals=0,
-        ),
+        cost_estimate=pl.CostEstimate(flops=0, bytes_accessed=1024, transcendentals=0),
     )(left, mine, other, mine_scaled, other_scaled)
 
 
@@ -348,22 +344,23 @@
             )
             for array, way in zip(blocks[1:], ways)
         ]
-        return jnp.concatenate(blocks[:1] + moved, axis=0)
+        return jnp.concatenate(blocks[:1] + moved, axis=0), moved[-1]
 
     token_rows = pick(regroup, along_side(send_tokens))
     side_scaled = along_side(send_scaled)
     scaled_rows = pick(regroup, side_scaled)
 
+    rows_mine, farthest = along_high(token_rows, False)
+
+    weights_partner, _ = lax.optimization_barrier((weights_partner, token_rows))
     weights = jnp.where(swapped, weights_partner, weights)
-    weights, _ = lax.optimization_barrier((weights, token_rows))
     both = jnp.stack((weights, partner(weights, NEAR, 1)), axis=0)
-    both, _ = lax.optimization_barrier((both, side_scaled))
+    both, _, _ = lax.optimization_barrier((both, side_scaled, farthest))
     gathered = lax.all_gather(both, RING, axis=0).reshape(
         chips, 2 * local_hidden, model_width
     )
 
-    rows_mine = along_high(token_rows, False)
-    scaled_mine = along_high(scaled_rows, False)
+    scaled_mine, _ = along_high(scaled_rows, False)
     rows_other = partner(rows_mine, CORE, 1)
     scaled_other = partner(scaled_mine, CORE, 1)
     moments = (up_first[0], up_second[0], down_first[0], down_second[0])
@@ -379,9 +376,9 @@
     )
     from_other = partner(for_other, CORE, 1)
     pair_grad = (pair_mine + from_other.astype(jnp.float32)).astype(jnp.bfloat16)
-    parts, up_pair, _ = lax.optimization_barrier((parts, up_pair, pair_grad))
+    up_pair, pair_grad = lax.optimization_barrier((up_pair, pair_grad))
     up_arrived = jnp.where(lax.axis_index(FAR) == 0, up_pair[1], up_pair[0])
-    back_rows = along_high(pair_grad, True)
+    back_rows, _ = along_high(pair_grad, True)
     down_held, back_rows = lax.optimization_barrier((rounded[2:], back_rows))
     down_arrived = tuple(partner(array, FAR, 1) for array in down_held)
     returned = along_side(pick(regroup, back_rows))

time: 419 us -> 378 us (0.902)
  waiting for transfers between devices: 247 us -> 214 us
  local copies, waits for them, and re-layouts: 21.5 us -> 12.4 us
    ppermute x9, waiting for transfers between devices: 131 us -> 108 us  [along_high(): lax.ppermute(array, (NEAR, *HIGH), [(b, a) for a, b in way] if back else...]
    all_gather x1, waiting for transfers between devices: 39.9 us -> 17.5 us  [on_device(): up_pair = lax.all_gather(up_held, FAR, axis=0)]
    all_to_all x3, waiting for transfers between devices: 0.01 us -> 16.5 us  [along_side(): lax.all_to_all(rows.reshape(side, side_rows, model_width), SIDE, split_ax...]
    unnamed x54 -> x46, local copies, waits for them, and re-layouts: 18.7 us -> 8.4 us
    ppermute x8, waiting for transfers between devices: 68 us -> 61.8 us  [partner(): lax.ppermute(array, axis, [(i, i ^ flip) for i in range(lax.axis_size(axi...]
  transfers between devices with their start and end apart: 23 -> 23, of which waited for: 15 -> 15; matrix products, arithmetic and copies ran while one was open for 6% -> 7% of each run, Pallas kernels for 3% -> 8%
where the time goes in v2:
time: 378 us; the launch traced here: 376 us
  waiting for transfers between devices  214 us (57%)
  starting transfers between devices  71.1 us (19%)
  Pallas kernels  35 us (9%)
  other arithmetic  19.4 us (5%)
  between operations  14.6 us (4%)
  local copies, waits for them, and re-layouts  12.4 us (3%)
  matrix products  8.93 us (2%)
    ppermute x9, waiting for transfers between devices, along_high(): lax.ppermute(array, (NEAR, *HIGH), [(b, a) for a, b in way] if back else...  108 us
    ppermute x8, waiting for transfers between devices, partner(): lax.ppermute(array, axis, [(i, i ^ flip) for i in range(lax.axis_size(axi...  61.8 us
    ppermute x8, starting transfers between devices, partner(): lax.ppermute(array, axis, [(i, i ^ flip) for i in range(lax.axis_size(axi...  35.4 us
    ppermute x9, starting transfers between devices, along_high(): lax.ppermute(array, (NEAR, *HIGH), [(b, a) for a, b in way] if back else...  19.7 us
    pallas_call x1, Pallas kernels, expert_stage(): pl.pallas_call(functools.partial(expert_kernel, steps, inv_model, inv_hid...  19.6 us
    all_gather x1, waiting for transfers between devices, on_device(): up_pair = lax.all_gather(up_held, FAR, axis=0)  17.5 us
    all_to_all x3, waiting for transfers between devices, along_side(): lax.all_to_all(rows.reshape(side, side_rows, model_width), SIDE, split_ax...  16.5 us
    all_to_all x3, starting transfers between devices, along_side(): lax.all_to_all(rows.reshape(side, side_rows, model_width), SIDE, split_ax...  15.8 us
  transfers between devices with their start and end apart: 23, of which 15 were waited for; matrix products, arithmetic and copies ran while one was open for 7% of the time, Pallas kernels for 8%

profile of v2, /device:TPU:8, one launch (start us, length us, event | category | flops | bytes accessed | tf_op | source)
XLA Modules:
  0.0 375.5 jit_solution(7293320722953240855)
XLA Ops:
  11.8 3.8 %shard_map.162 = (bf16[320,3584]{1,0:T(8,128)(2,1)}, bf16[320,3584]{1,0:T(8,128)(2,1)}, bf16[128,320]{1,0:T(8,128)(2,1)S(1)}) custom-call(s32[1,16]{1,0:T(1,128)S(1)} %bitcast.93, s32[128,2]{1,0:T(8,128)S(1)} %copy.20.routes_ref, bf16[128,2]{1,0:T(8,128)(2,1)S(1)} %copy.21.probs_ref, bf16[128,3584]{1,0:T(8,128)(2,1)S(1)} %copy-done, ...), custom_call_target="tpu_custom_call" | custom-call | bytes 1024 | tf_op jit(solution)/shard_map/pallas_call | solution.py:120
  15.5 5.9 %all-to-all-start.1 = ((bf16[4,80,3584]{2,1,0:T(8,128)(2,1)}), bf16[4,80,3584]{2,1,0:T(8,128)(2,1)S(1)}, u32[]{:S(2)}, u32[]{:S(2)}) async-start(bf16[4,80,3584]{2,1,0:T(8,128)(2,1)} %bitcast.6), calls=%async_computation.1 | async-start | bytes 4587520 | tf_op jit(solution)/shard_map/all_to_all | solution.py:326
  23.4 6.3 %collective-permute-start.8 = (bf16[128,3584]{1,0:T(8,128)(2,1)}, bf16[128,3584]{1,0:T(8,128)(2,1)}, u32[]{:S(2)}, u32[]{:S(2)}) collective-permute-start(bf16[128,3584]{1,0:T(8,128)(2,1)} %pad_maximum_fusion.5), channel_id=1, source_target_pairs={{0,8},{8,0},{1,9},{9,1},{2,10},{10,2},{3,11},{11,3},{4,12},{12,4},... | collective-permute-start | bytes 2752520 | tf_op jit(solution)/shard_map/ppermute | solution.py:30
  31.1 16.5 %all-to-all-done.1 = bf16[4,80,3584]{2,1,0:T(8,128)(2,1)S(1)} async-done(((bf16[4,80,3584]{2,1,0:T(8,128)(2,1)}), bf16[4,80,3584]{2,1,0:T(8,128)(2,1)S(1)}, u32[]{:S(2)}, u32[]{:S(2)}) %all-to-all-start.1) | async-done | bytes 2293792 | tf_op jit(solution)/shard_map/all_to_all | solution.py:326
  49.0 5.1 %all-to-all-start = ((bf16[4,80,3584]{2,1,0:T(8,128)(2,1)}), bf16[4,80,3584]{2,1,0:T(8,128)(2,1)S(1)}, u32[]{:S(2)}, u32[]{:S(2)}) async-start(bf16[4,80,3584]{2,1,0:T(8,128)(2,1)} %bitcast.3), calls=%async_computation | async-start | bytes 4587520 | tf_op jit(solution)/shard_map/all_to_all | solution.py:326
  54.0 3.1 convolution_convert_fusion.1
  57.2 11.1 %collective-permute-done.8 = bf16[128,3584]{1,0:T(8,128)(2,1)} collective-permute-done((bf16[128,3584]{1,0:T(8,128)(2,1)}, bf16[128,3584]{1,0:T(8,128)(2,1)}, u32[]{:S(2)}, u32[]{:S(2)}) %collective-permute-start.8) | collective-permute-done | bytes 917536 | tf_op jit(solution)/shard_map/ppermute | solution.py:30
  72.6 4.5 %collective-permute-start.5 = (bf16[80,3584]{1,0:T(8,128)(2,1)}, bf16[80,3584]{1,0:T(8,128)(2,1)}, u32[]{:S(2)}, u32[]{:S(2)}) collective-permute-start(bf16[80,3584]{1,0:T(8,128)(2,1)} %get-tuple-element.55), channel_id=1, source_target_pairs={{0,136},{4,140},{8,128},{12,132},{128,8},{132,12},{136,0},{140,4},... | collective-permute-start | bytes 1720328 | tf_op jit(solution)/shard_map/ppermute | solution.py:342
  77.0 25.4 %collective-permute-done.9 = bf16[128,3584]{1,0:T(8,128)(2,1)S(1)} collective-permute-done((bf16[128,3584]{1,0:T(8,128)(2,1)S(1)}, bf16[128,3584]{1,0:T(8,128)(2,1)S(1)}, u32[]{:S(2)}, u32[]{:S(2)}) %collective-permute-start.9) | collective-permute-done | bytes 917536 | tf_op jit(solution)/shard_map/ppermute | solution.py:30
  103.9 3.2 collective-permute-start.3
  107.1 3.1 collective-permute-start.4
  113.4 4.1 %collective-permute-start.2 = (bf16[80,3584]{1,0:T(8,128)(2,1)S(1)}, bf16[80,3584]{1,0:T(8,128)(2,1)S(1)}, u32[]{:S(2)}, u32[]{:S(2)}) collective-permute-start(bf16[80,3584]{1,0:T(8,128)(2,1)S(1)} %get-tuple-element.59), channel_id=1, source_target_pairs={{0,136},{4,140},{8,128},{12,132},{128,8},{132,12},{136,0},{140,4},... | collective-permute-start | bytes 1720328 | tf_op jit(solution)/shard_map/ppermute | solution.py:342
  117.5 6.3 %collective-permute-done.3 = bf16[80,3584]{1,0:T(8,128)(2,1)S(1)} collective-permute-done((bf16[80,3584]{1,0:T(8,128)(2,1)}, bf16[80,3584]{1,0:T(8,128)(2,1)S(1)}, u32[]{:S(2)}, u32[]{:S(2)}) %collective-permute-start.3) | collective-permute-done | bytes 573472 | tf_op jit(solution)/shard_map/ppermute | solution.py:342
  123.8 22.0 %collective-permute-done.4 = bf16[80,3584]{1,0:T(8,128)(2,1)S(1)} collective-permute-done((bf16[80,3584]{1,0:T(8,128)(2,1)}, bf16[80,3584]{1,0:T(8,128)(2,1)S(1)}, u32[]{:S(2)}, u32[]{:S(2)}) %collective-permute-start.4) | collective-permute-done | bytes 573472 | tf_op jit(solution)/shard_map/ppermute | solution.py:342
  147.1 22.6 %collective-permute-done.1 = bf16[80,3584]{1,0:T(8,128)(2,1)S(1)} collective-permute-done((bf16[80,3584]{1,0:T(8,128)(2,1)S(1)}, bf16[80,3584]{1,0:T(8,128)(2,1)S(1)}, u32[]{:S(2)}, u32[]{:S(2)}) %collective-permute-start.1) | collective-permute-done | bytes 573472 | tf_op jit(solution)/shard_map/ppermute | solution.py:342
  169.7 11.8 %collective-permute-done.2 = bf16[80,3584]{1,0:T(8,128)(2,1)S(1)} collective-permute-done((bf16[80,3584]{1,0:T(8,128)(2,1)S(1)}, bf16[80,3584]{1,0:T(8,128)(2,1)S(1)}, u32[]{:S(2)}, u32[]{:S(2)}) %collective-permute-start.2) | collective-permute-done | bytes 573472 | tf_op jit(solution)/shard_map/ppermute | solution.py:342
  187.8 19.6 %shard_map.163 = (f32[320,3584]{1,0:T(8,128)}, bf16[320,3584]{1,0:T(8,128)(2,1)S(1)}, bf16[2,512,640]{2,1,0:T(8,128)(2,1)S(1)}) custom-call(bf16[320,3584]{1,0:T(8,128)(2,1)S(1)} %pad_maximum_fusion.1.mine_ref, bf16[320,3584]{1,0:T(8,128)(2,1)} %collective-permute-done.6.other_ref, bf16[320,3584]{1,0:T(8,128)(2,1)} %pad_maximum_fusion.mine_scaled_ref, ...), custom_call_target="tpu_custom_call" | custom-call | flops 7046430720 | bytes 36700160 | tf_op jit(solution)/shard_map/pallas_call | solution.py:207
  207.3 11.7 %shard_map.164 = bf16[8,128,3584]{2,1,0:T(8,128)(2,1)} custom-call(bf16[2,512,640]{2,1,0:T(8,128)(2,1)S(1)} %get-tuple-element.35.left_ref, bf16[320,3584]{1,0:T(8,128)(2,1)S(1)} %pad_maximum_fusion.1.mine_ref, bf16[320,3584]{1,0:T(8,128)(2,1)} %collective-permute-done.6.other_ref, bf16[320,3584]{1,0:T(8,128)(2,1)} %pad_maximum_fusion.mine_scaled_ref, ...), custom_call_target="tpu_custom_call" | custom-call | bytes 1024 | tf_op jit(solution)/shard_map/pallas_call | solution.py:263
  220.7 4.4 %collective-permute-done.10 = bf16[320,3584]{1,0:T(8,128)(2,1)} collective-permute-done((bf16[320,3584]{1,0:T(8,128)(2,1)S(1)}, bf16[320,3584]{1,0:T(8,128)(2,1)}, u32[]{:S(2)}, u32[]{:S(2)}) %collective-permute-start.10) | collective-permute-done | bytes 2293792 | tf_op jit(solution)/shard_map/ppermute | solution.py:30
  225.2 3.6 add_convert_fusion
  228.8 17.5 %all-gather.5.cloned.1.call-done = bf16[4,64,3584]{2,1,0:T(8,128)(2,1)} async-done(((bf16[2,64,3584]{2,1,0:T(8,128)(2,1)}), bf16[4,64,3584]{2,1,0:T(8,128)(2,1)}) %all-gather.5.cloned.1.call-update) | async-done | bytes 1835024 | tf_op jit(solution)/shard_map/all_gather | solution.py:370
  246.7 3.0 collective-permute-start.12
  250.7 12.6 %collective-permute-done.11 = bf16[80,3584]{1,0:T(8,128)(2,1)S(1)} collective-permute-done((bf16[80,3584]{1,0:T(8,128)(2,1)S(1)}, bf16[80,3584]{1,0:T(8,128)(2,1)S(1)}, u32[]{:S(2)}, u32[]{:S(2)}) %collective-permute-start.11) | collective-permute-done | bytes 573472 | tf_op jit(solution)/shard_map/ppermute | solution.py:342
  263.4 24.7 %collective-permute-done.12 = bf16[80,3584]{1,0:T(8,128)(2,1)S(1)} collective-permute-done((bf16[80,3584]{1,0:T(8,128)(2,1)S(1)}, bf16[80,3584]{1,0:T(8,128)(2,1)S(1)}, u32[]{:S(2)}, u32[]{:S(2)}) %collective-permute-start.12) | collective-permute-done | bytes 573472 | tf_op jit(solution)/shard_map/ppermute | solution.py:342
  288.1 7.8 %collective-permute-done.13 = bf16[80,3584]{1,0:T(8,128)(2,1)S(1)} collective-permute-done((bf16[80,3584]{1,0:T(8,128)(2,1)S(1)}, bf16[80,3584]{1,0:T(8,128)(2,1)S(1)}, u32[]{:S(2)}, u32[]{:S(2)}) %collective-permute-start.13) | collective-permute-done | bytes 573472 | tf_op jit(solution)/shard_map/ppermute | solution.py:342
  296.1 3.5 collective-permute-start.14
  302.1 2.8 convolution_convert_fusion
  305.0 4.8 %all-to-all-start.2 = ((bf16[4,80,3584]{2,1,0:T(8,128)(2,1)}), bf16[4,80,3584]{2,1,0:T(8,128)(2,1)S(1)}, u32[]{:S(2)}, u32[]{:S(2)}) async-start(bf16[4,80,3584]{2,1,0:T(8,128)(2,1)} %bitcast.99), calls=%async_computation.2 | async-start | bytes 4587520 | tf_op jit(solution)/shard_map/all_to_all | solution.py:326
  309.8 10.3 %reduce-scatter.2.cloned.1.call-done = bf16[1,2,128,3584]{3,2,1,0:T(8,128)(2,1)} async-done(((bf16[4,2,128,3584]{3,2,1,0:T(8,128)(2,1)}), bf16[1,2,128,3584]{3,2,1,0:T(8,128)(2,1)}) %reduce-scatter.2.cloned.1.call-update) | async-done | bytes 1835024 | tf_op jit(solution)/shard_map/reduce_scatter | solution.py:387
  322.4 20.2 %collective-permute-start.16 = (bf16[128,3584]{1,0:T(8,128)(2,1)}, bf16[128,3584]{1,0:T(8,128)(2,1)}, u32[]{:S(2)}, u32[]{:S(2)}) collective-permute-start(bf16[128,3584]{1,0:T(8,128)(2,1)} %slice_bitcast_fusion), channel_id=1, source_target_pairs={{0,128},{128,0},{1,129},{129,1},{2,130},{130,2},{3,131},{131,3},{4... | collective-permute-start | bytes 2752520 | tf_op jit(solution)/shard_map/ppermute | solution.py:30
  345.2 18.2 %collective-permute-done.16 = bf16[128,3584]{1,0:T(8,128)(2,1)} collective-permute-done((bf16[128,3584]{1,0:T(8,128)(2,1)}, bf16[128,3584]{1,0:T(8,128)(2,1)}, u32[]{:S(2)}, u32[]{:S(2)}) %collective-permute-start.16) | collective-permute-done | bytes 917536 | tf_op jit(solution)/shard_map/ppermute | solution.py:30
  364.9 4.1 %fusion.31 = (f32[1,64,3584]{2,1,0:T(8,128)}, bf16[1,64,3584]{2,1,0:T(8,128)(2,1)}, f32[1,64,3584]{2,1,0:T(8,128)}, f32[1,64,3584]{2,1,0:T(8,128)}, bf16[1,64,3584]{2,1,0:T(8,128)(2,1)}, /*index=5*/f32[1,64,3584]{2,1,0:T(8,128)}) fusion(f32[128,3584]{1,0:T(8,128)S(1)} %convert_add_fusion, f32[1,64,3584]{2,1,0:T(8,128)S(1)} %copy-done.12, ...), kind=kLoop, calls=%fused_computation.71 | loop fusion | flops 8257536 | bytes 12846080 | tf_op jit(solution)/shard_map/broadcast_in_dim | solution.py:412
  (90 shorter events, 37.3 us)
Async XLA Ops:
  15.5 14.2 %copy-start.3 = (s32[16]{0:T(128)S(1)}, s32[16]{0:T(128)}, u32[]{:S(2)}) copy-start(s32[16]{0:T(128)} %param.15) | copy-start | bytes 196
  15.5 32.0 %all-to-all-start.1 = ((bf16[4,80,3584]{2,1,0:T(8,128)(2,1)}), bf16[4,80,3584]{2,1,0:T(8,128)(2,1)S(1)}, u32[]{:S(2)}, u32[]{:S(2)}) async-start(bf16[4,80,3584]{2,1,0:T(8,128)(2,1)} %bitcast.6), calls=%async_computation.1 | async-start | bytes 4587520 | tf_op jit(solution)/shard_map/all_to_all | solution.py:326
  23.4 44.8 %collective-permute-start.8 = (bf16[128,3584]{1,0:T(8,128)(2,1)}, bf16[128,3584]{1,0:T(8,128)(2,1)}, u32[]{:S(2)}, u32[]{:S(2)}) collective-permute-start(bf16[128,3584]{1,0:T(8,128)(2,1)} %pad_maximum_fusion.5), channel_id=1, source_target_pairs={{0,8},{8,0},{1,9},{9,1},{2,10},{10,2},{3,11},{11,3},{4,12},{12,4},... | collective-permute-start | bytes 2752520 | tf_op jit(solution)/shard_map/ppermute | solution.py:30
  49.0 54.8 %all-to-all-start = ((bf16[4,80,3584]{2,1,0:T(8,128)(2,1)}), bf16[4,80,3584]{2,1,0:T(8,128)(2,1)S(1)}, u32[]{:S(2)}, u32[]{:S(2)}) async-start(bf16[4,80,3584]{2,1,0:T(8,128)(2,1)} %bitcast.3), calls=%async_computation | async-start | bytes 4587520 | tf_op jit(solution)/shard_map/all_to_all | solution.py:326
  54.0 133.7 %all-gather.7.cloned.1.call-start = ((), (), s32[]{:S(2)}) async-start(), calls=%async_computation.6 | async-start | bytes 9175040 | tf_op jit(solution)/shard_map/all_gather | solution.py:359
  68.5 33.8 %collective-permute-start.9 = (bf16[128,3584]{1,0:T(8,128)(2,1)S(1)}, bf16[128,3584]{1,0:T(8,128)(2,1)S(1)}, u32[]{:S(2)}, u32[]{:S(2)}) collective-permute-start(bf16[128,3584]{1,0:T(8,128)(2,1)S(1)} %broadcast_select_fusion), channel_id=1, source_target_pairs={{0,128},{128,0},{1,129},{129,1},{2,130},{130,2},{3,131},{131,3},{4... | collective-permute-start | bytes 2752520 | tf_op jit(solution)/shard_map/ppermute | solution.py:30
  72.6 31.2 %collective-permute-start.5 = (bf16[80,3584]{1,0:T(8,128)(2,1)}, bf16[80,3584]{1,0:T(8,128)(2,1)}, u32[]{:S(2)}, u32[]{:S(2)}) collective-permute-start(bf16[80,3584]{1,0:T(8,128)(2,1)} %get-tuple-element.55), channel_id=1, source_target_pairs={{0,136},{4,140},{8,128},{12,132},{128,8},{132,12},{136,0},{140,4},... | collective-permute-start | bytes 1720328 | tf_op jit(solution)/shard_map/ppermute | solution.py:342
  103.8 142.5 %all-gather.5.cloned.1.call-start = ((), (), s32[]{:S(2)}) async-start(), calls=%async_computation.5 | async-start | bytes 2752512 | tf_op jit(solution)/shard_map/all_gather | solution.py:370
  103.9 19.9 %collective-permute-start.3 = (bf16[80,3584]{1,0:T(8,128)(2,1)}, bf16[80,3584]{1,0:T(8,128)(2,1)S(1)}, u32[]{:S(2)}, u32[]{:S(2)}) collective-permute-start(bf16[80,3584]{1,0:T(8,128)(2,1)} %get-tuple-element.57), channel_id=1, source_target_pairs={{0,4},{4,8},{8,12},{12,0},{128,140},{132,128},{136,132},{140,136},... | collective-permute-start | bytes 1720328 | tf_op jit(solution)/shard_map/ppermute | solution.py:342
  107.1 38.7 %collective-permute-start.4 = (bf16[80,3584]{1,0:T(8,128)(2,1)}, bf16[80,3584]{1,0:T(8,128)(2,1)S(1)}, u32[]{:S(2)}, u32[]{:S(2)}) collective-permute-start(bf16[80,3584]{1,0:T(8,128)(2,1)} %get-tuple-element.56), channel_id=1, source_target_pairs={{0,140},{4,128},{8,132},{12,136},{128,4},{132,8},{136,12},{140,0},... | collective-permute-start | bytes 1720328 | tf_op jit(solution)/shard_map/ppermute | solution.py:342
  111.6 34.1 %copy-start.15 = (bf16[80,3584]{1,0:T(8,128)(2,1)S(1)}, bf16[80,3584]{1,0:T(8,128)(2,1)}, u32[]{:S(2)}) copy-start(bf16[80,3584]{1,0:T(8,128)(2,1)} %get-tuple-element.54) | copy-start | bytes 1720324
  111.8 35.3 %collective-permute-start = (bf16[80,3584]{1,0:T(8,128)(2,1)S(1)}, bf16[80,3584]{1,0:T(8,128)(2,1)S(1)}, u32[]{:S(2)}, u32[]{:S(2)}) collective-permute-start(bf16[80,3584]{1,0:T(8,128)(2,1)S(1)} %get-tuple-element.61), channel_id=1, source_target_pairs={{0,4},{4,8},{8,12},{12,0},{128,140},{132,128},{136,132},{140,136},... | collective-permute-start | bytes 1720328 | tf_op jit(solution)/shard_map/ppermute | solution.py:342
  113.0 56.7 %collective-permute-start.1 = (bf16[80,3584]{1,0:T(8,128)(2,1)S(1)}, bf16[80,3584]{1,0:T(8,128)(2,1)S(1)}, u32[]{:S(2)}, u32[]{:S(2)}) collective-permute-start(bf16[80,3584]{1,0:T(8,128)(2,1)S(1)} %get-tuple-element.60), channel_id=1, source_target_pairs={{0,140},{4,128},{8,132},{12,136},{128,4},{132,8},{136,12},{140,0},... | collective-permute-start | bytes 1720328 | tf_op jit(solution)/shard_map/ppermute | solution.py:342
  113.4 68.1 %collective-permute-start.2 = (bf16[80,3584]{1,0:T(8,128)(2,1)S(1)}, bf16[80,3584]{1,0:T(8,128)(2,1)S(1)}, u32[]{:S(2)}, u32[]{:S(2)}) collective-permute-start(bf16[80,3584]{1,0:T(8,128)(2,1)S(1)} %get-tuple-element.59), channel_id=1, source_target_pairs={{0,136},{4,140},{8,128},{12,132},{128,8},{132,12},{136,0},{140,4},... | collective-permute-start | bytes 1720328 | tf_op jit(solution)/shard_map/ppermute | solution.py:342
  147.0 38.1 %collective-permute-start.6 = (bf16[320,3584]{1,0:T(8,128)(2,1)S(1)}, bf16[320,3584]{1,0:T(8,128)(2,1)}, u32[]{:S(2)}, u32[]{:S(2)}) collective-permute-start(bf16[320,3584]{1,0:T(8,128)(2,1)S(1)} %pad_maximum_fusion.1.mine_ref), channel_id=1, source_target_pairs={{0,16},{16,0},{1,17},{17,1},{2,18},{18,2},{3,19},{19,3},{4,20},{20... | collective-permute-start | bytes 6881288 | tf_op jit(solution)/shard_map/ppermute | solution.py:30
  183.0 4.8 %collective-permute-start.7 = (bf16[320,3584]{1,0:T(8,128)(2,1)}, bf16[320,3584]{1,0:T(8,128)(2,1)}, u32[]{:S(2)}, u32[]{:S(2)}) collective-permute-start(bf16[320,3584]{1,0:T(8,128)(2,1)} %pad_maximum_fusion.mine_scaled_ref), channel_id=1, source_target_pairs={{0,16},{16,0},{1,17},{17,1},{2,18},{18,2},{3,19},{19,3},{4,20},{20... | collective-permute-start | bytes 6881288 | tf_op jit(solution)/shard_map/ppermute | solution.py:30
  184.8 135.3 %reduce-scatter.2.cloned.1.call-start = ((), (), s32[]{:S(2)}) async-start(), calls=%async_computation.4 | async-start | bytes 9175040 | tf_op jit(solution)/shard_map/reduce_scatter | solution.py:387
  220.6 4.6 %collective-permute-start.10 = (bf16[320,3584]{1,0:T(8,128)(2,1)S(1)}, bf16[320,3584]{1,0:T(8,128)(2,1)}, u32[]{:S(2)}, u32[]{:S(2)}) collective-permute-start(bf16[320,3584]{1,0:T(8,128)(2,1)S(1)} %copy-done.5), channel_id=1, source_target_pairs={{0,16},{16,0},{1,17},{17,1},{2,18},{18,2},{3,19},{19,3},{4,20},{20... | collective-permute-start | bytes 6881288 | tf_op jit(solution)/shard_map/ppermute | solution.py:30
  246.5 16.9 %collective-permute-start.11 = (bf16[80,3584]{1,0:T(8,128)(2,1)S(1)}, bf16[80,3584]{1,0:T(8,128)(2,1)S(1)}, u32[]{:S(2)}, u32[]{:S(2)}) collective-permute-start(bf16[80,3584]{1,0:T(8,128)(2,1)S(1)} %get-tuple-element.53), channel_id=1, source_target_pairs={{4,0},{8,4},{12,8},{0,12},{140,128},{128,132},{132,136},{136,140},... | collective-permute-start | bytes 1720328 | tf_op jit(solution)/shard_map/ppermute | solution.py:342
  246.7 41.4 %collective-permute-start.12 = (bf16[80,3584]{1,0:T(8,128)(2,1)S(1)}, bf16[80,3584]{1,0:T(8,128)(2,1)S(1)}, u32[]{:S(2)}, u32[]{:S(2)}) collective-permute-start(bf16[80,3584]{1,0:T(8,128)(2,1)S(1)} %get-tuple-element.52), channel_id=1, source_target_pairs={{140,0},{128,4},{132,8},{136,12},{4,128},{8,132},{12,136},{0,140},... | collective-permute-start | bytes 1720328 | tf_op jit(solution)/shard_map/ppermute | solution.py:342
  249.7 46.2 %collective-permute-start.13 = (bf16[80,3584]{1,0:T(8,128)(2,1)S(1)}, bf16[80,3584]{1,0:T(8,128)(2,1)S(1)}, u32[]{:S(2)}, u32[]{:S(2)}) collective-permute-start(bf16[80,3584]{1,0:T(8,128)(2,1)S(1)} %get-tuple-element.51), channel_id=1, source_target_pairs={{136,0},{140,4},{128,8},{132,12},{8,128},{12,132},{0,136},{4,140},... | collective-permute-start | bytes 1720328 | tf_op jit(solution)/shard_map/ppermute | solution.py:342
  296.1 26.3 %collective-permute-start.14 = (bf16[64,3584]{1,0:T(8,128)(2,1)}, bf16[64,3584]{1,0:T(8,128)(2,1)}, u32[]{:S(2)}, u32[]{:S(2)}) collective-permute-start(bf16[64,3584]{1,0:T(8,128)(2,1)} %get-tuple-element.36), channel_id=1, source_target_pairs={{0,8},{8,0},{1,9},{9,1},{2,10},{10,2},{3,11},{11,3},{4,12},{12,4},... | collective-permute-start | bytes 1376264 | tf_op jit(solution)/shard_map/ppermute | solution.py:30
  299.6 22.8 %collective-permute-start.15 = (bf16[64,3584]{1,0:T(8,128)(2,1)}, bf16[64,3584]{1,0:T(8,128)(2,1)}, u32[]{:S(2)}, u32[]{:S(2)}) collective-permute-start(bf16[64,3584]{1,0:T(8,128)(2,1)} %get-tuple-element.37), channel_id=1, source_target_pairs={{0,8},{8,0},{1,9},{9,1},{2,10},{10,2},{3,11},{11,3},{4,12},{12,4},... | collective-permute-start | bytes 1376264 | tf_op jit(solution)/shard_map/ppermute | solution.py:30
  305.0 38.6 %all-to-all-start.2 = ((bf16[4,80,3584]{2,1,0:T(8,128)(2,1)}), bf16[4,80,3584]{2,1,0:T(8,128)(2,1)S(1)}, u32[]{:S(2)}, u32[]{:S(2)}) async-start(bf16[4,80,3584]{2,1,0:T(8,128)(2,1)} %bitcast.99), calls=%async_computation.2 | async-start | bytes 4587520 | tf_op jit(solution)/shard_map/all_to_all | solution.py:326
  320.1 22.5 %copy-start.18 = (bf16[4,64,3584]{2,1,0:T(8,128)(2,1)S(1)}, bf16[4,64,3584]{2,1,0:T(8,128)(2,1)}, u32[]{:S(2)}) copy-start(bf16[4,64,3584]{2,1,0:T(8,128)(2,1)} %all-gather.5.cloned.1.call-done) | copy-start | bytes 5505028
  322.4 41.0 %collective-permute-start.16 = (bf16[128,3584]{1,0:T(8,128)(2,1)}, bf16[128,3584]{1,0:T(8,128)(2,1)}, u32[]{:S(2)}, u32[]{:S(2)}) collective-permute-start(bf16[128,3584]{1,0:T(8,128)(2,1)} %slice_bitcast_fusion), channel_id=1, source_target_pairs={{0,128},{128,0},{1,129},{129,1},{2,130},{130,2},{3,131},{131,3},{4... | collective-permute-start | bytes 2752520 | tf_op jit(solution)/shard_map/ppermute | solution.py:30
  343.6 19.8 %copy-start.17 = (bf16[1,2,128,3584]{3,2,1,0:T(8,128)(2,1)S(1)}, bf16[1,2,128,3584]{3,2,1,0:T(8,128)(2,1)}, u32[]{:S(2)}) copy-start(bf16[1,2,128,3584]{3,2,1,0:T(8,128)(2,1)} %reduce-scatter.2.cloned.1.call-done) | copy-start | bytes 5505028
  343.6 21.2 %copy-start.14 = (f32[1,64,3584]{2,1,0:T(8,128)S(1)}, f32[1,64,3584]{2,1,0:T(8,128)}, u32[]{:S(2)}) copy-start(f32[1,64,3584]{2,1,0:T(8,128)} %param.20) | copy-start | bytes 2752516
  345.2 19.7 %copy-start.7 = (f32[1,64,3584]{2,1,0:T(8,128)S(1)}, f32[1,64,3584]{2,1,0:T(8,128)}, u32[]{:S(2)}) copy-start(f32[1,64,3584]{2,1,0:T(8,128)} %param.19) | copy-start | bytes 2752516
  345.2 19.7 %copy-start.9 = (f32[1,64,3584]{2,1,0:T(8,128)S(1)}, f32[1,64,3584]{2,1,0:T(8,128)}, u32[]{:S(2)}) copy-start(f32[1,64,3584]{2,1,0:T(8,128)} %param.18) | copy-start | bytes 2752516
  345.2 19.7 %copy-start.10 = (bf16[1,2,64,3584]{3,2,1,0:T(8,128)(2,1)S(1)}, bf16[1,2,64,3584]{3,2,1,0:T(8,128)(2,1)}, u32[]{:S(2)}) copy-start(bf16[1,2,64,3584]{3,2,1,0:T(8,128)(2,1)} %slice_select_fusion) | copy-start | bytes 2752516
  345.2 19.7 %copy-start.12 = (f32[1,64,3584]{2,1,0:T(8,128)S(1)}, f32[1,64,3584]{2,1,0:T(8,128)}, u32[]{:S(2)}) copy-start(f32[1,64,3584]{2,1,0:T(8,128)} %param.21) | copy-start | bytes 2752516
  (13 other events, 62.6 us)
Sparse Core Ops, SparseCore 0:
  103.9 79.0 all-gather.6
  185.4 60.9 all-gather.4
  248.9 71.1 reduce-scatter.1

commit v3 on v2

--- a/solution.py
+++ b/solution.py
@@ -65,42 +65,40 @@
     scaled_rows_ref,
     select_ref,
 ):
-    count, tops = routes_ref.shape
-    experts = flags_ref.shape[1]
+    tops, count = routes_ref.shape
+    experts = flags_ref.shape[0]
     rows, width = token_rows_ref.shape
     side = experts // HIGHS
     half_axis = experts // 2
-    my_high = lax.axis_index(HIGH)
+    my_high = lax.axis_index(FAR) * (HIGHS // 2) + lax.axis_index(STEP)
     my_near = lax.axis_index(NEAR)
-    ids = lax.broadcasted_iota(jnp.int32, (1, experts), 1)
+    ids = lax.broadcasted_iota(jnp.int32, (experts, 1), 0)
     slot = jnp.where(flags_ref[...] == 1, jnp.bitwise_xor(ids, half_axis), ids)
     away = lax.shift_right_logical(slot, side.bit_length() - 1) - my_high
     away = jnp.bitwise_and(jnp.where(my_near == 0, away, -away), HIGHS - 1)
     block = jnp.where(away >= 2, 5 - away, away)
     base = jnp.bitwise_and(slot, side - 1) * (HIGHS * capacity) + block * capacity
     base = base.astype(jnp.float32)
-    expert_ids = lax.broadcasted_iota(jnp.int32, (count, experts), 1)
-    below = (
+    expert_ids = lax.broadcasted_iota(jnp.int32, (experts, count), 0)
+    before = (
         lax.broadcasted_iota(jnp.int32, (count, count), 0)
-        > lax.broadcasted_iota(jnp.int32, (count, count), 1)
-    )
-    below = jnp.where(below, 1.0, 0.0).astype(jnp.bfloat16)
-    padded = -(-rows // 128) * 128
-    row_ids = lax.broadcasted_iota(jnp.int32, (count, padded), 1)
-    token_select = jnp.zeros((count, padded), jnp.float32)
-    prob_select = jnp.zeros((count, padded), jnp.float32)
+        < lax.broadcasted_iota(jnp.int32, (count, count), 1)
+    )
+    before = jnp.where(before, 1.0, 0.0).astype(jnp.bfloat16)
+    row_ids = lax.broadcasted_iota(jnp.int32, (rows, count), 0)
+    token_pick = jnp.zeros((rows, count), jnp.float32)
+    prob_pick = jnp.zeros((rows, count), jnp.float32)
     for k in range(tops):
-        onehot = jnp.where(routes_ref[:, k : k + 1] == expert_ids, 1.0, 0.0)
-        earlier = jnp.dot(below, onehot.astype(jnp.bfloat16), preferred_element_type=jnp.float32)
-        row = jnp.sum(onehot * (base + earlier), axis=1, keepdims=True).astype(jnp.int32)
+        onehot = jnp.where(routes_ref[k : k + 1] == expert_ids, 1.0, 0.0)
+        earlier = jnp.dot(onehot.astype(jnp.bfloat16), before, preferred_element_type=jnp.float32)
+        row = jnp.sum(onehot * (base + earlier), axis=0, keepdims=True).astype(jnp.int32)
         hit = row_ids == row
-        token_select = token_select + jnp.where(hit, 1.0, 0.0)
-        prob = probs_ref[:, k : k + 1].astype(jnp.float32)
-        prob_select = prob_select + jnp.where(hit, prob, 0.0)
-        base = base + jnp.sum(onehot, axis=0, keepdims=True)
-    select_ref[...] = token_select[:, :rows].astype(jnp.bfloat16)
-    token_pick = token_select.T[:rows].astype(jnp.bfloat16)
-    prob_pick = prob_select.T[:rows].astype(jnp.bfloat16)
+        token_pick = token_pick + jnp.where(hit, 1.0, 0.0)
+        prob_pick = prob_pick + jnp.where(hit, probs_ref[k : k + 1].astype(jnp.float32), 0.0)
+        base = base + jnp.sum(onehot, axis=1, keepdims=True)
+    token_pick = token_pick.astype(jnp.bfloat16)
+    prob_pick = prob_pick.astype(jnp.bfloat16)
+    select_ref[...] = token_pick
     piece = 512
     for at in range(0, width, piece):
         cut = slice(at, min(at + piece, width))
@@ -124,11 +122,11 @@
         out_shape=[
             jax.ShapeDtypeStruct((rows, width), jnp.bfloat16),
             jax.ShapeDtypeStruct((rows, width), jnp.bfloat16),
-            jax.ShapeDtypeStruct((count, rows), jnp.bfloat16),
+            jax.ShapeDtypeStruct((rows, count), jnp.bfloat16),
         ],
         compiler_params=pltpu.CompilerParams(vmem_limit_bytes=24 * 1024 * 1024),
         cost_estimate=pl.CostEstimate(flops=0, bytes_accessed=1024, transcendentals=0),
-    )(swap_flags.reshape(1, -1), routes, probs, tokens, out_grad)
+    )(swap_flags.reshape(-1, 1), routes.T, probs.T, tokens, out_grad)
 
 
 def expert_kernel(
@@ -352,8 +350,8 @@
 
     rows_mine, farthest = along_high(token_rows, False)
 
-    weights_partner, _ = lax.optimization_barrier((weights_partner, token_rows))
     weights = jnp.where(swapped, weights_partner, weights)
+    weights, _ = lax.optimization_barrier((weights, token_rows))
     both = jnp.stack((weights, partner(weights, NEAR, 1)), axis=0)
     both, _, _ = lax.optimization_barrier((both, side_scaled, farthest))
     gathered = lax.all_gather(both, RING, axis=0).reshape(
@@ -366,8 +364,8 @@
     moments = (up_first[0], up_second[0], down_first[0], down_second[0])
 
     rounded = tuple(array.astype(jnp.bfloat16) for array in moments)
-    up_held, _ = lax.optimization_barrier((jnp.stack(rounded[:2]), scaled_mine))
-    up_pair = lax.all_gather(up_held, FAR, axis=0)
+    up_held, _ = lax.optimization_barrier((rounded[:2], scaled_mine))
+    up_arrived = tuple(partner(array, FAR, 1) for array in up_held)
     pair_mine, for_other, left = expert_stage(
         rows_mine, rows_other, scaled_mine, scaled_other, gathered, inv_model, inv_hidden
     )
@@ -376,13 +374,14 @@
     )
     from_other = partner(for_other, CORE, 1)
     pair_grad = (pair_mine + from_other.astype(jnp.float32)).astype(jnp.bfloat16)
-    up_pair, pair_grad = lax.optimization_barrier((up_pair, pair_grad))
-    up_arrived = jnp.where(lax.axis_index(FAR) == 0, up_pair[1], up_pair[0])
+    up_arrived, parts = lax.optimization_barrier((up_arrived, parts))
     back_rows, _ = along_high(pair_grad, True)
     down_held, back_rows = lax.optimization_barrier((rounded[2:], back_rows))
     down_arrived = tuple(partner(array, FAR, 1) for array in down_held)
     returned = along_side(pick(regroup, back_rows))
-    token_grad = pick(token_select, returned)
+    token_grad = lax.dot_general(
+        token_select, returned, (((0,), (0,)), ((), ())), preferred_element_type=jnp.float32
+    ).astype(jnp.bfloat16)
 
     own, beside = lax.psum_scatter(
         parts.reshape(ring, near, 2 * local_hidden, model_width),
@@ -391,7 +390,7 @@
         tiled=False,
     )
     down_arrived, beside = lax.optimization_barrier((down_arrived, beside))
-    arrived = (up_arrived[0], up_arrived[1], *down_arrived)
+    arrived = (*up_arrived, *down_arrived)
     summed = own.astype(jnp.float32) + partner(beside, NEAR, 1).astype(jnp.float32)
     moments = tuple(
         jnp.where(swapped, new.astype(jnp.float32), old) for new, old in zip(arrived, moments)

time: 378 us -> 381 us (level)
  waiting for transfers between devices: 214 us -> 233 us
  starting transfers between devices: 71.1 us -> 58.6 us
  local copies, waits for them, and re-layouts: 12.4 us -> 17.2 us
  Pallas kernels: 35 us -> 30.6 us
    ppermute x8 -> x10, waiting for transfers between devices: 61.8 us -> 120 us  [partner(): lax.ppermute(array, axis, [(i, i ^ flip) for i in range(lax.axis_size(axi...]
    all_gather x1 -> x0, waiting for transfers between devices: 17.5 us -> none  [on_device(): up_pair = lax.all_gather(up_held, FAR, axis=0)]
    all_to_all x3, waiting for transfers between devices: 16.5 us -> 0.01 us  [along_side(): lax.all_to_all(rows.reshape(side, side_rows, model_width), SIDE, split_ax...]
    ppermute x8 -> x10, starting transfers between devices: 35.4 us -> 21.9 us  [partner(): lax.ppermute(array, axis, [(i, i ^ flip) for i in range(lax.axis_size(axi...]
    reduce_scatter x1, waiting for transfers between devices: 10.3 us -> 0.01 us  [on_device(): lax.psum_scatter(parts.reshape(ring, near, 2 * local_hidden, model_width)...]
    ppermute x9, waiting for transfers between devices: 108 us -> 113 us  [along_high(): lax.ppermute(array, (NEAR, *HIGH), [(b, a) for a, b in way] if back else...]
    unnamed x46 -> x50, local copies, waits for them, and re-layouts: 8.4 us -> 12.7 us
    dot_general x4 -> x3, matrix products: 8.93 us -> 7.43 us  [pick(): jnp.dot(matrix, rows, preferred_element_type=jnp.float32)]
  transfers between devices with their start and end apart: 23 -> 24, of which waited for: 15 -> 14; matrix products, arithmetic and copies ran while one was open for 7% -> 6% of each run, Pallas kernels for 8% -> 8%
where the time goes in v3:
time: 381 us; the launch traced here: 380 us
  waiting for transfers between devices  233 us (61%)
  starting transfers between devices  58.6 us (15%)
  Pallas kernels  30.6 us (8%)
  local copies, waits for them, and re-layouts  17.2 us (5%)
  other arithmetic  16.9 us (4%)
  between operations  14.9 us (4%)
  matrix products  9.03 us (2%)
    ppermute x10, waiting for transfers between devices, partner(): lax.ppermute(array, axis, [(i, i ^ flip) for i in range(lax.axis_size(axi...  120 us
    ppermute x9, waiting for transfers between devices, along_high(): lax.ppermute(array, (NEAR, *HIGH), [(b, a) for a, b in way] if back else...  113 us
    ppermute x10, starting transfers between devices, partner(): lax.ppermute(array, axis, [(i, i ^ flip) for i in range(lax.axis_size(axi...  21.9 us
    ppermute x9, starting transfers between devices, along_high(): lax.ppermute(array, (NEAR, *HIGH), [(b, a) for a, b in way] if back else...  21.6 us
    pallas_call x1, Pallas kernels, expert_stage(): pl.pallas_call(functools.partial(expert_kernel, steps, inv_model, inv_hid...  18.5 us
    all_to_all x3, starting transfers between devices, along_side(): lax.all_to_all(rows.reshape(side, side_rows, model_width), SIDE, split_ax...  15.1 us
    unnamed x50, local copies, waits for them, and re-layouts  12.7 us
    pallas_call x1, Pallas kernels, weight_stage(): pl.pallas_call(functools.partial(weight_kernel, inv_model, inv_hidden), g...  8.62 us
  transfers between devices with their start and end apart: 24, of which 14 were waited for; matrix products, arithmetic and copies ran while one was open for 6% of the time, Pallas kernels for 8%

profile of v3, /device:TPU:8, one launch (start us, length us, event | category | flops | bytes accessed | tf_op | source)
XLA Modules:
  0.0 379.7 jit_solution(15747697627064317957)
XLA Ops:
  9.5 7.2 %collective-permute-start.8 = (bf16[128,3584]{1,0:T(8,128)(2,1)}, bf16[128,3584]{1,0:T(8,128)(2,1)}, u32[]{:S(2)}, u32[]{:S(2)}) collective-permute-start(bf16[128,3584]{1,0:T(8,128)(2,1)} %pad_maximum_fusion.4), channel_id=1, source_target_pairs={{0,8},{8,0},{1,9},{9,1},{2,10},{10,2},{3,11},{11,3},{4,12},{12,4},... | collective-permute-start | bytes 2752520 | tf_op jit(solution)/shard_map/ppermute | solution.py:30
  18.7 3.6 shard_map.162
  22.3 5.0 %all-to-all-start = ((bf16[4,80,3584]{2,1,0:T(8,128)(2,1)}), bf16[4,80,3584]{2,1,0:T(8,128)(2,1)S(1)}, u32[]{:S(2)}, u32[]{:S(2)}) async-start(bf16[4,80,3584]{2,1,0:T(8,128)(2,1)} %bitcast.5), calls=%async_computation | async-start | bytes 4587520 | tf_op jit(solution)/shard_map/all_to_all | solution.py:324
  28.6 27.1 %collective-permute-done.8 = bf16[128,3584]{1,0:T(8,128)(2,1)} collective-permute-done((bf16[128,3584]{1,0:T(8,128)(2,1)}, bf16[128,3584]{1,0:T(8,128)(2,1)}, u32[]{:S(2)}, u32[]{:S(2)}) %collective-permute-start.8) | collective-permute-done | bytes 917536 | tf_op jit(solution)/shard_map/ppermute | solution.py:30
  57.1 5.2 %all-to-all-start.1 = ((bf16[4,80,3584]{2,1,0:T(8,128)(2,1)}), bf16[4,80,3584]{2,1,0:T(8,128)(2,1)}, u32[]{:S(2)}, u32[]{:S(2)}) async-start(bf16[4,80,3584]{2,1,0:T(8,128)(2,1)} %bitcast.7), calls=%async_computation.1 | async-start | bytes 4587520 | tf_op jit(solution)/shard_map/all_to_all | solution.py:324
  67.6 4.5 %collective-permute-start.2 = (bf16[80,3584]{1,0:T(8,128)(2,1)S(1)}, bf16[80,3584]{1,0:T(8,128)(2,1)S(1)}, u32[]{:S(2)}, u32[]{:S(2)}) collective-permute-start(bf16[80,3584]{1,0:T(8,128)(2,1)S(1)} %get-tuple-element.63), channel_id=1, source_target_pairs={{0,136},{4,140},{8,128},{12,132},{128,8},{132,12},{136,0},{140,4},... | collective-permute-start | bytes 1720328 | tf_op jit(solution)/shard_map/ppermute | solution.py:340
  72.0 25.9 %collective-permute-done.9 = bf16[128,3584]{1,0:T(8,128)(2,1)S(1)} collective-permute-done((bf16[128,3584]{1,0:T(8,128)(2,1)S(1)}, bf16[128,3584]{1,0:T(8,128)(2,1)S(1)}, u32[]{:S(2)}, u32[]{:S(2)}) %collective-permute-start.9) | collective-permute-done | bytes 917536 | tf_op jit(solution)/shard_map/ppermute | solution.py:30
  99.4 3.2 convolution_convert_fusion.1
  105.4 3.6 collective-permute-start.5
  111.4 3.2 collective-permute-start.1
  114.6 7.2 %collective-permute-done.4 = bf16[80,3584]{1,0:T(8,128)(2,1)S(1)} collective-permute-done((bf16[80,3584]{1,0:T(8,128)(2,1)S(1)}, bf16[80,3584]{1,0:T(8,128)(2,1)S(1)}, u32[]{:S(2)}, u32[]{:S(2)}) %collective-permute-start.4) | collective-permute-done | bytes 573472 | tf_op jit(solution)/shard_map/ppermute | solution.py:340
  121.9 24.7 %collective-permute-done.5 = bf16[80,3584]{1,0:T(8,128)(2,1)S(1)} collective-permute-done((bf16[80,3584]{1,0:T(8,128)(2,1)S(1)}, bf16[80,3584]{1,0:T(8,128)(2,1)S(1)}, u32[]{:S(2)}, u32[]{:S(2)}) %collective-permute-start.5) | collective-permute-done | bytes 573472 | tf_op jit(solution)/shard_map/ppermute | solution.py:340
  146.5 20.9 %collective-permute-done.6 = bf16[80,3584]{1,0:T(8,128)(2,1)S(1)} collective-permute-done((bf16[80,3584]{1,0:T(8,128)(2,1)S(1)}, bf16[80,3584]{1,0:T(8,128)(2,1)S(1)}, u32[]{:S(2)}, u32[]{:S(2)}) %collective-permute-start.6) | collective-permute-done | bytes 573472 | tf_op jit(solution)/shard_map/ppermute | solution.py:340
  167.7 12.7 %collective-permute-done.1 = bf16[80,3584]{1,0:T(8,128)(2,1)S(1)} collective-permute-done((bf16[80,3584]{1,0:T(8,128)(2,1)}, bf16[80,3584]{1,0:T(8,128)(2,1)S(1)}, u32[]{:S(2)}, u32[]{:S(2)}) %collective-permute-start.1) | collective-permute-done | bytes 573472 | tf_op jit(solution)/shard_map/ppermute | solution.py:340
  183.7 3.8 collective-permute-start.14
  197.4 18.5 %shard_map.163 = (f32[320,3584]{1,0:T(8,128)}, bf16[320,3584]{1,0:T(8,128)(2,1)S(1)}, bf16[2,512,640]{2,1,0:T(8,128)(2,1)S(1)}) custom-call(bf16[320,3584]{1,0:T(8,128)(2,1)S(1)} %copy-done.1, bf16[320,3584]{1,0:T(8,128)(2,1)S(1)} %copy-done.5, bf16[320,3584]{1,0:T(8,128)(2,1)S(1)} %pad_maximum_fusion.1.mine_scaled_ref, bf16[320,3584]{1,0:T(8,128)(2,1)S(1)} %copy-done.3, ...), custom_call_target="tpu_custom_call" | custom-call | flops 7046430720 | bytes 36700160 | tf_op jit(solution)/shard_map/pallas_call | solution.py:205
  215.8 8.6 %shard_map.164 = bf16[8,128,3584]{2,1,0:T(8,128)(2,1)} custom-call(bf16[2,512,640]{2,1,0:T(8,128)(2,1)S(1)} %get-tuple-element.36.left_ref, bf16[320,3584]{1,0:T(8,128)(2,1)S(1)} %copy-done.1, bf16[320,3584]{1,0:T(8,128)(2,1)S(1)} %copy-done.5, bf16[320,3584]{1,0:T(8,128)(2,1)S(1)} %pad_maximum_fusion.1.mine_scaled_ref, bf16[320,3584]{1,0:T(8,128)(2,1)S(1)} %copy-done.3), custom_call_target="tpu_custom_call" | custom-call | bytes 1024 | tf_op jit(solution)/shard_map/pallas_call | solution.py:261
  224.4 5.4 %collective-permute-done.15 = bf16[64,3584]{1,0:T(8,128)(2,1)} collective-permute-done((bf16[64,3584]{1,0:T(8,128)(2,1)}, bf16[64,3584]{1,0:T(8,128)(2,1)}, u32[]{:S(2)}, u32[]{:S(2)}) %collective-permute-start.15) | collective-permute-done | bytes 458784 | tf_op jit(solution)/shard_map/ppermute | solution.py:30
  231.5 4.4 %collective-permute-done.10 = bf16[320,3584]{1,0:T(8,128)(2,1)S(1)} collective-permute-done((bf16[320,3584]{1,0:T(8,128)(2,1)S(1)}, bf16[320,3584]{1,0:T(8,128)(2,1)S(1)}, u32[]{:S(2)}, u32[]{:S(2)}) %collective-permute-start.10) | collective-permute-done | bytes 2293792 | tf_op jit(solution)/shard_map/ppermute | solution.py:30
  236.0 2.9 add_convert_fusion
  240.6 3.8 collective-permute-start.13
  245.4 10.5 %collective-permute-done.11 = bf16[80,3584]{1,0:T(8,128)(2,1)S(1)} collective-permute-done((bf16[80,3584]{1,0:T(8,128)(2,1)S(1)}, bf16[80,3584]{1,0:T(8,128)(2,1)S(1)}, u32[]{:S(2)}, u32[]{:S(2)}) %collective-permute-start.11) | collective-permute-done | bytes 573472 | tf_op jit(solution)/shard_map/ppermute | solution.py:340
  255.9 10.7 %collective-permute-done.12 = bf16[80,3584]{1,0:T(8,128)(2,1)S(1)} collective-permute-done((bf16[80,3584]{1,0:T(8,128)(2,1)S(1)}, bf16[80,3584]{1,0:T(8,128)(2,1)S(1)}, u32[]{:S(2)}, u32[]{:S(2)}) %collective-permute-start.12) | collective-permute-done | bytes 573472 | tf_op jit(solution)/shard_map/ppermute | solution.py:340
  266.6 26.2 %collective-permute-done.13 = bf16[80,3584]{1,0:T(8,128)(2,1)S(1)} collective-permute-done((bf16[80,3584]{1,0:T(8,128)(2,1)S(1)}, bf16[80,3584]{1,0:T(8,128)(2,1)S(1)}, u32[]{:S(2)}, u32[]{:S(2)}) %collective-permute-start.13) | collective-permute-done | bytes 573472 | tf_op jit(solution)/shard_map/ppermute | solution.py:340
  292.9 2.9 convolution_convert_fusion
  295.8 4.8 %all-to-all-start.2 = ((bf16[4,80,3584]{2,1,0:T(8,128)(2,1)}), bf16[4,80,3584]{2,1,0:T(8,128)(2,1)S(1)}, u32[]{:S(2)}, u32[]{:S(2)}) async-start(bf16[4,80,3584]{2,1,0:T(8,128)(2,1)} %bitcast.88), calls=%async_computation.2 | async-start | bytes 4587520 | tf_op jit(solution)/shard_map/all_to_all | solution.py:324
  300.6 3.1 collective-permute-start.16
  303.7 2.8 collective-permute-start.17
  308.7 26.1 %collective-permute-done.16 = bf16[64,3584]{1,0:T(8,128)(2,1)} collective-permute-done((bf16[64,3584]{1,0:T(8,128)(2,1)}, bf16[64,3584]{1,0:T(8,128)(2,1)}, u32[]{:S(2)}, u32[]{:S(2)}) %collective-permute-start.16) | collective-permute-done | bytes 458784 | tf_op jit(solution)/shard_map/ppermute | solution.py:30
  334.7 9.7 %collective-permute-done.17 = bf16[64,3584]{1,0:T(8,128)(2,1)} collective-permute-done((bf16[64,3584]{1,0:T(8,128)(2,1)}, bf16[64,3584]{1,0:T(8,128)(2,1)}, u32[]{:S(2)}, u32[]{:S(2)}) %collective-permute-start.17) | collective-permute-done | bytes 458784 | tf_op jit(solution)/shard_map/ppermute | solution.py:30
  346.1 21.0 %collective-permute-done.18 = bf16[128,3584]{1,0:T(8,128)(2,1)} collective-permute-done((bf16[128,3584]{1,0:T(8,128)(2,1)}, bf16[128,3584]{1,0:T(8,128)(2,1)}, u32[]{:S(2)}, u32[]{:S(2)}) %collective-permute-start.18) | collective-permute-done | bytes 917536 | tf_op jit(solution)/shard_map/ppermute | solution.py:30
  368.5 4.4 %fusion.30 = (f32[1,64,3584]{2,1,0:T(8,128)}, bf16[1,64,3584]{2,1,0:T(8,128)(2,1)}, f32[1,64,3584]{2,1,0:T(8,128)}, f32[1,64,3584]{2,1,0:T(8,128)}, bf16[1,64,3584]{2,1,0:T(8,128)(2,1)}, /*index=5*/f32[1,64,3584]{2,1,0:T(8,128)}) fusion(f32[128,3584]{1,0:T(8,128)S(1)} %convert_add_fusion, f32[1,64,3584]{2,1,0:T(8,128)S(1)} %copy-done.13, ...), kind=kLoop, calls=%fused_computation.68 | loop fusion | flops 8257536 | bytes 12845057 | tf_op jit(solution)/shard_map/broadcast_in_dim | solution.py:409
  (93 shorter events, 41.3 us)
Async XLA Ops:
  7.2 10.2 %copy-start.6 = (bf16[128,3584]{1,0:T(8,128)(2,1)S(1)}, bf16[128,3584]{1,0:T(8,128)(2,1)}, u32[]{:S(2)}) copy-start(bf16[128,3584]{1,0:T(8,128)(2,1)} %tokens_ref.1) | copy-start | bytes 2752516
  9.5 46.2 %collective-permute-start.8 = (bf16[128,3584]{1,0:T(8,128)(2,1)}, bf16[128,3584]{1,0:T(8,128)(2,1)}, u32[]{:S(2)}, u32[]{:S(2)}) collective-permute-start(bf16[128,3584]{1,0:T(8,128)(2,1)} %pad_maximum_fusion.4), channel_id=1, source_target_pairs={{0,8},{8,0},{1,9},{9,1},{2,10},{10,2},{3,11},{11,3},{4,12},{12,4},... | collective-permute-start | bytes 2752520 | tf_op jit(solution)/shard_map/ppermute | solution.py:30
  22.3 34.8 %all-to-all-start = ((bf16[4,80,3584]{2,1,0:T(8,128)(2,1)}), bf16[4,80,3584]{2,1,0:T(8,128)(2,1)S(1)}, u32[]{:S(2)}, u32[]{:S(2)}) async-start(bf16[4,80,3584]{2,1,0:T(8,128)(2,1)} %bitcast.5), calls=%async_computation | async-start | bytes 4587520 | tf_op jit(solution)/shard_map/all_to_all | solution.py:324
  57.1 42.2 %all-to-all-start.1 = ((bf16[4,80,3584]{2,1,0:T(8,128)(2,1)}), bf16[4,80,3584]{2,1,0:T(8,128)(2,1)}, u32[]{:S(2)}, u32[]{:S(2)}) async-start(bf16[4,80,3584]{2,1,0:T(8,128)(2,1)} %bitcast.7), calls=%async_computation.1 | async-start | bytes 4587520 | tf_op jit(solution)/shard_map/all_to_all | solution.py:324
  62.3 130.1 %all-gather.3.cloned.1.call-start = ((), (), s32[]{:S(2)}) async-start(), calls=%async_computation.5 | async-start | bytes 9175040 | tf_op jit(solution)/shard_map/all_gather | solution.py:357
  63.7 34.2 %collective-permute-start.9 = (bf16[128,3584]{1,0:T(8,128)(2,1)S(1)}, bf16[128,3584]{1,0:T(8,128)(2,1)S(1)}, u32[]{:S(2)}, u32[]{:S(2)}) collective-permute-start(bf16[128,3584]{1,0:T(8,128)(2,1)S(1)} %broadcast_select_fusion), channel_id=1, source_target_pairs={{0,128},{128,0},{1,129},{129,1},{2,130},{130,2},{3,131},{131,3},{4... | collective-permute-start | bytes 2752520 | tf_op jit(solution)/shard_map/ppermute | solution.py:30
  67.6 31.8 %collective-permute-start.2 = (bf16[80,3584]{1,0:T(8,128)(2,1)S(1)}, bf16[80,3584]{1,0:T(8,128)(2,1)S(1)}, u32[]{:S(2)}, u32[]{:S(2)}) collective-permute-start(bf16[80,3584]{1,0:T(8,128)(2,1)S(1)} %get-tuple-element.63), channel_id=1, source_target_pairs={{0,136},{4,140},{8,128},{12,132},{128,8},{132,12},{136,0},{140,4},... | collective-permute-start | bytes 1720328 | tf_op jit(solution)/shard_map/ppermute | solution.py:340
  99.3 207.2 %reduce-scatter.2.cloned.1.call-start = ((), (), s32[]{:S(2)}) async-start(), calls=%async_computation.4 | async-start | bytes 9175040 | tf_op jit(solution)/shard_map/reduce_scatter | solution.py:386
  102.8 19.1 %collective-permute-start.4 = (bf16[80,3584]{1,0:T(8,128)(2,1)S(1)}, bf16[80,3584]{1,0:T(8,128)(2,1)S(1)}, u32[]{:S(2)}, u32[]{:S(2)}) collective-permute-start(bf16[80,3584]{1,0:T(8,128)(2,1)S(1)} %get-tuple-element.61), channel_id=1, source_target_pairs={{0,4},{4,8},{8,12},{12,0},{128,140},{132,128},{136,132},{140,136},... | collective-permute-start | bytes 1720328 | tf_op jit(solution)/shard_map/ppermute | solution.py:340
  105.4 41.2 %collective-permute-start.5 = (bf16[80,3584]{1,0:T(8,128)(2,1)S(1)}, bf16[80,3584]{1,0:T(8,128)(2,1)S(1)}, u32[]{:S(2)}, u32[]{:S(2)}) collective-permute-start(bf16[80,3584]{1,0:T(8,128)(2,1)S(1)} %get-tuple-element.60), channel_id=1, source_target_pairs={{0,140},{4,128},{8,132},{12,136},{128,4},{132,8},{136,12},{140,0},... | collective-permute-start | bytes 1720328 | tf_op jit(solution)/shard_map/ppermute | solution.py:340
  109.0 58.4 %collective-permute-start.6 = (bf16[80,3584]{1,0:T(8,128)(2,1)S(1)}, bf16[80,3584]{1,0:T(8,128)(2,1)S(1)}, u32[]{:S(2)}, u32[]{:S(2)}) collective-permute-start(bf16[80,3584]{1,0:T(8,128)(2,1)S(1)} %get-tuple-element.59), channel_id=1, source_target_pairs={{0,136},{4,140},{8,128},{12,132},{128,8},{132,12},{136,0},{140,4},... | collective-permute-start | bytes 1720328 | tf_op jit(solution)/shard_map/ppermute | solution.py:340
  109.5 58.3 %collective-permute-start = (bf16[80,3584]{1,0:T(8,128)(2,1)}, bf16[80,3584]{1,0:T(8,128)(2,1)S(1)}, u32[]{:S(2)}, u32[]{:S(2)}) collective-permute-start(bf16[80,3584]{1,0:T(8,128)(2,1)} %get-tuple-element.65), channel_id=1, source_target_pairs={{0,4},{4,8},{8,12},{12,0},{128,140},{132,128},{136,132},{140,136},... | collective-permute-start | bytes 1720328 | tf_op jit(solution)/shard_map/ppermute | solution.py:340
  111.4 69.0 %collective-permute-start.1 = (bf16[80,3584]{1,0:T(8,128)(2,1)}, bf16[80,3584]{1,0:T(8,128)(2,1)S(1)}, u32[]{:S(2)}, u32[]{:S(2)}) collective-permute-start(bf16[80,3584]{1,0:T(8,128)(2,1)} %get-tuple-element.64), channel_id=1, source_target_pairs={{0,140},{4,128},{8,132},{12,136},{128,4},{132,8},{136,12},{140,0},... | collective-permute-start | bytes 1720328 | tf_op jit(solution)/shard_map/ppermute | solution.py:340
  167.5 12.9 %copy-start.20 = (bf16[80,3584]{1,0:T(8,128)(2,1)S(1)}, bf16[80,3584]{1,0:T(8,128)(2,1)}, u32[]{:S(2)}) copy-start(bf16[80,3584]{1,0:T(8,128)(2,1)} %get-tuple-element.62) | copy-start | bytes 1720324
  167.5 12.9 %copy-start.23 = (bf16[80,3584]{1,0:T(8,128)(2,1)S(1)}, bf16[80,3584]{1,0:T(8,128)(2,1)}, u32[]{:S(2)}) copy-start(bf16[80,3584]{1,0:T(8,128)(2,1)} %copy-done.22) | copy-start | bytes 1720324
  167.6 22.0 %collective-permute-start.7 = (bf16[320,3584]{1,0:T(8,128)(2,1)S(1)}, bf16[320,3584]{1,0:T(8,128)(2,1)S(1)}, u32[]{:S(2)}, u32[]{:S(2)}) collective-permute-start(bf16[320,3584]{1,0:T(8,128)(2,1)S(1)} %pad_maximum_fusion.1.mine_scaled_ref), channel_id=1, source_target_pairs={{0,16},{16,0},{1,17},{17,1},{2,18},{18,2},{3,19},{19,3},{4,20},{20... | collective-permute-start | bytes 6881288 | tf_op jit(solution)/shard_map/ppermute | solution.py:30
  180.6 10.4 %collective-permute-start.3 = (bf16[320,3584]{1,0:T(8,128)(2,1)S(1)}, bf16[320,3584]{1,0:T(8,128)(2,1)S(1)}, u32[]{:S(2)}, u32[]{:S(2)}) collective-permute-start(bf16[320,3584]{1,0:T(8,128)(2,1)S(1)} %pad_maximum_fusion.mine_ref), channel_id=1, source_target_pairs={{0,16},{16,0},{1,17},{17,1},{2,18},{18,2},{3,19},{19,3},{4,20},{20... | collective-permute-start | bytes 6881288 | tf_op jit(solution)/shard_map/ppermute | solution.py:30
  183.7 40.7 %collective-permute-start.14 = (bf16[64,3584]{1,0:T(8,128)(2,1)}, bf16[64,3584]{1,0:T(8,128)(2,1)}, u32[]{:S(2)}, u32[]{:S(2)}) collective-permute-start(bf16[64,3584]{1,0:T(8,128)(2,1)} %get-tuple-element.34), channel_id=1, source_target_pairs={{0,8},{8,0},{1,9},{9,1},{2,10},{10,2},{3,11},{11,3},{4,12},{12,4},... | collective-permute-start | bytes 1376264 | tf_op jit(solution)/shard_map/ppermute | solution.py:30
  187.5 42.4 %collective-permute-start.15 = (bf16[64,3584]{1,0:T(8,128)(2,1)}, bf16[64,3584]{1,0:T(8,128)(2,1)}, u32[]{:S(2)}, u32[]{:S(2)}) collective-permute-start(bf16[64,3584]{1,0:T(8,128)(2,1)} %get-tuple-element.35), channel_id=1, source_target_pairs={{0,8},{8,0},{1,9},{9,1},{2,10},{10,2},{3,11},{11,3},{4,12},{12,4},... | collective-permute-start | bytes 1376264 | tf_op jit(solution)/shard_map/ppermute | solution.py:30
  231.5 4.4 %collective-permute-start.10 = (bf16[320,3584]{1,0:T(8,128)(2,1)S(1)}, bf16[320,3584]{1,0:T(8,128)(2,1)S(1)}, u32[]{:S(2)}, u32[]{:S(2)}) collective-permute-start(bf16[320,3584]{1,0:T(8,128)(2,1)S(1)} %copy-done.11), channel_id=1, source_target_pairs={{0,16},{16,0},{1,17},{17,1},{2,18},{18,2},{3,19},{19,3},{4,20},{20... | collective-permute-start | bytes 6881288 | tf_op jit(solution)/shard_map/ppermute | solution.py:30
  239.1 16.8 %collective-permute-start.11 = (bf16[80,3584]{1,0:T(8,128)(2,1)S(1)}, bf16[80,3584]{1,0:T(8,128)(2,1)S(1)}, u32[]{:S(2)}, u32[]{:S(2)}) collective-permute-start(bf16[80,3584]{1,0:T(8,128)(2,1)S(1)} %get-tuple-element.57), channel_id=1, source_target_pairs={{4,0},{8,4},{12,8},{0,12},{140,128},{128,132},{132,136},{136,140},... | collective-permute-start | bytes 1720328 | tf_op jit(solution)/shard_map/ppermute | solution.py:340
  239.2 27.4 %collective-permute-start.12 = (bf16[80,3584]{1,0:T(8,128)(2,1)S(1)}, bf16[80,3584]{1,0:T(8,128)(2,1)S(1)}, u32[]{:S(2)}, u32[]{:S(2)}) collective-permute-start(bf16[80,3584]{1,0:T(8,128)(2,1)S(1)} %get-tuple-element.56), channel_id=1, source_target_pairs={{140,0},{128,4},{132,8},{136,12},{4,128},{8,132},{12,136},{0,140},... | collective-permute-start | bytes 1720328 | tf_op jit(solution)/shard_map/ppermute | solution.py:340
  240.6 52.1 %collective-permute-start.13 = (bf16[80,3584]{1,0:T(8,128)(2,1)S(1)}, bf16[80,3584]{1,0:T(8,128)(2,1)S(1)}, u32[]{:S(2)}, u32[]{:S(2)}) collective-permute-start(bf16[80,3584]{1,0:T(8,128)(2,1)S(1)} %get-tuple-element.55), channel_id=1, source_target_pairs={{136,0},{140,4},{128,8},{132,12},{8,128},{12,132},{0,136},{4,140},... | collective-permute-start | bytes 1720328 | tf_op jit(solution)/shard_map/ppermute | solution.py:340
  295.8 48.7 %all-to-all-start.2 = ((bf16[4,80,3584]{2,1,0:T(8,128)(2,1)}), bf16[4,80,3584]{2,1,0:T(8,128)(2,1)S(1)}, u32[]{:S(2)}, u32[]{:S(2)}) async-start(bf16[4,80,3584]{2,1,0:T(8,128)(2,1)} %bitcast.88), calls=%async_computation.2 | async-start | bytes 4587520 | tf_op jit(solution)/shard_map/all_to_all | solution.py:324
  300.6 34.2 %collective-permute-start.16 = (bf16[64,3584]{1,0:T(8,128)(2,1)}, bf16[64,3584]{1,0:T(8,128)(2,1)}, u32[]{:S(2)}, u32[]{:S(2)}) collective-permute-start(bf16[64,3584]{1,0:T(8,128)(2,1)} %get-tuple-element.39), channel_id=1, source_target_pairs={{0,8},{8,0},{1,9},{9,1},{2,10},{10,2},{3,11},{11,3},{4,12},{12,4},... | collective-permute-start | bytes 1376264 | tf_op jit(solution)/shard_map/ppermute | solution.py:30
  303.7 40.8 %collective-permute-start.17 = (bf16[64,3584]{1,0:T(8,128)(2,1)}, bf16[64,3584]{1,0:T(8,128)(2,1)}, u32[]{:S(2)}, u32[]{:S(2)}) collective-permute-start(bf16[64,3584]{1,0:T(8,128)(2,1)} %get-tuple-element.40), channel_id=1, source_target_pairs={{0,8},{8,0},{1,9},{9,1},{2,10},{10,2},{3,11},{11,3},{4,12},{12,4},... | collective-permute-start | bytes 1376264 | tf_op jit(solution)/shard_map/ppermute | solution.py:30
  344.5 22.6 %collective-permute-start.18 = (bf16[128,3584]{1,0:T(8,128)(2,1)}, bf16[128,3584]{1,0:T(8,128)(2,1)}, u32[]{:S(2)}, u32[]{:S(2)}) collective-permute-start(bf16[128,3584]{1,0:T(8,128)(2,1)} %slice_bitcast_fusion), channel_id=1, source_target_pairs={{0,128},{128,0},{1,129},{129,1},{2,130},{130,2},{3,131},{131,3},{4... | collective-permute-start | bytes 2752520 | tf_op jit(solution)/shard_map/ppermute | solution.py:30
  344.5 22.6 %copy-start.21 = (bf16[1,2,128,3584]{3,2,1,0:T(8,128)(2,1)S(1)}, bf16[1,2,128,3584]{3,2,1,0:T(8,128)(2,1)}, u32[]{:S(2)}) copy-start(bf16[1,2,128,3584]{3,2,1,0:T(8,128)(2,1)} %reduce-scatter.2.cloned.1.call-done) | copy-start | bytes 5505028
  346.1 22.4 %copy-start.13 = (f32[1,64,3584]{2,1,0:T(8,128)S(1)}, f32[1,64,3584]{2,1,0:T(8,128)}, u32[]{:S(2)}) copy-start(f32[1,64,3584]{2,1,0:T(8,128)} %param.19) | copy-start | bytes 2752516
  346.1 22.4 %copy-start.15 = (f32[1,64,3584]{2,1,0:T(8,128)S(1)}, f32[1,64,3584]{2,1,0:T(8,128)}, u32[]{:S(2)}) copy-start(f32[1,64,3584]{2,1,0:T(8,128)} %param.18) | copy-start | bytes 2752516
  346.1 22.4 %copy-start.17 = (f32[1,64,3584]{2,1,0:T(8,128)S(1)}, f32[1,64,3584]{2,1,0:T(8,128)}, u32[]{:S(2)}) copy-start(f32[1,64,3584]{2,1,0:T(8,128)} %param.20) | copy-start | bytes 2752516
  346.1 22.4 %copy-start.19 = (f32[1,64,3584]{2,1,0:T(8,128)S(1)}, f32[1,64,3584]{2,1,0:T(8,128)}, u32[]{:S(2)}) copy-start(f32[1,64,3584]{2,1,0:T(8,128)} %param.21) | copy-start | bytes 2752516
  (17 other events, 61.6 us)
Sparse Core Ops, SparseCore 0:
  99.5 78.1 all-gather.2
  230.0 73.8 reduce-scatter.1

commit v4 on v3

--- a/solution.py
+++ b/solution.py
@@ -222,7 +222,7 @@
             pltpu.VMEM((2 * rows, hidden), jnp.bfloat16),
         ],
         compiler_params=pltpu.CompilerParams(
-            dimension_semantics=("arbitrary",), vmem_limit_bytes=40 * 1024 * 1024
+            dimension_semantics=("arbitrary",), vmem_limit_bytes=60 * 1024 * 1024
         ),
         cost_estimate=pl.CostEstimate(
             flops=12 * rows * hidden * width, bytes_accessed=32 * rows * width, transcendentals=0
@@ -265,7 +265,7 @@
         out_specs=pl.BlockSpec((chips, both, block), lambda i: (0, 0, i)),
         out_shape=jax.ShapeDtypeStruct((chips, both, width), jnp.bfloat16),
         compiler_params=pltpu.CompilerParams(
-            dimension_semantics=("arbitrary",), vmem_limit_bytes=40 * 1024 * 1024
+            dimension_semantics=("arbitrary",), vmem_limit_bytes=60 * 1024 * 1024
         ),
         cost_estimate=pl.CostEstimate(flops=0, bytes_accessed=1024, transcendentals=0),
     )(left, mine, other, mine_scaled, other_scaled)
@@ -375,10 +375,14 @@
     from_other = partner(for_other, CORE, 1)
     pair_grad = (pair_mine + from_other.astype(jnp.float32)).astype(jnp.bfloat16)
     up_arrived, parts = lax.optimization_barrier((up_arrived, parts))
+    down_held, _ = lax.optimization_barrier((rounded[2], parts))
+    down_arrived = partner(down_held, FAR, 1)
+    down_arrived, pair_grad = lax.optimization_barrier((down_arrived, pair_grad))
     back_rows, _ = along_high(pair_grad, True)
-    down_held, back_rows = lax.optimization_barrier((rounded[2:], back_rows))
-    down_arrived = tuple(partner(array, FAR, 1) for array in down_held)
+    late_held, back_rows = lax.optimization_barrier((rounded[3], back_rows))
+    late_arrived = partner(late_held, FAR, 1)
     returned = along_side(pick(regroup, back_rows))
+    late_arrived, returned = lax.optimization_barrier((late_arrived, returned))
     token_grad = lax.dot_general(
         token_select, returned, (((0,), (0,)), ((), ())), preferred_element_type=jnp.float32
     ).astype(jnp.bfloat16)
@@ -389,8 +393,7 @@
         scatter_dimension=0,
         tiled=False,
     )
-    down_arrived, beside = lax.optimization_barrier((down_arrived, beside))
-    arrived = (*up_arrived, *down_arrived)
+    arrived = (*up_arrived, down_arrived, late_arrived)
     summed = own.astype(jnp.float32) + partner(beside, NEAR, 1).astype(jnp.float32)
     moments = tuple(
         jnp.where(swapped, new.astype(jnp.float32), old) for new, old in zip(arrived, moments)

time: 381 us -> 374 us (0.982)
  waiting for transfers between devices: 233 us -> 212 us
  starting transfers between devices: 58.6 us -> 72.1 us
  local copies, waits for them, and re-layouts: 17.2 us -> 10.1 us
  Pallas kernels: 30.6 us -> 36.1 us
    ppermute x10, waiting for transfers between devices: 120 us -> 104 us  [partner(): lax.ppermute(array, axis, [(i, i ^ flip) for i in range(lax.axis_size(axi...]
    ppermute x9, starting transfers between devices: 21.6 us -> 32 us  [along_high(): lax.ppermute(array, (NEAR, *HIGH), [(b, a) for a, b in way] if back else...]
    unnamed x50 -> x30, local copies, waits for them, and re-layouts: 12.7 us -> 5.96 us
    ppermute x9, waiting for transfers between devices: 113 us -> 108 us  [along_high(): lax.ppermute(array, (NEAR, *HIGH), [(b, a) for a, b in way] if back else...]
  transfers between devices with their start and end apart: 24 -> 24, of which waited for: 14 -> 12; matrix products, arithmetic and copies ran while one was open for 6% -> 6% of each run, Pallas kernels for 8% -> 10%
where the time goes in v4:
time: 374 us; the launch traced here: 373 us
  waiting for transfers between devices  212 us (57%)
  starting transfers between devices  72.1 us (19%)
  Pallas kernels  36.1 us (10%)
  other arithmetic  16.8 us (4%)
  between operations  14.9 us (4%)
  matrix products  10.6 us (3%)
  local copies, waits for them, and re-layouts  10.1 us (3%)
    ppermute x9, waiting for transfers between devices, along_high(): lax.ppermute(array, (NEAR, *HIGH), [(b, a) for a, b in way] if back else...  108 us
    ppermute x10, waiting for transfers between devices, partner(): lax.ppermute(array, axis, [(i, i ^ flip) for i in range(lax.axis_size(axi...  104 us
    ppermute x9, starting transfers between devices, along_high(): lax.ppermute(array, (NEAR, *HIGH), [(b, a) for a, b in way] if back else...  32 us
    ppermute x10, starting transfers between devices, partner(): lax.ppermute(array, axis, [(i, i ^ flip) for i in range(lax.axis_size(axi...  24.7 us
    pallas_call x1, Pallas kernels, expert_stage(): pl.pallas_call(functools.partial(expert_kernel, steps, inv_model, inv_hid...  20.6 us
    all_to_all x3, starting transfers between devices, along_side(): lax.all_to_all(rows.reshape(side, side_rows, model_width), SIDE, split_ax...  15.4 us
    pallas_call x1, Pallas kernels, weight_stage(): pl.pallas_call(functools.partial(weight_kernel, inv_model, inv_hidden), g...  11.9 us
  transfers between devices with their start and end apart: 24, of which 12 were waited for; matrix products, arithmetic and copies ran while one was open for 6% of the time, Pallas kernels for 10%

profile of v4, /device:TPU:8, one launch (start us, length us, event | category | flops | bytes accessed | tf_op | source)
XLA Modules:
  0.0 372.7 jit_solution(2306654535974643901)
XLA Ops:
  9.5 7.2 %collective-permute-start.10 = (bf16[128,3584]{1,0:T(8,128)(2,1)}, bf16[128,3584]{1,0:T(8,128)(2,1)}, u32[]{:S(2)}, u32[]{:S(2)}) collective-permute-start(bf16[128,3584]{1,0:T(8,128)(2,1)} %pad_maximum_fusion.4), channel_id=1, source_target_pairs={{0,8},{8,0},{1,9},{9,1},{2,10},{10,2},{3,11},{11,3},{4,12},{12,4},... | collective-permute-start | bytes 2752520 | tf_op jit(solution)/shard_map/ppermute | solution.py:30
  18.7 3.6 shard_map.162
  22.3 5.0 %all-to-all-start.1 = ((bf16[4,80,3584]{2,1,0:T(8,128)(2,1)}), bf16[4,80,3584]{2,1,0:T(8,128)(2,1)S(1)}, u32[]{:S(2)}, u32[]{:S(2)}) async-start(bf16[4,80,3584]{2,1,0:T(8,128)(2,1)} %bitcast.9), calls=%async_computation.1 | async-start | bytes 4587520 | tf_op jit(solution)/shard_map/all_to_all | solution.py:324
  28.7 27.0 %collective-permute-done.10 = bf16[128,3584]{1,0:T(8,128)(2,1)} collective-permute-done((bf16[128,3584]{1,0:T(8,128)(2,1)}, bf16[128,3584]{1,0:T(8,128)(2,1)}, u32[]{:S(2)}, u32[]{:S(2)}) %collective-permute-start.10) | collective-permute-done | bytes 917536 | tf_op jit(solution)/shard_map/ppermute | solution.py:30
  57.1 5.2 %all-to-all-start = ((bf16[4,80,3584]{2,1,0:T(8,128)(2,1)}), bf16[4,80,3584]{2,1,0:T(8,128)(2,1)}, u32[]{:S(2)}, u32[]{:S(2)}) async-start(bf16[4,80,3584]{2,1,0:T(8,128)(2,1)} %bitcast.7), calls=%async_computation | async-start | bytes 4587520 | tf_op jit(solution)/shard_map/all_to_all | solution.py:324
  63.7 2.6 collective-permute-start.11
  67.3 4.5 %collective-permute-start.7 = (bf16[80,3584]{1,0:T(8,128)(2,1)}, bf16[80,3584]{1,0:T(8,128)(2,1)S(1)}, u32[]{:S(2)}, u32[]{:S(2)}) collective-permute-start(bf16[80,3584]{1,0:T(8,128)(2,1)} %get-tuple-element.61), channel_id=1, source_target_pairs={{0,136},{4,140},{8,128},{12,132},{128,8},{132,12},{136,0},{140,4},... | collective-permute-start | bytes 1720328 | tf_op jit(solution)/shard_map/ppermute | solution.py:340
  71.8 26.1 %collective-permute-done.11 = bf16[128,3584]{1,0:T(8,128)(2,1)S(1)} collective-permute-done((bf16[128,3584]{1,0:T(8,128)(2,1)S(1)}, bf16[128,3584]{1,0:T(8,128)(2,1)S(1)}, u32[]{:S(2)}, u32[]{:S(2)}) %collective-permute-start.11) | collective-permute-done | bytes 917536 | tf_op jit(solution)/shard_map/ppermute | solution.py:30
  99.4 2.6 collective-permute-start.5
  102.0 3.6 collective-permute-start.6
  105.6 3.0 convolution_convert_fusion.2
  109.9 4.6 %collective-permute-start.2 = (bf16[80,3584]{1,0:T(8,128)(2,1)S(1)}, bf16[80,3584]{1,0:T(8,128)(2,1)S(1)}, u32[]{:S(2)}, u32[]{:S(2)}) collective-permute-start(bf16[80,3584]{1,0:T(8,128)(2,1)S(1)} %get-tuple-element.65), channel_id=1, source_target_pairs={{0,136},{4,140},{8,128},{12,132},{128,8},{132,12},{136,0},{140,4},... | collective-permute-start | bytes 1720328 | tf_op jit(solution)/shard_map/ppermute | solution.py:340
  114.5 3.9 %collective-permute-done.5 = bf16[80,3584]{1,0:T(8,128)(2,1)S(1)} collective-permute-done((bf16[80,3584]{1,0:T(8,128)(2,1)S(1)}, bf16[80,3584]{1,0:T(8,128)(2,1)S(1)}, u32[]{:S(2)}, u32[]{:S(2)}) %collective-permute-start.5) | collective-permute-done | bytes 573472 | tf_op jit(solution)/shard_map/ppermute | solution.py:340
  118.5 21.8 %collective-permute-done.6 = bf16[80,3584]{1,0:T(8,128)(2,1)S(1)} collective-permute-done((bf16[80,3584]{1,0:T(8,128)(2,1)S(1)}, bf16[80,3584]{1,0:T(8,128)(2,1)S(1)}, u32[]{:S(2)}, u32[]{:S(2)}) %collective-permute-start.6) | collective-permute-done | bytes 573472 | tf_op jit(solution)/shard_map/ppermute | solution.py:340
  140.5 14.9 %collective-permute-done.1 = bf16[80,3584]{1,0:T(8,128)(2,1)S(1)} collective-permute-done((bf16[80,3584]{1,0:T(8,128)(2,1)S(1)}, bf16[80,3584]{1,0:T(8,128)(2,1)S(1)}, u32[]{:S(2)}, u32[]{:S(2)}) %collective-permute-start.1) | collective-permute-done | bytes 573472 | tf_op jit(solution)/shard_map/ppermute | solution.py:340
  155.4 20.9 %collective-permute-done.2 = bf16[80,3584]{1,0:T(8,128)(2,1)S(1)} collective-permute-done((bf16[80,3584]{1,0:T(8,128)(2,1)S(1)}, bf16[80,3584]{1,0:T(8,128)(2,1)S(1)}, u32[]{:S(2)}, u32[]{:S(2)}) %collective-permute-start.2) | collective-permute-done | bytes 573472 | tf_op jit(solution)/shard_map/ppermute | solution.py:340
  181.1 4.4 %collective-permute-start.4 = (bf16[64,3584]{1,0:T(8,128)(2,1)}, bf16[64,3584]{1,0:T(8,128)(2,1)}, u32[]{:S(2)}, u32[]{:S(2)}) collective-permute-start(bf16[64,3584]{1,0:T(8,128)(2,1)} %get-tuple-element.30), channel_id=1, source_target_pairs={{0,8},{8,0},{1,9},{9,1},{2,10},{10,2},{3,11},{11,3},{4,12},{12,4},... | collective-permute-start | bytes 1376264 | tf_op jit(solution)/shard_map/ppermute | solution.py:30
  186.9 20.6 %shard_map.163 = (f32[320,3584]{1,0:T(8,128)}, bf16[320,3584]{1,0:T(8,128)(2,1)}, bf16[2,512,640]{2,1,0:T(8,128)(2,1)}) custom-call(bf16[320,3584]{1,0:T(8,128)(2,1)} %copy-done.4, bf16[320,3584]{1,0:T(8,128)(2,1)} %copy-done.12, bf16[320,3584]{1,0:T(8,128)(2,1)} %copy-done.5, bf16[320,3584]{1,0:T(8,128)(2,1)} %collective-permute-done.9.other_scaled_ref, ...), custom_call_target="tpu_custom_call" | custom-call | flops 7046430720 | bytes 36700160 | tf_op jit(solution)/shard_map/pallas_call | solution.py:205
  207.5 11.9 %shard_map.164 = bf16[8,128,3584]{2,1,0:T(8,128)(2,1)} custom-call(bf16[2,512,640]{2,1,0:T(8,128)(2,1)} %get-tuple-element.34.left_ref, bf16[320,3584]{1,0:T(8,128)(2,1)} %copy-done.4, bf16[320,3584]{1,0:T(8,128)(2,1)} %copy-done.12, bf16[320,3584]{1,0:T(8,128)(2,1)} %copy-done.5, bf16[320,3584]{1,0:T(8,128)(2,1)} %collective-permute-done.9.other_scaled_ref), custom_call_target="tpu_custom_call" | custom-call | bytes 1024 | tf_op jit(solution)/shard_map/pallas_call | solution.py:261
  224.2 2.9 add_convert_fusion
  227.2 9.5 %collective-permute-done.12 = bf16[64,3584]{1,0:T(8,128)(2,1)S(1)} collective-permute-done((bf16[64,3584]{1,0:T(8,128)(2,1)S(1)}, bf16[64,3584]{1,0:T(8,128)(2,1)S(1)}, u32[]{:S(2)}, u32[]{:S(2)}) %collective-permute-start.12) | collective-permute-done | bytes 458784 | tf_op jit(solution)/shard_map/ppermute | solution.py:30
  236.8 14.1 %collective-permute-start.14 = (bf16[80,3584]{1,0:T(8,128)(2,1)S(1)}, bf16[80,3584]{1,0:T(8,128)(2,1)S(1)}, u32[]{:S(2)}, u32[]{:S(2)}) collective-permute-start(bf16[80,3584]{1,0:T(8,128)(2,1)S(1)} %get-tuple-element.59), channel_id=1, source_target_pairs={{4,0},{8,4},{12,8},{0,12},{140,128},{128,132},{132,136},{136,140},... | collective-permute-start | bytes 1720328 | tf_op jit(solution)/shard_map/ppermute | solution.py:340
  253.3 11.0 %collective-permute-done.14 = bf16[80,3584]{1,0:T(8,128)(2,1)S(1)} collective-permute-done((bf16[80,3584]{1,0:T(8,128)(2,1)S(1)}, bf16[80,3584]{1,0:T(8,128)(2,1)S(1)}, u32[]{:S(2)}, u32[]{:S(2)}) %collective-permute-start.14) | collective-permute-done | bytes 573472 | tf_op jit(solution)/shard_map/ppermute | solution.py:340
  264.3 25.3 %collective-permute-done.15 = bf16[80,3584]{1,0:T(8,128)(2,1)S(1)} collective-permute-done((bf16[80,3584]{1,0:T(8,128)(2,1)S(1)}, bf16[80,3584]{1,0:T(8,128)(2,1)S(1)}, u32[]{:S(2)}, u32[]{:S(2)}) %collective-permute-start.15) | collective-permute-done | bytes 573472 | tf_op jit(solution)/shard_map/ppermute | solution.py:340
  289.6 10.6 %collective-permute-done.16 = bf16[80,3584]{1,0:T(8,128)(2,1)S(1)} collective-permute-done((bf16[80,3584]{1,0:T(8,128)(2,1)S(1)}, bf16[80,3584]{1,0:T(8,128)(2,1)S(1)}, u32[]{:S(2)}, u32[]{:S(2)}) %collective-permute-start.16) | collective-permute-done | bytes 573472 | tf_op jit(solution)/shard_map/ppermute | solution.py:340
  300.3 2.8 convolution_convert_fusion
  303.1 5.2 %all-to-all-start.2 = ((bf16[4,80,3584]{2,1,0:T(8,128)(2,1)}), bf16[4,80,3584]{2,1,0:T(8,128)(2,1)}, u32[]{:S(2)}, u32[]{:S(2)}) async-start(bf16[4,80,3584]{2,1,0:T(8,128)(2,1)} %bitcast.87), calls=%async_computation.2 | async-start | bytes 4587520 | tf_op jit(solution)/shard_map/all_to_all | solution.py:324
  310.5 2.7 collective-permute-start.18
  313.1 4.3 %collective-permute-start.17 = (bf16[64,3584]{1,0:T(8,128)(2,1)}, bf16[64,3584]{1,0:T(8,128)(2,1)}, u32[]{:S(2)}, u32[]{:S(2)}) collective-permute-start(bf16[64,3584]{1,0:T(8,128)(2,1)} %bitcast_convert_fusion.3), channel_id=1, source_target_pairs={{0,8},{8,0},{1,9},{9,1},{2,10},{10,2},{3,11},{11,3},{4,12},{12,4},... | collective-permute-start | bytes 1376264 | tf_op jit(solution)/shard_map/ppermute | solution.py:30
  317.4 39.1 %collective-permute-done.17 = bf16[64,3584]{1,0:T(8,128)(2,1)} collective-permute-done((bf16[64,3584]{1,0:T(8,128)(2,1)}, bf16[64,3584]{1,0:T(8,128)(2,1)}, u32[]{:S(2)}, u32[]{:S(2)}) %collective-permute-start.17) | collective-permute-done | bytes 458784 | tf_op jit(solution)/shard_map/ppermute | solution.py:30
  356.5 3.4 convolution_convert_fusion.3
  361.6 4.3 %fusion.30 = (f32[1,64,3584]{2,1,0:T(8,128)}, bf16[1,64,3584]{2,1,0:T(8,128)(2,1)}, f32[1,64,3584]{2,1,0:T(8,128)}, f32[1,64,3584]{2,1,0:T(8,128)}, bf16[1,64,3584]{2,1,0:T(8,128)(2,1)}, /*index=5*/f32[1,64,3584]{2,1,0:T(8,128)}) fusion(f32[128,3584]{1,0:T(8,128)S(1)} %convert_add_fusion, f32[1,64,3584]{2,1,0:T(8,128)S(1)} %copy-done.9, ...), kind=kLoop, calls=%fused_computation.68 | loop fusion | flops 8257536 | bytes 12845057 | tf_op jit(solution)/shard_map/broadcast_in_dim | solution.py:412
  (74 shorter events, 29.3 us)
Async XLA Ops:
  7.2 10.2 %copy-start = (bf16[128,3584]{1,0:T(8,128)(2,1)S(1)}, bf16[128,3584]{1,0:T(8,128)(2,1)}, u32[]{:S(2)}) copy-start(bf16[128,3584]{1,0:T(8,128)(2,1)} %tokens_ref.1) | copy-start | bytes 2752516
  7.2 10.2 %copy-start.1 = (bf16[128,3584]{1,0:T(8,128)(2,1)S(1)}, bf16[128,3584]{1,0:T(8,128)(2,1)}, u32[]{:S(2)}) copy-start(bf16[128,3584]{1,0:T(8,128)(2,1)} %out_grad_ref.1) | copy-start | bytes 2752516
  9.5 46.2 %collective-permute-start.10 = (bf16[128,3584]{1,0:T(8,128)(2,1)}, bf16[128,3584]{1,0:T(8,128)(2,1)}, u32[]{:S(2)}, u32[]{:S(2)}) collective-permute-start(bf16[128,3584]{1,0:T(8,128)(2,1)} %pad_maximum_fusion.4), channel_id=1, source_target_pairs={{0,8},{8,0},{1,9},{9,1},{2,10},{10,2},{3,11},{11,3},{4,12},{12,4},... | collective-permute-start | bytes 2752520 | tf_op jit(solution)/shard_map/ppermute | solution.py:30
  22.3 5.0 %copy-start.14 = (s32[16]{0:T(128)S(1)}, s32[16]{0:T(128)}, u32[]{:S(2)}) copy-start(s32[16]{0:T(128)} %param.15) | copy-start | bytes 196
  22.3 34.8 %all-to-all-start.1 = ((bf16[4,80,3584]{2,1,0:T(8,128)(2,1)}), bf16[4,80,3584]{2,1,0:T(8,128)(2,1)S(1)}, u32[]{:S(2)}, u32[]{:S(2)}) async-start(bf16[4,80,3584]{2,1,0:T(8,128)(2,1)} %bitcast.9), calls=%async_computation.1 | async-start | bytes 4587520 | tf_op jit(solution)/shard_map/all_to_all | solution.py:324
  57.1 42.2 %all-to-all-start = ((bf16[4,80,3584]{2,1,0:T(8,128)(2,1)}), bf16[4,80,3584]{2,1,0:T(8,128)(2,1)}, u32[]{:S(2)}, u32[]{:S(2)}) async-start(bf16[4,80,3584]{2,1,0:T(8,128)(2,1)} %bitcast.7), calls=%async_computation | async-start | bytes 4587520 | tf_op jit(solution)/shard_map/all_to_all | solution.py:324
  62.3 123.2 %all-gather.3.cloned.1.call-start = ((), (), s32[]{:S(2)}) async-start(), calls=%async_computation.5 | async-start | bytes 9175040 | tf_op jit(solution)/shard_map/all_gather | solution.py:357
  63.7 34.2 %collective-permute-start.11 = (bf16[128,3584]{1,0:T(8,128)(2,1)S(1)}, bf16[128,3584]{1,0:T(8,128)(2,1)S(1)}, u32[]{:S(2)}, u32[]{:S(2)}) collective-permute-start(bf16[128,3584]{1,0:T(8,128)(2,1)S(1)} %broadcast_select_fusion), channel_id=1, source_target_pairs={{0,128},{128,0},{1,129},{129,1},{2,130},{130,2},{3,131},{131,3},{4... | collective-permute-start | bytes 2752520 | tf_op jit(solution)/shard_map/ppermute | solution.py:30
  67.3 32.0 %collective-permute-start.7 = (bf16[80,3584]{1,0:T(8,128)(2,1)}, bf16[80,3584]{1,0:T(8,128)(2,1)S(1)}, u32[]{:S(2)}, u32[]{:S(2)}) collective-permute-start(bf16[80,3584]{1,0:T(8,128)(2,1)} %get-tuple-element.61), channel_id=1, source_target_pairs={{0,136},{4,140},{8,128},{12,132},{128,8},{132,12},{136,0},{140,4},... | collective-permute-start | bytes 1720328 | tf_op jit(solution)/shard_map/ppermute | solution.py:340
  99.3 209.0 %reduce-scatter.2.cloned.1.call-start = ((), (), s32[]{:S(2)}) async-start(), calls=%async_computation.4 | async-start | bytes 9175040 | tf_op jit(solution)/shard_map/reduce_scatter | solution.py:390
  99.4 19.1 %collective-permute-start.5 = (bf16[80,3584]{1,0:T(8,128)(2,1)S(1)}, bf16[80,3584]{1,0:T(8,128)(2,1)S(1)}, u32[]{:S(2)}, u32[]{:S(2)}) collective-permute-start(bf16[80,3584]{1,0:T(8,128)(2,1)S(1)} %get-tuple-element.63), channel_id=1, source_target_pairs={{0,4},{4,8},{8,12},{12,0},{128,140},{132,128},{136,132},{140,136},... | collective-permute-start | bytes 1720328 | tf_op jit(solution)/shard_map/ppermute | solution.py:340
  102.0 38.2 %collective-permute-start.6 = (bf16[80,3584]{1,0:T(8,128)(2,1)S(1)}, bf16[80,3584]{1,0:T(8,128)(2,1)S(1)}, u32[]{:S(2)}, u32[]{:S(2)}) collective-permute-start(bf16[80,3584]{1,0:T(8,128)(2,1)S(1)} %get-tuple-element.62), channel_id=1, source_target_pairs={{0,140},{4,128},{8,132},{12,136},{128,4},{132,8},{136,12},{140,0},... | collective-permute-start | bytes 1720328 | tf_op jit(solution)/shard_map/ppermute | solution.py:340
  108.9 31.7 %collective-permute-start = (bf16[80,3584]{1,0:T(8,128)(2,1)S(1)}, bf16[80,3584]{1,0:T(8,128)(2,1)S(1)}, u32[]{:S(2)}, u32[]{:S(2)}) collective-permute-start(bf16[80,3584]{1,0:T(8,128)(2,1)S(1)} %get-tuple-element.67), channel_id=1, source_target_pairs={{0,4},{4,8},{8,12},{12,0},{128,140},{132,128},{136,132},{140,136},... | collective-permute-start | bytes 1720328 | tf_op jit(solution)/shard_map/ppermute | solution.py:340
  109.6 45.8 %collective-permute-start.1 = (bf16[80,3584]{1,0:T(8,128)(2,1)S(1)}, bf16[80,3584]{1,0:T(8,128)(2,1)S(1)}, u32[]{:S(2)}, u32[]{:S(2)}) collective-permute-start(bf16[80,3584]{1,0:T(8,128)(2,1)S(1)} %get-tuple-element.66), channel_id=1, source_target_pairs={{0,140},{4,128},{8,132},{12,136},{128,4},{132,8},{136,12},{140,0},... | collective-permute-start | bytes 1720328 | tf_op jit(solution)/shard_map/ppermute | solution.py:340
  109.9 66.3 %collective-permute-start.2 = (bf16[80,3584]{1,0:T(8,128)(2,1)S(1)}, bf16[80,3584]{1,0:T(8,128)(2,1)S(1)}, u32[]{:S(2)}, u32[]{:S(2)}) collective-permute-start(bf16[80,3584]{1,0:T(8,128)(2,1)S(1)} %get-tuple-element.65), channel_id=1, source_target_pairs={{0,136},{4,140},{8,128},{12,132},{128,8},{132,12},{136,0},{140,4},... | collective-permute-start | bytes 1720328 | tf_op jit(solution)/shard_map/ppermute | solution.py:340
  140.4 36.0 %copy-start.4 = (bf16[320,3584]{1,0:T(8,128)(2,1)}, bf16[320,3584]{1,0:T(8,128)(2,1)S(1)}, u32[]{:S(2)}) copy-start(bf16[320,3584]{1,0:T(8,128)(2,1)S(1)} %pad_maximum_fusion.1.mine_ref) | copy-start | bytes 6881284
  140.4 45.1 %collective-permute-start.8 = (bf16[320,3584]{1,0:T(8,128)(2,1)S(1)}, bf16[320,3584]{1,0:T(8,128)(2,1)S(1)}, u32[]{:S(2)}, u32[]{:S(2)}) collective-permute-start(bf16[320,3584]{1,0:T(8,128)(2,1)S(1)} %pad_maximum_fusion.1.mine_ref), channel_id=1, source_target_pairs={{0,16},{16,0},{1,17},{17,1},{2,18},{18,2},{3,19},{19,3},{4,20},{20... | collective-permute-start | bytes 6881288 | tf_op jit(solution)/shard_map/ppermute | solution.py:30
  176.3 2.3 copy-start.10
  176.4 9.1 %copy-start.5 = (bf16[320,3584]{1,0:T(8,128)(2,1)}, bf16[320,3584]{1,0:T(8,128)(2,1)S(1)}, u32[]{:S(2)}) copy-start(bf16[320,3584]{1,0:T(8,128)(2,1)S(1)} %pad_maximum_fusion.mine_scaled_ref) | copy-start | bytes 6881284
  176.5 9.1 %collective-permute-start.9 = (bf16[320,3584]{1,0:T(8,128)(2,1)S(1)}, bf16[320,3584]{1,0:T(8,128)(2,1)}, u32[]{:S(2)}, u32[]{:S(2)}) collective-permute-start(bf16[320,3584]{1,0:T(8,128)(2,1)S(1)} %pad_maximum_fusion.mine_scaled_ref), channel_id=1, source_target_pairs={{0,16},{16,0},{1,17},{17,1},{2,18},{18,2},{3,19},{19,3},{4,20},{20... | collective-permute-start | bytes 6881288 | tf_op jit(solution)/shard_map/ppermute | solution.py:30
  179.6 39.9 %collective-permute-start.3 = (bf16[64,3584]{1,0:T(8,128)(2,1)}, bf16[64,3584]{1,0:T(8,128)(2,1)}, u32[]{:S(2)}, u32[]{:S(2)}) collective-permute-start(bf16[64,3584]{1,0:T(8,128)(2,1)} %get-tuple-element.29), channel_id=1, source_target_pairs={{0,8},{8,0},{1,9},{9,1},{2,10},{10,2},{3,11},{11,3},{4,12},{12,4},... | collective-permute-start | bytes 1376264 | tf_op jit(solution)/shard_map/ppermute | solution.py:30
  181.1 38.3 %collective-permute-start.4 = (bf16[64,3584]{1,0:T(8,128)(2,1)}, bf16[64,3584]{1,0:T(8,128)(2,1)}, u32[]{:S(2)}, u32[]{:S(2)}) collective-permute-start(bf16[64,3584]{1,0:T(8,128)(2,1)} %get-tuple-element.30), channel_id=1, source_target_pairs={{0,8},{8,0},{1,9},{9,1},{2,10},{10,2},{3,11},{11,3},{4,12},{12,4},... | collective-permute-start | bytes 1376264 | tf_op jit(solution)/shard_map/ppermute | solution.py:30
  219.5 4.7 %collective-permute-start.13 = (bf16[320,3584]{1,0:T(8,128)(2,1)}, bf16[320,3584]{1,0:T(8,128)(2,1)S(1)}, u32[]{:S(2)}, u32[]{:S(2)}) collective-permute-start(bf16[320,3584]{1,0:T(8,128)(2,1)} %get-tuple-element.38), channel_id=1, source_target_pairs={{0,16},{16,0},{1,17},{17,1},{2,18},{18,2},{3,19},{19,3},{4,20},{20... | collective-permute-start | bytes 6881288 | tf_op jit(solution)/shard_map/ppermute | solution.py:30
  220.7 16.0 %collective-permute-start.12 = (bf16[64,3584]{1,0:T(8,128)(2,1)S(1)}, bf16[64,3584]{1,0:T(8,128)(2,1)S(1)}, u32[]{:S(2)}, u32[]{:S(2)}) collective-permute-start(bf16[64,3584]{1,0:T(8,128)(2,1)S(1)} %bitcast_convert_fusion.2), channel_id=1, source_target_pairs={{0,8},{8,0},{1,9},{9,1},{2,10},{10,2},{3,11},{11,3},{4,12},{12,4},... | collective-permute-start | bytes 1376264 | tf_op jit(solution)/shard_map/ppermute | solution.py:30
  227.2 25.3 %copy-start.7 = (f32[1,64,3584]{2,1,0:T(8,128)S(1)}, f32[1,64,3584]{2,1,0:T(8,128)}, u32[]{:S(2)}) copy-start(f32[1,64,3584]{2,1,0:T(8,128)} %param.21) | copy-start | bytes 2752516
  236.8 27.4 %collective-permute-start.14 = (bf16[80,3584]{1,0:T(8,128)(2,1)S(1)}, bf16[80,3584]{1,0:T(8,128)(2,1)S(1)}, u32[]{:S(2)}, u32[]{:S(2)}) collective-permute-start(bf16[80,3584]{1,0:T(8,128)(2,1)S(1)} %get-tuple-element.59), channel_id=1, source_target_pairs={{4,0},{8,4},{12,8},{0,12},{140,128},{128,132},{132,136},{136,140},... | collective-permute-start | bytes 1720328 | tf_op jit(solution)/shard_map/ppermute | solution.py:340
  250.9 38.7 %collective-permute-start.15 = (bf16[80,3584]{1,0:T(8,128)(2,1)S(1)}, bf16[80,3584]{1,0:T(8,128)(2,1)S(1)}, u32[]{:S(2)}, u32[]{:S(2)}) collective-permute-start(bf16[80,3584]{1,0:T(8,128)(2,1)S(1)} %get-tuple-element.58), channel_id=1, source_target_pairs={{140,0},{128,4},{132,8},{136,12},{4,128},{8,132},{12,136},{0,140},... | collective-permute-start | bytes 1720328 | tf_op jit(solution)/shard_map/ppermute | solution.py:340
  251.2 49.0 %collective-permute-start.16 = (bf16[80,3584]{1,0:T(8,128)(2,1)S(1)}, bf16[80,3584]{1,0:T(8,128)(2,1)S(1)}, u32[]{:S(2)}, u32[]{:S(2)}) collective-permute-start(bf16[80,3584]{1,0:T(8,128)(2,1)S(1)} %get-tuple-element.57), channel_id=1, source_target_pairs={{136,0},{140,4},{128,8},{132,12},{8,128},{12,132},{0,136},{4,140},... | collective-permute-start | bytes 1720328 | tf_op jit(solution)/shard_map/ppermute | solution.py:340
  303.1 53.4 %all-to-all-start.2 = ((bf16[4,80,3584]{2,1,0:T(8,128)(2,1)}), bf16[4,80,3584]{2,1,0:T(8,128)(2,1)}, u32[]{:S(2)}, u32[]{:S(2)}) async-start(bf16[4,80,3584]{2,1,0:T(8,128)(2,1)} %bitcast.87), calls=%async_computation.2 | async-start | bytes 4587520 | tf_op jit(solution)/shard_map/all_to_all | solution.py:324
  310.5 49.4 %collective-permute-start.18 = (bf16[128,3584]{1,0:T(8,128)(2,1)}, bf16[128,3584]{1,0:T(8,128)(2,1)}, u32[]{:S(2)}, u32[]{:S(2)}) collective-permute-start(bf16[128,3584]{1,0:T(8,128)(2,1)} %slice_bitcast_fusion), channel_id=1, source_target_pairs={{0,128},{128,0},{1,129},{129,1},{2,130},{130,2},{3,131},{131,3},{4... | collective-permute-start | bytes 2752520 | tf_op jit(solution)/shard_map/ppermute | solution.py:30
  313.1 43.4 %collective-permute-start.17 = (bf16[64,3584]{1,0:T(8,128)(2,1)}, bf16[64,3584]{1,0:T(8,128)(2,1)}, u32[]{:S(2)}, u32[]{:S(2)}) collective-permute-start(bf16[64,3584]{1,0:T(8,128)(2,1)} %bitcast_convert_fusion.3), channel_id=1, source_target_pairs={{0,8},{8,0},{1,9},{9,1},{2,10},{10,2},{3,11},{11,3},{4,12},{12,4},... | collective-permute-start | bytes 1376264 | tf_op jit(solution)/shard_map/ppermute | solution.py:30
  356.5 3.4 copy-start.13
  (7 other events, 8.6 us)
Sparse Core Ops, SparseCore 0:
  99.5 78.1 all-gather.2
  219.6 79.3 reduce-scatter.1

commit v5 on v4

--- a/solution.py
+++ b/solution.py
@@ -138,36 +138,31 @@
     mine_scaled_ref,
     other_scaled_ref,
     weight_ref,
-    pair_ref,
-    pair_other_ref,
+    delta_ref,
+    delta_other_ref,
     left_ref,
     pre_ref,
     back_ref,
-    delta_ref,
 ):
     step = pl.program_id(0)
     chips, both, _ = weight_ref.shape
     local = both // 2
     rows = mine_ref.shape[0]
     contract_last = (((1,), (1,)), ((), ()))
-    up = jnp.concatenate([weight_ref[i, :local] for i in range(chips)], axis=0)
 
     @pl.when(step == 0)
     def _():
         pre_ref[...] = jnp.zeros_like(pre_ref)
         back_ref[...] = jnp.zeros_like(back_ref)
 
-    @pl.when(step < steps)
-    def _():
-        down = jnp.concatenate([weight_ref[i, local:] for i in range(chips)], axis=0)
-        token = jnp.concatenate((mine_ref[...], other_ref[...]), axis=0)
-        pre_ref[...] += lax.dot_general(
-            up, token, contract_last, preferred_element_type=jnp.float32
-        )
-        scaled = jnp.concatenate((mine_scaled_ref[...], other_scaled_ref[...]), axis=0)
-        back_ref[...] += lax.dot_general(
-            down, scaled, contract_last, preferred_element_type=jnp.float32
-        )
+    up = jnp.concatenate([weight_ref[i, :local] for i in range(chips)], axis=0)
+    token = jnp.concatenate((mine_ref[...], other_ref[...]), axis=0)
+    pre_ref[...] += lax.dot_general(up, token, contract_last, preferred_element_type=jnp.float32)
+    down = jnp.concatenate([weight_ref[i, local:] for i in range(chips)], axis=0)
+    scaled = jnp.concatenate((mine_scaled_ref[...], other_scaled_ref[...]), axis=0)
+    back_ref[...] += lax.dot_general(
+        down, scaled, contract_last, preferred_element_type=jnp.float32
+    )
 
     @pl.when(step == steps - 1)
     def _():
@@ -178,48 +173,36 @@
         ).astype(jnp.bfloat16)
         left_ref[0] = delta
         left_ref[1] = (pre_act * sigmoid_act).astype(jnp.bfloat16)
-        delta_ref[...] = delta.T
-
-    @pl.when(step >= steps)
-    def _():
-        pair = jnp.dot(delta_ref[...], up, preferred_element_type=jnp.float32) * inv_model
-        pair_ref[...] = pair[:rows]
-        pair_other_ref[...] = pair[rows:].astype(jnp.bfloat16)
+        turned = delta.T
+        delta_ref[...] = turned[:rows]
+        delta_other_ref[...] = turned[rows:]
 
 
 def expert_stage(mine, other, mine_scaled, other_scaled, weights, inv_model, inv_hidden):
     rows, width = mine.shape
     chips, both, _ = weights.shape
     hidden = chips * both // 2
-    block = 512
+    block = 896
     steps = width // block
-
-    def early(i):
-        return jnp.minimum(i, steps - 1)
-
-    def late(i):
-        return jnp.maximum(i - steps, 0)
-
-    row_spec = pl.BlockSpec((rows, block), lambda i: (0, early(i)))
-    late_spec = pl.BlockSpec((rows, block), lambda i: (0, late(i)))
+    row_spec = pl.BlockSpec((rows, block), lambda i: (0, i))
+    delta_spec = pl.BlockSpec((rows, hidden), lambda i: (0, 0))
     return pl.pallas_call(
         functools.partial(expert_kernel, steps, inv_model, inv_hidden),
-        grid=(2 * steps,),
-        in_specs=[row_spec] * 4 + [pl.BlockSpec((chips, both, block), lambda i: (0, 0, i % steps))],
+        grid=(steps,),
+        in_specs=[row_spec] * 4 + [pl.BlockSpec((chips, both, block), lambda i: (0, 0, i))],
         out_specs=[
-            late_spec,
-            late_spec,
+            delta_spec,
+            delta_spec,
             pl.BlockSpec((2, hidden, 2 * rows), lambda i: (0, 0, 0)),
         ],
         out_shape=[
-            jax.ShapeDtypeStruct((rows, width), jnp.float32),
-            jax.ShapeDtypeStruct((rows, width), jnp.bfloat16),
+            jax.ShapeDtypeStruct((rows, hidden), jnp.bfloat16),
+            jax.ShapeDtypeStruct((rows, hidden), jnp.bfloat16),
             jax.ShapeDtypeStruct((2, hidden, 2 * rows), jnp.bfloat16),
         ],
         scratch_shapes=[
             pltpu.VMEM((hidden, 2 * rows), jnp.float32),
             pltpu.VMEM((hidden, 2 * rows), jnp.float32),
-            pltpu.VMEM((2 * rows, hidden), jnp.bfloat16),
         ],
         compiler_params=pltpu.CompilerParams(
             dimension_semantics=("arbitrary",), vmem_limit_bytes=60 * 1024 * 1024
@@ -228,6 +211,43 @@
             flops=12 * rows * hidden * width, bytes_accessed=32 * rows * width, transcendentals=0
         ),
     )(mine, other, mine_scaled, other_scaled, weights)
+
+
+def pair_kernel(inv_model, delta_ref, delta_other_ref, weight_ref, pair_ref, pair_other_ref):
+    chips, both, _ = weight_ref.shape
+    local = both // 2
+    up = jnp.concatenate([weight_ref[i, :local] for i in range(chips)], axis=0)
+    rows = delta_ref.shape[0]
+    delta = jnp.concatenate((delta_ref[...], delta_other_ref[...]), axis=0)
+    pair = jnp.dot(delta, up, preferred_element_type=jnp.float32) * inv_model
+    pair_ref[...] = pair[:rows]
+    pair_other_ref[...] = pair[rows:].astype(jnp.bfloat16)
+
+
+def pair_stage(delta, delta_other, weights, inv_model):
+    rows, hidden = delta.shape
+    chips, both, width = weights.shape
+    block = 896
+    delta_spec = pl.BlockSpec((rows, hidden), lambda i: (0, 0))
+    pair_spec = pl.BlockSpec((rows, block), lambda i: (0, i))
+    return pl.pallas_call(
+        functools.partial(pair_kernel, inv_model),
+        grid=(width // block,),
+        in_specs=[
+            delta_spec,
+            delta_spec,
+            pl.BlockSpec((chips, both, block), lambda i: (0, 0, i)),
+        ],
+        out_specs=[pair_spec, pair_spec],
+        out_shape=[
+            jax.ShapeDtypeStruct((rows, width), jnp.float32),
+            jax.ShapeDtypeStruct((rows, width), jnp.bfloat16),
+        ],
+        compiler_params=pltpu.CompilerParams(
+            dimension_semantics=("arbitrary",), vmem_limit_bytes=60 * 1024 * 1024
+        ),
+        cost_estimate=pl.CostEstimate(flops=0, bytes_accessed=1024, transcendentals=0),
+    )(delta, delta_other, weights)
 
 
 def weight_kernel(
@@ -256,7 +276,7 @@
 def weight_stage(left, mine, other, mine_scaled, other_scaled, chips, inv_model, inv_hidden):
     rows, width = mine.shape
     both = 2 * left.shape[1] // chips
-    block = 512
+    block = 896
     row_spec = pl.BlockSpec((rows, block), lambda i: (0, i))
     return pl.pallas_call(
         functools.partial(weight_kernel, inv_model, inv_hidden),
@@ -342,18 +362,18 @@
             )
             for array, way in zip(blocks[1:], ways)
         ]
-        return jnp.concatenate(blocks[:1] + moved, axis=0), moved[-1]
+        return jnp.concatenate(blocks[:1] + moved, axis=0), moved
 
     token_rows = pick(regroup, along_side(send_tokens))
     side_scaled = along_side(send_scaled)
     scaled_rows = pick(regroup, side_scaled)
 
-    rows_mine, farthest = along_high(token_rows, False)
+    rows_mine, token_blocks = along_high(token_rows, False)
 
     weights = jnp.where(swapped, weights_partner, weights)
     weights, _ = lax.optimization_barrier((weights, token_rows))
     both = jnp.stack((weights, partner(weights, NEAR, 1)), axis=0)
-    both, _, _ = lax.optimization_barrier((both, side_scaled, farthest))
+    both, _, _ = lax.optimization_barrier((both, side_scaled, token_blocks))
     gathered = lax.all_gather(both, RING, axis=0).reshape(
         chips, 2 * local_hidden, model_width
     )
@@ -366,15 +386,16 @@
     rounded = tuple(array.astype(jnp.bfloat16) for array in moments)
     up_held, _ = lax.optimization_barrier((rounded[:2], scaled_mine))
     up_arrived = tuple(partner(array, FAR, 1) for array in up_held)
-    pair_mine, for_other, left = expert_stage(
+    delta_mine, delta_other, left = expert_stage(
         rows_mine, rows_other, scaled_mine, scaled_other, gathered, inv_model, inv_hidden
     )
     parts = weight_stage(
         left, rows_mine, rows_other, scaled_mine, scaled_other, chips, inv_model, inv_hidden
     )
+    up_arrived, delta_mine, parts = lax.optimization_barrier((up_arrived, delta_mine, parts))
+    pair_mine, for_other = pair_stage(delta_mine, delta_other, gathered, inv_model)
     from_other = partner(for_other, CORE, 1)
     pair_grad = (pair_mine + from_other.astype(jnp.float32)).astype(jnp.bfloat16)
-    up_arrived, parts = lax.optimization_barrier((up_arrived, parts))
     down_held, _ = lax.optimization_barrier((rounded[2], parts))
     down_arrived = partner(down_held, FAR, 1)
     down_arrived, pair_grad = lax.optimization_barrier((down_arrived, pair_grad))
@@ -382,7 +403,6 @@
     late_held, back_rows = lax.optimization_barrier((rounded[3], back_rows))
     late_arrived = partner(late_held, FAR, 1)
     returned = along_side(pick(regroup, back_rows))
-    late_arrived, returned = lax.optimization_barrier((late_arrived, returned))
     token_grad = lax.dot_general(
         token_select, returned, (((0,), (0,)), ((), ())), preferred_element_type=jnp.float32
     ).astype(jnp.bfloat16)
@@ -393,6 +413,7 @@
         scatter_dimension=0,
         tiled=False,
     )
+    late_arrived, beside = lax.optimization_barrier((late_arrived, beside))
     arrived = (*up_arrived, down_arrived, late_arrived)
     summed = own.astype(jnp.float32) + partner(beside, NEAR, 1).astype(jnp.float32)
     moments = tuple(

time: 374 us -> 382 us (1.021)
  waiting for transfers between devices: 212 us -> 234 us
  starting transfers between devices: 72.1 us -> 60.6 us
    all_gather x1, waiting for transfers between devices: 0.02 us -> 17.1 us  [on_device(): lax.all_gather(both, RING, axis=0)]
    ppermute x9, starting transfers between devices: 32 us -> 19.7 us  [along_high(): lax.ppermute(array, (NEAR, *HIGH), [(b, a) for a, b in way] if back else...]
    pallas_call x1, Pallas kernels: 20.6 us -> 12.1 us  [expert_stage(): pl.pallas_call(functools.partial(expert_kernel, steps, inv_model, inv_hid...]
    pallas_call x0 -> x1, Pallas kernels: none -> 8.09 us  [pair_stage(): pl.pallas_call(functools.partial(pair_kernel, inv_model), grid=(width //...]
    ppermute x9, waiting for transfers between devices: 108 us -> 116 us  [along_high(): lax.ppermute(array, (NEAR, *HIGH), [(b, a) for a, b in way] if back else...]
  transfers between devices with their start and end apart: 24 -> 24, of which waited for: 12 -> 15; matrix products, arithmetic and copies ran while one was open for 6% -> 6% of each run, Pallas kernels for 10% -> 9%
where the time goes in v5:
time: 382 us; the launch traced here: 381 us
  waiting for transfers between devices  234 us (61%)
  starting transfers between devices  60.6 us (16%)
  Pallas kernels  34.9 us (9%)
  between operations  14.9 us (4%)
  other arithmetic  13.5 us (4%)
  matrix products  12.3 us (3%)
  local copies, waits for them, and re-layouts  10.6 us (3%)
    ppermute x9, waiting for transfers between devices, along_high(): lax.ppermute(array, (NEAR, *HIGH), [(b, a) for a, b in way] if back else...  116 us
    ppermute x10, waiting for transfers between devices, partner(): lax.ppermute(array, axis, [(i, i ^ flip) for i in range(lax.axis_size(axi...  100 us
    ppermute x10, starting transfers between devices, partner(): lax.ppermute(array, axis, [(i, i ^ flip) for i in range(lax.axis_size(axi...  22.7 us
    ppermute x9, starting transfers between devices, along_high(): lax.ppermute(array, (NEAR, *HIGH), [(b, a) for a, b in way] if back else...  19.7 us
    all_to_all x3, starting transfers between devices, along_side(): lax.all_to_all(rows.reshape(side, side_rows, model_width), SIDE, split_ax...  18.1 us
    all_gather x1, waiting for transfers between devices, on_device(): lax.all_gather(both, RING, axis=0)  17.1 us
    pallas_call x1, Pallas kernels, expert_stage(): pl.pallas_call(functools.partial(expert_kernel, steps, inv_model, inv_hid...  12.1 us
    pallas_call x1, Pallas kernels, weight_stage(): pl.pallas_call(functools.partial(weight_kernel, inv_model, inv_hidden), g...  11.2 us
  transfers between devices with their start and end apart: 24, of which 15 were waited for; matrix products, arithmetic and copies ran while one was open for 6% of the time, Pallas kernels for 9%

profile of v5, /device:TPU:8, one launch (start us, length us, event | category | flops | bytes accessed | tf_op | source)
XLA Modules:
  0.0 381.3 jit_solution(11983373218758174727)
XLA Ops:
  8.5 7.3 %collective-permute-start.10 = (bf16[128,3584]{1,0:T(8,128)(2,1)S(1)}, bf16[128,3584]{1,0:T(8,128)(2,1)}, u32[]{:S(2)}, u32[]{:S(2)}) collective-permute-start(bf16[128,3584]{1,0:T(8,128)(2,1)S(1)} %pad_maximum_fusion.4), channel_id=1, source_target_pairs={{0,8},{8,0},{1,9},{9,1},{2,10},{10,2},{3,11},{11,3},{4,12},{12,4},... | collective-permute-start | bytes 2752520 | tf_op jit(solution)/shard_map/ppermute | solution.py:30
  17.9 3.5 shard_map.162
  21.4 5.0 %all-to-all-start.1 = ((bf16[4,80,3584]{2,1,0:T(8,128)(2,1)}), bf16[4,80,3584]{2,1,0:T(8,128)(2,1)}, u32[]{:S(2)}, u32[]{:S(2)}) async-start(bf16[4,80,3584]{2,1,0:T(8,128)(2,1)} %bitcast.9), calls=%async_computation.1 | async-start | bytes 4587520 | tf_op jit(solution)/shard_map/all_to_all | solution.py:344
  27.8 26.8 %collective-permute-done.10 = bf16[128,3584]{1,0:T(8,128)(2,1)} collective-permute-done((bf16[128,3584]{1,0:T(8,128)(2,1)S(1)}, bf16[128,3584]{1,0:T(8,128)(2,1)}, u32[]{:S(2)}, u32[]{:S(2)}) %collective-permute-start.10) | collective-permute-done | bytes 917536 | tf_op jit(solution)/shard_map/ppermute | solution.py:30
  54.8 6.1 %all-to-all-start = ((bf16[4,80,3584]{2,1,0:T(8,128)(2,1)}), bf16[4,80,3584]{2,1,0:T(8,128)(2,1)}, u32[]{:S(2)}, u32[]{:S(2)}) async-start(bf16[4,80,3584]{2,1,0:T(8,128)(2,1)} %bitcast.7), calls=%async_computation | async-start | bytes 4587520 | tf_op jit(solution)/shard_map/all_to_all | solution.py:344
  61.0 3.0 convolution_convert_fusion.1
  68.6 4.4 %collective-permute-start.6 = (bf16[80,3584]{1,0:T(8,128)(2,1)}, bf16[80,3584]{1,0:T(8,128)(2,1)S(1)}, u32[]{:S(2)}, u32[]{:S(2)}) collective-permute-start(bf16[80,3584]{1,0:T(8,128)(2,1)} %get-tuple-element.68), channel_id=1, source_target_pairs={{0,140},{4,128},{8,132},{12,136},{128,4},{132,8},{136,12},{140,0},... | collective-permute-start | bytes 1720328 | tf_op jit(solution)/shard_map/ppermute | solution.py:360
  73.5 16.5 %collective-permute-done.11 = bf16[128,3584]{1,0:T(8,128)(2,1)S(1)} collective-permute-done((bf16[128,3584]{1,0:T(8,128)(2,1)S(1)}, bf16[128,3584]{1,0:T(8,128)(2,1)S(1)}, u32[]{:S(2)}, u32[]{:S(2)}) %collective-permute-start.11) | collective-permute-done | bytes 917536 | tf_op jit(solution)/shard_map/ppermute | solution.py:30
  91.5 16.1 %collective-permute-done.5 = bf16[80,3584]{1,0:T(8,128)(2,1)S(1)} collective-permute-done((bf16[80,3584]{1,0:T(8,128)(2,1)}, bf16[80,3584]{1,0:T(8,128)(2,1)S(1)}, u32[]{:S(2)}, u32[]{:S(2)}) %collective-permute-start.5) | collective-permute-done | bytes 573472 | tf_op jit(solution)/shard_map/ppermute | solution.py:360
  107.6 14.1 %collective-permute-done.7 = bf16[80,3584]{1,0:T(8,128)(2,1)S(1)} collective-permute-done((bf16[80,3584]{1,0:T(8,128)(2,1)}, bf16[80,3584]{1,0:T(8,128)(2,1)S(1)}, u32[]{:S(2)}, u32[]{:S(2)}) %collective-permute-start.7) | collective-permute-done | bytes 573472 | tf_op jit(solution)/shard_map/ppermute | solution.py:360
  121.8 3.0 convolution_convert_fusion.2
  131.0 6.0 %collective-permute-done = bf16[80,3584]{1,0:T(8,128)(2,1)S(1)} collective-permute-done((bf16[80,3584]{1,0:T(8,128)(2,1)S(1)}, bf16[80,3584]{1,0:T(8,128)(2,1)S(1)}, u32[]{:S(2)}, u32[]{:S(2)}) %collective-permute-start) | collective-permute-done | bytes 573472 | tf_op jit(solution)/shard_map/ppermute | solution.py:360
  137.0 17.9 %collective-permute-done.1 = bf16[80,3584]{1,0:T(8,128)(2,1)S(1)} collective-permute-done((bf16[80,3584]{1,0:T(8,128)(2,1)S(1)}, bf16[80,3584]{1,0:T(8,128)(2,1)S(1)}, u32[]{:S(2)}, u32[]{:S(2)}) %collective-permute-start.1) | collective-permute-done | bytes 573472 | tf_op jit(solution)/shard_map/ppermute | solution.py:360
  154.9 18.0 %collective-permute-done.2 = bf16[80,3584]{1,0:T(8,128)(2,1)S(1)} collective-permute-done((bf16[80,3584]{1,0:T(8,128)(2,1)S(1)}, bf16[80,3584]{1,0:T(8,128)(2,1)S(1)}, u32[]{:S(2)}, u32[]{:S(2)}) %collective-permute-start.2) | collective-permute-done | bytes 573472 | tf_op jit(solution)/shard_map/ppermute | solution.py:360
  176.2 5.0 %collective-permute-start.4 = (bf16[64,3584]{1,0:T(8,128)(2,1)S(1)}, bf16[64,3584]{1,0:T(8,128)(2,1)S(1)}, u32[]{:S(2)}, u32[]{:S(2)}) collective-permute-start(bf16[64,3584]{1,0:T(8,128)(2,1)S(1)} %get-tuple-element.33), channel_id=1, source_target_pairs={{0,8},{8,0},{1,9},{9,1},{2,10},{10,2},{3,11},{11,3},{4,12},{12,4},... | collective-permute-start | bytes 1376264 | tf_op jit(solution)/shard_map/ppermute | solution.py:30
  182.7 17.1 %all-gather.3.cloned.1.call-done.weight_ref = bf16[8,128,3584]{2,1,0:T(8,128)(2,1)} async-done(((bf16[2,128,3584]{2,1,0:T(8,128)(2,1)}), bf16[8,128,3584]{2,1,0:T(8,128)(2,1)}) %all-gather.3.cloned.1.call-update) | async-done | bytes 7340048 | tf_op jit(solution)/shard_map/all_gather | solution.py:377
  199.7 12.1 %shard_map.163 = (bf16[320,512]{1,0:T(8,128)(2,1)}, bf16[320,512]{1,0:T(8,128)(2,1)}, bf16[2,512,640]{2,1,0:T(8,128)(2,1)}) custom-call(bf16[320,3584]{1,0:T(8,128)(2,1)} %copy-done.4, bf16[320,3584]{1,0:T(8,128)(2,1)} %copy-done.12, bf16[320,3584]{1,0:T(8,128)(2,1)} %copy-done.5, bf16[320,3584]{1,0:T(8,128)(2,1)} %collective-permute-done.9.other_scaled_ref, ...), custom_call_target="tpu_custom_call" | custom-call | flops 7046430720 | bytes 36700160 | tf_op jit(solution)/shard_map/pallas_call | solution.py:189
  211.8 11.2 %shard_map.164 = bf16[8,128,3584]{2,1,0:T(8,128)(2,1)} custom-call(bf16[2,512,640]{2,1,0:T(8,128)(2,1)} %get-tuple-element.38.left_ref, bf16[320,3584]{1,0:T(8,128)(2,1)} %copy-done.4, bf16[320,3584]{1,0:T(8,128)(2,1)} %copy-done.12, bf16[320,3584]{1,0:T(8,128)(2,1)} %copy-done.5, bf16[320,3584]{1,0:T(8,128)(2,1)} %collective-permute-done.9.other_scaled_ref), custom_call_target="tpu_custom_call" | custom-call | bytes 1024 | tf_op jit(solution)/shard_map/pallas_call | solution.py:281
  223.8 8.1 %shard_map.165 = (f32[320,3584]{1,0:T(8,128)}, bf16[320,3584]{1,0:T(8,128)(2,1)}) custom-call(bf16[320,512]{1,0:T(8,128)(2,1)} %get-tuple-element.41.delta_ref, bf16[320,512]{1,0:T(8,128)(2,1)} %get-tuple-element.42.delta_other_ref, bf16[8,128,3584]{2,1,0:T(8,128)(2,1)} %all-gather.3.cloned.1.call-done.weight_ref), custom_call_target="tpu_custom_call" | custom-call | bytes 1024 | tf_op jit(solution)/shard_map/pallas_call | solution.py:233
  232.0 5.8 %collective-permute-start.12 = (bf16[64,3584]{1,0:T(8,128)(2,1)S(1)}, bf16[64,3584]{1,0:T(8,128)(2,1)S(1)}, u32[]{:S(2)}, u32[]{:S(2)}) collective-permute-start(bf16[64,3584]{1,0:T(8,128)(2,1)S(1)} %bitcast_convert_fusion.2), channel_id=1, source_target_pairs={{0,8},{8,0},{1,9},{9,1},{2,10},{10,2},{3,11},{11,3},{4,12},{12,4},... | collective-permute-start | bytes 1376264 | tf_op jit(solution)/shard_map/ppermute | solution.py:30
  237.8 3.1 add_convert_fusion
  240.9 17.2 %collective-permute-done.12 = bf16[64,3584]{1,0:T(8,128)(2,1)S(1)} collective-permute-done((bf16[64,3584]{1,0:T(8,128)(2,1)S(1)}, bf16[64,3584]{1,0:T(8,128)(2,1)S(1)}, u32[]{:S(2)}, u32[]{:S(2)}) %collective-permute-start.12) | collective-permute-done | bytes 458784 | tf_op jit(solution)/shard_map/ppermute | solution.py:30
  258.9 4.5 %collective-permute-start.14 = (bf16[80,3584]{1,0:T(8,128)(2,1)S(1)}, bf16[80,3584]{1,0:T(8,128)(2,1)S(1)}, u32[]{:S(2)}, u32[]{:S(2)}) collective-permute-start(bf16[80,3584]{1,0:T(8,128)(2,1)S(1)} %get-tuple-element.65), channel_id=1, source_target_pairs={{4,0},{8,4},{12,8},{0,12},{140,128},{128,132},{132,136},{136,140},... | collective-permute-start | bytes 1720328 | tf_op jit(solution)/shard_map/ppermute | solution.py:360
  263.7 3.6 collective-permute-start.16
  268.2 8.7 %collective-permute-done.14 = bf16[80,3584]{1,0:T(8,128)(2,1)S(1)} collective-permute-done((bf16[80,3584]{1,0:T(8,128)(2,1)S(1)}, bf16[80,3584]{1,0:T(8,128)(2,1)S(1)}, u32[]{:S(2)}, u32[]{:S(2)}) %collective-permute-start.14) | collective-permute-done | bytes 573472 | tf_op jit(solution)/shard_map/ppermute | solution.py:360
  276.8 25.3 %collective-permute-done.15 = bf16[80,3584]{1,0:T(8,128)(2,1)S(1)} collective-permute-done((bf16[80,3584]{1,0:T(8,128)(2,1)S(1)}, bf16[80,3584]{1,0:T(8,128)(2,1)S(1)}, u32[]{:S(2)}, u32[]{:S(2)}) %collective-permute-start.15) | collective-permute-done | bytes 573472 | tf_op jit(solution)/shard_map/ppermute | solution.py:360
  302.2 10.2 %collective-permute-done.16 = bf16[80,3584]{1,0:T(8,128)(2,1)S(1)} collective-permute-done((bf16[80,3584]{1,0:T(8,128)(2,1)S(1)}, bf16[80,3584]{1,0:T(8,128)(2,1)S(1)}, u32[]{:S(2)}, u32[]{:S(2)}) %collective-permute-start.16) | collective-permute-done | bytes 573472 | tf_op jit(solution)/shard_map/ppermute | solution.py:360
  315.4 6.9 %all-to-all-start.2 = ((bf16[4,80,3584]{2,1,0:T(8,128)(2,1)}), bf16[4,80,3584]{2,1,0:T(8,128)(2,1)}, u32[]{:S(2)}, u32[]{:S(2)}) async-start(bf16[4,80,3584]{2,1,0:T(8,128)(2,1)} %bitcast.86), calls=%async_computation.2 | async-start | bytes 4587520 | tf_op jit(solution)/shard_map/all_to_all | solution.py:344
  325.0 22.9 %collective-permute-done.17 = bf16[64,3584]{1,0:T(8,128)(2,1)} collective-permute-done((bf16[64,3584]{1,0:T(8,128)(2,1)}, bf16[64,3584]{1,0:T(8,128)(2,1)}, u32[]{:S(2)}, u32[]{:S(2)}) %collective-permute-start.17) | collective-permute-done | bytes 458784 | tf_op jit(solution)/shard_map/ppermute | solution.py:30
  349.0 3.4 convolution_convert_fusion.3
  352.4 16.6 %collective-permute-done.18 = bf16[128,3584]{1,0:T(8,128)(2,1)} collective-permute-done((bf16[128,3584]{1,0:T(8,128)(2,1)}, bf16[128,3584]{1,0:T(8,128)(2,1)}, u32[]{:S(2)}, u32[]{:S(2)}) %collective-permute-start.18) | collective-permute-done | bytes 917536 | tf_op jit(solution)/shard_map/ppermute | solution.py:30
  370.4 4.0 %fusion.30 = (f32[1,64,3584]{2,1,0:T(8,128)}, bf16[1,64,3584]{2,1,0:T(8,128)(2,1)}, f32[1,64,3584]{2,1,0:T(8,128)}, f32[1,64,3584]{2,1,0:T(8,128)}, bf16[1,64,3584]{2,1,0:T(8,128)(2,1)}, /*index=5*/f32[1,64,3584]{2,1,0:T(8,128)}) fusion(f32[128,3584]{1,0:T(8,128)S(1)} %convert_add_fusion, f32[1,64,3584]{2,1,0:T(8,128)S(1)} %copy-done.9, ...), kind=kLoop, calls=%fused_computation.68 | loop fusion | flops 8257536 | bytes 12845057 | tf_op jit(solution)/shard_map/broadcast_in_dim | solution.py:433
  (87 shorter events, 32.6 us)
Async XLA Ops:
  8.5 46.0 %collective-permute-start.10 = (bf16[128,3584]{1,0:T(8,128)(2,1)S(1)}, bf16[128,3584]{1,0:T(8,128)(2,1)}, u32[]{:S(2)}, u32[]{:S(2)}) collective-permute-start(bf16[128,3584]{1,0:T(8,128)(2,1)S(1)} %pad_maximum_fusion.4), channel_id=1, source_target_pairs={{0,8},{8,0},{1,9},{9,1},{2,10},{10,2},{3,11},{11,3},{4,12},{12,4},... | collective-permute-start | bytes 2752520 | tf_op jit(solution)/shard_map/ppermute | solution.py:30
  21.4 33.1 %copy-start.14 = (bf16[1,64,3584]{2,1,0:T(8,128)(2,1)S(1)}, bf16[1,64,3584]{2,1,0:T(8,128)(2,1)}, u32[]{:S(2)}) copy-start(bf16[1,64,3584]{2,1,0:T(8,128)(2,1)} %param.17) | copy-start | bytes 1376260
  21.4 33.1 %copy-start.15 = (bf16[1,64,3584]{2,1,0:T(8,128)(2,1)S(1)}, bf16[1,64,3584]{2,1,0:T(8,128)(2,1)}, u32[]{:S(2)}) copy-start(bf16[1,64,3584]{2,1,0:T(8,128)(2,1)} %param.16) | copy-start | bytes 1376260
  21.4 33.4 %all-to-all-start.1 = ((bf16[4,80,3584]{2,1,0:T(8,128)(2,1)}), bf16[4,80,3584]{2,1,0:T(8,128)(2,1)}, u32[]{:S(2)}, u32[]{:S(2)}) async-start(bf16[4,80,3584]{2,1,0:T(8,128)(2,1)} %bitcast.9), calls=%async_computation.1 | async-start | bytes 4587520 | tf_op jit(solution)/shard_map/all_to_all | solution.py:344
  54.8 36.7 %all-to-all-start = ((bf16[4,80,3584]{2,1,0:T(8,128)(2,1)}), bf16[4,80,3584]{2,1,0:T(8,128)(2,1)}, u32[]{:S(2)}, u32[]{:S(2)}) async-start(bf16[4,80,3584]{2,1,0:T(8,128)(2,1)} %bitcast.7), calls=%async_computation | async-start | bytes 4587520 | tf_op jit(solution)/shard_map/all_to_all | solution.py:344
  61.0 138.8 %all-gather.3.cloned.1.call-start = ((), (), s32[]{:S(2)}) async-start(), calls=%async_computation.5 | async-start | bytes 9175040 | tf_op jit(solution)/shard_map/all_gather | solution.py:377
  64.0 26.1 %collective-permute-start.11 = (bf16[128,3584]{1,0:T(8,128)(2,1)S(1)}, bf16[128,3584]{1,0:T(8,128)(2,1)S(1)}, u32[]{:S(2)}, u32[]{:S(2)}) collective-permute-start(bf16[128,3584]{1,0:T(8,128)(2,1)S(1)} %broadcast_select_fusion), channel_id=1, source_target_pairs={{0,128},{128,0},{1,129},{129,1},{2,130},{130,2},{3,131},{131,3},{4... | collective-permute-start | bytes 2752520 | tf_op jit(solution)/shard_map/ppermute | solution.py:30
  68.0 39.6 %collective-permute-start.5 = (bf16[80,3584]{1,0:T(8,128)(2,1)}, bf16[80,3584]{1,0:T(8,128)(2,1)S(1)}, u32[]{:S(2)}, u32[]{:S(2)}) collective-permute-start(bf16[80,3584]{1,0:T(8,128)(2,1)} %get-tuple-element.69), channel_id=1, source_target_pairs={{0,4},{4,8},{8,12},{12,0},{128,140},{132,128},{136,132},{140,136},... | collective-permute-start | bytes 1720328 | tf_op jit(solution)/shard_map/ppermute | solution.py:360
  68.6 39.0 %collective-permute-start.6 = (bf16[80,3584]{1,0:T(8,128)(2,1)}, bf16[80,3584]{1,0:T(8,128)(2,1)S(1)}, u32[]{:S(2)}, u32[]{:S(2)}) collective-permute-start(bf16[80,3584]{1,0:T(8,128)(2,1)} %get-tuple-element.68), channel_id=1, source_target_pairs={{0,140},{4,128},{8,132},{12,136},{128,4},{132,8},{136,12},{140,0},... | collective-permute-start | bytes 1720328 | tf_op jit(solution)/shard_map/ppermute | solution.py:360
  73.0 48.7 %collective-permute-start.7 = (bf16[80,3584]{1,0:T(8,128)(2,1)}, bf16[80,3584]{1,0:T(8,128)(2,1)S(1)}, u32[]{:S(2)}, u32[]{:S(2)}) collective-permute-start(bf16[80,3584]{1,0:T(8,128)(2,1)} %get-tuple-element.67), channel_id=1, source_target_pairs={{0,136},{4,140},{8,128},{12,132},{128,8},{132,12},{136,0},{140,4},... | collective-permute-start | bytes 1720328 | tf_op jit(solution)/shard_map/ppermute | solution.py:360
  121.7 201.1 %reduce-scatter.2.cloned.1.call-start = ((), (), s32[]{:S(2)}) async-start(), calls=%async_computation.4 | async-start | bytes 9175040 | tf_op jit(solution)/shard_map/reduce_scatter | solution.py:410
  125.0 12.0 %collective-permute-start = (bf16[80,3584]{1,0:T(8,128)(2,1)S(1)}, bf16[80,3584]{1,0:T(8,128)(2,1)S(1)}, u32[]{:S(2)}, u32[]{:S(2)}) collective-permute-start(bf16[80,3584]{1,0:T(8,128)(2,1)S(1)} %get-tuple-element.73), channel_id=1, source_target_pairs={{0,4},{4,8},{8,12},{12,0},{128,140},{132,128},{136,132},{140,136},... | collective-permute-start | bytes 1720328 | tf_op jit(solution)/shard_map/ppermute | solution.py:360
  125.8 29.1 %collective-permute-start.1 = (bf16[80,3584]{1,0:T(8,128)(2,1)S(1)}, bf16[80,3584]{1,0:T(8,128)(2,1)S(1)}, u32[]{:S(2)}, u32[]{:S(2)}) collective-permute-start(bf16[80,3584]{1,0:T(8,128)(2,1)S(1)} %get-tuple-element.72), channel_id=1, source_target_pairs={{0,140},{4,128},{8,132},{12,136},{128,4},{132,8},{136,12},{140,0},... | collective-permute-start | bytes 1720328 | tf_op jit(solution)/shard_map/ppermute | solution.py:360
  128.8 44.1 %collective-permute-start.2 = (bf16[80,3584]{1,0:T(8,128)(2,1)S(1)}, bf16[80,3584]{1,0:T(8,128)(2,1)S(1)}, u32[]{:S(2)}, u32[]{:S(2)}) collective-permute-start(bf16[80,3584]{1,0:T(8,128)(2,1)S(1)} %get-tuple-element.71), channel_id=1, source_target_pairs={{0,136},{4,140},{8,128},{12,132},{128,8},{132,12},{136,0},{140,4},... | collective-permute-start | bytes 1720328 | tf_op jit(solution)/shard_map/ppermute | solution.py:360
  130.9 42.2 %copy-start.4 = (bf16[320,3584]{1,0:T(8,128)(2,1)}, bf16[320,3584]{1,0:T(8,128)(2,1)S(1)}, u32[]{:S(2)}) copy-start(bf16[320,3584]{1,0:T(8,128)(2,1)S(1)} %pad_maximum_fusion.1.mine_ref) | copy-start | bytes 6881284
  130.9 50.4 %collective-permute-start.8 = (bf16[320,3584]{1,0:T(8,128)(2,1)S(1)}, bf16[320,3584]{1,0:T(8,128)(2,1)S(1)}, u32[]{:S(2)}, u32[]{:S(2)}) collective-permute-start(bf16[320,3584]{1,0:T(8,128)(2,1)S(1)} %pad_maximum_fusion.1.mine_ref), channel_id=1, source_target_pairs={{0,16},{16,0},{1,17},{17,1},{2,18},{18,2},{3,19},{19,3},{4,20},{20... | collective-permute-start | bytes 6881288 | tf_op jit(solution)/shard_map/ppermute | solution.py:30
  173.0 9.6 %collective-permute-start.9 = (bf16[320,3584]{1,0:T(8,128)(2,1)S(1)}, bf16[320,3584]{1,0:T(8,128)(2,1)}, u32[]{:S(2)}, u32[]{:S(2)}) collective-permute-start(bf16[320,3584]{1,0:T(8,128)(2,1)S(1)} %pad_maximum_fusion.mine_scaled_ref), channel_id=1, source_target_pairs={{0,16},{16,0},{1,17},{17,1},{2,18},{18,2},{3,19},{19,3},{4,20},{20... | collective-permute-start | bytes 6881288 | tf_op jit(solution)/shard_map/ppermute | solution.py:30
  175.2 47.8 %collective-permute-start.3 = (bf16[64,3584]{1,0:T(8,128)(2,1)S(1)}, bf16[64,3584]{1,0:T(8,128)(2,1)S(1)}, u32[]{:S(2)}, u32[]{:S(2)}) collective-permute-start(bf16[64,3584]{1,0:T(8,128)(2,1)S(1)} %get-tuple-element.32), channel_id=1, source_target_pairs={{0,8},{8,0},{1,9},{9,1},{2,10},{10,2},{3,11},{11,3},{4,12},{12,4},... | collective-permute-start | bytes 1376264 | tf_op jit(solution)/shard_map/ppermute | solution.py:30
  176.2 46.8 %collective-permute-start.4 = (bf16[64,3584]{1,0:T(8,128)(2,1)S(1)}, bf16[64,3584]{1,0:T(8,128)(2,1)S(1)}, u32[]{:S(2)}, u32[]{:S(2)}) collective-permute-start(bf16[64,3584]{1,0:T(8,128)(2,1)S(1)} %get-tuple-element.33), channel_id=1, source_target_pairs={{0,8},{8,0},{1,9},{9,1},{2,10},{10,2},{3,11},{11,3},{4,12},{12,4},... | collective-permute-start | bytes 1376264 | tf_op jit(solution)/shard_map/ppermute | solution.py:30
  231.9 5.9 %collective-permute-start.13 = (bf16[320,3584]{1,0:T(8,128)(2,1)}, bf16[320,3584]{1,0:T(8,128)(2,1)S(1)}, u32[]{:S(2)}, u32[]{:S(2)}) collective-permute-start(bf16[320,3584]{1,0:T(8,128)(2,1)} %get-tuple-element.44), channel_id=1, source_target_pairs={{0,16},{16,0},{1,17},{17,1},{2,18},{18,2},{3,19},{19,3},{4,20},{20... | collective-permute-start | bytes 6881288 | tf_op jit(solution)/shard_map/ppermute | solution.py:30
  232.0 26.1 %collective-permute-start.12 = (bf16[64,3584]{1,0:T(8,128)(2,1)S(1)}, bf16[64,3584]{1,0:T(8,128)(2,1)S(1)}, u32[]{:S(2)}, u32[]{:S(2)}) collective-permute-start(bf16[64,3584]{1,0:T(8,128)(2,1)S(1)} %bitcast_convert_fusion.2), channel_id=1, source_target_pairs={{0,8},{8,0},{1,9},{9,1},{2,10},{10,2},{3,11},{11,3},{4,12},{12,4},... | collective-permute-start | bytes 1376264 | tf_op jit(solution)/shard_map/ppermute | solution.py:30
  240.9 26.5 %copy-start.7 = (f32[1,64,3584]{2,1,0:T(8,128)S(1)}, f32[1,64,3584]{2,1,0:T(8,128)}, u32[]{:S(2)}) copy-start(f32[1,64,3584]{2,1,0:T(8,128)} %param.21) | copy-start | bytes 2752516
  258.9 17.9 %collective-permute-start.14 = (bf16[80,3584]{1,0:T(8,128)(2,1)S(1)}, bf16[80,3584]{1,0:T(8,128)(2,1)S(1)}, u32[]{:S(2)}, u32[]{:S(2)}) collective-permute-start(bf16[80,3584]{1,0:T(8,128)(2,1)S(1)} %get-tuple-element.65), channel_id=1, source_target_pairs={{4,0},{8,4},{12,8},{0,12},{140,128},{128,132},{132,136},{136,140},... | collective-permute-start | bytes 1720328 | tf_op jit(solution)/shard_map/ppermute | solution.py:360
  263.4 38.7 %collective-permute-start.15 = (bf16[80,3584]{1,0:T(8,128)(2,1)S(1)}, bf16[80,3584]{1,0:T(8,128)(2,1)S(1)}, u32[]{:S(2)}, u32[]{:S(2)}) collective-permute-start(bf16[80,3584]{1,0:T(8,128)(2,1)S(1)} %get-tuple-element.64), channel_id=1, source_target_pairs={{140,0},{128,4},{132,8},{136,12},{4,128},{8,132},{12,136},{0,140},... | collective-permute-start | bytes 1720328 | tf_op jit(solution)/shard_map/ppermute | solution.py:360
  263.7 48.7 %collective-permute-start.16 = (bf16[80,3584]{1,0:T(8,128)(2,1)S(1)}, bf16[80,3584]{1,0:T(8,128)(2,1)S(1)}, u32[]{:S(2)}, u32[]{:S(2)}) collective-permute-start(bf16[80,3584]{1,0:T(8,128)(2,1)S(1)} %get-tuple-element.63), channel_id=1, source_target_pairs={{136,0},{140,4},{128,8},{132,12},{8,128},{12,132},{0,136},{4,140},... | collective-permute-start | bytes 1720328 | tf_op jit(solution)/shard_map/ppermute | solution.py:360
  315.4 33.6 %all-to-all-start.2 = ((bf16[4,80,3584]{2,1,0:T(8,128)(2,1)}), bf16[4,80,3584]{2,1,0:T(8,128)(2,1)}, u32[]{:S(2)}, u32[]{:S(2)}) async-start(bf16[4,80,3584]{2,1,0:T(8,128)(2,1)} %bitcast.86), calls=%async_computation.2 | async-start | bytes 4587520 | tf_op jit(solution)/shard_map/all_to_all | solution.py:344
  322.3 25.6 %collective-permute-start.17 = (bf16[64,3584]{1,0:T(8,128)(2,1)}, bf16[64,3584]{1,0:T(8,128)(2,1)}, u32[]{:S(2)}, u32[]{:S(2)}) collective-permute-start(bf16[64,3584]{1,0:T(8,128)(2,1)} %bitcast_convert_fusion.3), channel_id=1, source_target_pairs={{0,8},{8,0},{1,9},{9,1},{2,10},{10,2},{3,11},{11,3},{4,12},{12,4},... | collective-permute-start | bytes 1376264 | tf_op jit(solution)/shard_map/ppermute | solution.py:30
  347.9 21.0 %collective-permute-start.18 = (bf16[128,3584]{1,0:T(8,128)(2,1)}, bf16[128,3584]{1,0:T(8,128)(2,1)}, u32[]{:S(2)}, u32[]{:S(2)}) collective-permute-start(bf16[128,3584]{1,0:T(8,128)(2,1)} %slice_bitcast_fusion), channel_id=1, source_target_pairs={{0,128},{128,0},{1,129},{129,1},{2,130},{130,2},{3,131},{131,3},{4... | collective-permute-start | bytes 2752520 | tf_op jit(solution)/shard_map/ppermute | solution.py:30
  349.0 20.0 %copy-start.13 = (bf16[1,2,128,3584]{3,2,1,0:T(8,128)(2,1)S(1)}, bf16[1,2,128,3584]{3,2,1,0:T(8,128)(2,1)}, u32[]{:S(2)}) copy-start(bf16[1,2,128,3584]{3,2,1,0:T(8,128)(2,1)} %reduce-scatter.2.cloned.1.call-done) | copy-start | bytes 5505028
  352.4 18.0 %copy-start.11 = (f32[1,64,3584]{2,1,0:T(8,128)S(1)}, f32[1,64,3584]{2,1,0:T(8,128)}, u32[]{:S(2)}) copy-start(f32[1,64,3584]{2,1,0:T(8,128)} %param.18) | copy-start | bytes 2752516
  352.4 18.0 %copy-start.17 = (bf16[64,3584]{1,0:T(8,128)(2,1)S(1)}, bf16[64,3584]{1,0:T(8,128)(2,1)}, u32[]{:S(2)}) copy-start(bf16[64,3584]{1,0:T(8,128)(2,1)} %copy-done.16) | copy-start | bytes 1376260
  352.4 18.0 %copy-start.19 = (bf16[64,3584]{1,0:T(8,128)(2,1)S(1)}, bf16[64,3584]{1,0:T(8,128)(2,1)}, u32[]{:S(2)}) copy-start(bf16[64,3584]{1,0:T(8,128)(2,1)} %copy-done.18) | copy-start | bytes 1376260
  (13 other events, 66.1 us)
Sparse Core Ops, SparseCore 0:
  121.9 77.8 all-gather.2
  223.2 76.7 reduce-scatter.1

commit v6 on v4

--- a/solution.py
+++ b/solution.py
@@ -191,7 +191,7 @@
     rows, width = mine.shape
     chips, both, _ = weights.shape
     hidden = chips * both // 2
-    block = 512
+    block = 1792
     steps = width // block
 
     def early(i):
@@ -256,7 +256,7 @@
 def weight_stage(left, mine, other, mine_scaled, other_scaled, chips, inv_model, inv_hidden):
     rows, width = mine.shape
     both = 2 * left.shape[1] // chips
-    block = 512
+    block = 896
     row_spec = pl.BlockSpec((rows, block), lambda i: (0, i))
     return pl.pallas_call(
         functools.partial(weight_kernel, inv_model, inv_hidden),
@@ -342,18 +342,18 @@
             )
             for array, way in zip(blocks[1:], ways)
         ]
-        return jnp.concatenate(blocks[:1] + moved, axis=0), moved[-1]
+        return jnp.concatenate(blocks[:1] + moved, axis=0), moved[1]
 
     token_rows = pick(regroup, along_side(send_tokens))
     side_scaled = along_side(send_scaled)
     scaled_rows = pick(regroup, side_scaled)
 
-    rows_mine, farthest = along_high(token_rows, False)
+    rows_mine, nearest = along_high(token_rows, False)
 
     weights = jnp.where(swapped, weights_partner, weights)
     weights, _ = lax.optimization_barrier((weights, token_rows))
     both = jnp.stack((weights, partner(weights, NEAR, 1)), axis=0)
-    both, _, _ = lax.optimization_barrier((both, side_scaled, farthest))
+    both, _, _ = lax.optimization_barrier((both, side_scaled, nearest))
     gathered = lax.all_gather(both, RING, axis=0).reshape(
         chips, 2 * local_hidden, model_width
     )
@@ -382,7 +382,6 @@
     late_held, back_rows = lax.optimization_barrier((rounded[3], back_rows))
     late_arrived = partner(late_held, FAR, 1)
     returned = along_side(pick(regroup, back_rows))
-    late_arrived, returned = lax.optimization_barrier((late_arrived, returned))
     token_grad = lax.dot_general(
         token_select, returned, (((0,), (0,)), ((), ())), preferred_element_type=jnp.float32
     ).astype(jnp.bfloat16)
@@ -393,6 +392,7 @@
         scatter_dimension=0,
         tiled=False,
     )
+    late_arrived, beside = lax.optimization_barrier((late_arrived, beside))
     arrived = (*up_arrived, down_arrived, late_arrived)
     summed = own.astype(jnp.float32) + partner(beside, NEAR, 1).astype(jnp.float32)
     moments = tuple(

time: 374 us -> 374 us (level)
  waiting for transfers between devices: 212 us -> 230 us
  starting transfers between devices: 72.1 us -> 59.5 us
  Pallas kernels: 36.1 us -> 31.3 us
    ppermute x9, waiting for transfers between devices: 108 us -> 126 us  [along_high(): lax.ppermute(array, (NEAR, *HIGH), [(b, a) for a, b in way] if back else...]
    ppermute x9, starting transfers between devices: 32 us -> 24.3 us  [along_high(): lax.ppermute(array, (NEAR, *HIGH), [(b, a) for a, b in way] if back else...]
    ppermute x10, starting transfers between devices: 24.7 us -> 19 us  [partner(): lax.ppermute(array, axis, [(i, i ^ flip) for i in range(lax.axis_size(axi...]
    pallas_call x1, Pallas kernels: 20.6 us -> 16.6 us  [expert_stage(): pl.pallas_call(functools.partial(expert_kernel, steps, inv_model, inv_hid...]
  transfers between devices with their start and end apart: 24 -> 24, of which waited for: 12 -> 15; matrix products, arithmetic and copies ran while one was open for 6% -> 6% of each run, Pallas kernels for 10% -> 8%
where the time goes in v6:
time: 374 us; the launch traced here: 373 us
  waiting for transfers between devices  230 us (61%)
  starting transfers between devices  59.5 us (16%)
  Pallas kernels  31.3 us (8%)
  other arithmetic  16.6 us (4%)
  between operations  14.9 us (4%)
  matrix products  10.6 us (3%)
  local copies, waits for them, and re-layouts  10 us (3%)
    ppermute x9, waiting for transfers between devices, along_high(): lax.ppermute(array, (NEAR, *HIGH), [(b, a) for a, b in way] if back else...  126 us
    ppermute x10, waiting for transfers between devices, partner(): lax.ppermute(array, axis, [(i, i ^ flip) for i in range(lax.axis_size(axi...  99.9 us
    ppermute x9, starting transfers between devices, along_high(): lax.ppermute(array, (NEAR, *HIGH), [(b, a) for a, b in way] if back else...  24.3 us
    ppermute x10, starting transfers between devices, partner(): lax.ppermute(array, axis, [(i, i ^ flip) for i in range(lax.axis_size(axi...  19 us
    pallas_call x1, Pallas kernels, expert_stage(): pl.pallas_call(functools.partial(expert_kernel, steps, inv_model, inv_hid...  16.6 us
    all_to_all x3, starting transfers between devices, along_side(): lax.all_to_all(rows.reshape(side, side_rows, model_width), SIDE, split_ax...  16.2 us
    pallas_call x1, Pallas kernels, weight_stage(): pl.pallas_call(functools.partial(weight_kernel, inv_model, inv_hidden), g...  11.1 us
  transfers between devices with their start and end apart: 24, of which 15 were waited for; matrix products, arithmetic and copies ran while one was open for 6% of the time, Pallas kernels for 8%

profile of v6, /device:TPU:8, one launch (start us, length us, event | category | flops | bytes accessed | tf_op | source)
XLA Modules:
  0.0 372.9 jit_solution(4854458177883782628)
XLA Ops:
  9.5 7.2 %collective-permute-start.10 = (bf16[128,3584]{1,0:T(8,128)(2,1)}, bf16[128,3584]{1,0:T(8,128)(2,1)}, u32[]{:S(2)}, u32[]{:S(2)}) collective-permute-start(bf16[128,3584]{1,0:T(8,128)(2,1)} %pad_maximum_fusion.4), channel_id=1, source_target_pairs={{0,8},{8,0},{1,9},{9,1},{2,10},{10,2},{3,11},{11,3},{4,12},{12,4},... | collective-permute-start | bytes 2752520 | tf_op jit(solution)/shard_map/ppermute | solution.py:30
  18.7 3.6 shard_map.162
  22.3 5.0 %all-to-all-start.1 = ((bf16[4,80,3584]{2,1,0:T(8,128)(2,1)}), bf16[4,80,3584]{2,1,0:T(8,128)(2,1)S(1)}, u32[]{:S(2)}, u32[]{:S(2)}) async-start(bf16[4,80,3584]{2,1,0:T(8,128)(2,1)} %bitcast.9), calls=%async_computation.1 | async-start | bytes 4587520 | tf_op jit(solution)/shard_map/all_to_all | solution.py:324
  28.7 27.0 %collective-permute-done.10 = bf16[128,3584]{1,0:T(8,128)(2,1)} collective-permute-done((bf16[128,3584]{1,0:T(8,128)(2,1)}, bf16[128,3584]{1,0:T(8,128)(2,1)}, u32[]{:S(2)}, u32[]{:S(2)}) %collective-permute-start.10) | collective-permute-done | bytes 917536 | tf_op jit(solution)/shard_map/ppermute | solution.py:30
  57.1 5.2 %all-to-all-start = ((bf16[4,80,3584]{2,1,0:T(8,128)(2,1)}), bf16[4,80,3584]{2,1,0:T(8,128)(2,1)}, u32[]{:S(2)}, u32[]{:S(2)}) async-start(bf16[4,80,3584]{2,1,0:T(8,128)(2,1)} %bitcast.7), calls=%async_computation | async-start | bytes 4587520 | tf_op jit(solution)/shard_map/all_to_all | solution.py:324
  67.3 3.8 %collective-permute-start.6 = (bf16[80,3584]{1,0:T(8,128)(2,1)}, bf16[80,3584]{1,0:T(8,128)(2,1)S(1)}, u32[]{:S(2)}, u32[]{:S(2)}) collective-permute-start(bf16[80,3584]{1,0:T(8,128)(2,1)} %get-tuple-element.62), channel_id=1, source_target_pairs={{0,140},{4,128},{8,132},{12,136},{128,4},{132,8},{136,12},{140,0},... | collective-permute-start | bytes 1720328 | tf_op jit(solution)/shard_map/ppermute | solution.py:340
  71.1 14.5 %collective-permute-done.11 = bf16[128,3584]{1,0:T(8,128)(2,1)S(1)} collective-permute-done((bf16[128,3584]{1,0:T(8,128)(2,1)S(1)}, bf16[128,3584]{1,0:T(8,128)(2,1)S(1)}, u32[]{:S(2)}, u32[]{:S(2)}) %collective-permute-start.11) | collective-permute-done | bytes 917536 | tf_op jit(solution)/shard_map/ppermute | solution.py:30
  87.1 5.3 %collective-permute-start.5 = (bf16[80,3584]{1,0:T(8,128)(2,1)S(1)}, bf16[80,3584]{1,0:T(8,128)(2,1)S(1)}, u32[]{:S(2)}, u32[]{:S(2)}) collective-permute-start(bf16[80,3584]{1,0:T(8,128)(2,1)S(1)} %get-tuple-element.63), channel_id=1, source_target_pairs={{0,4},{4,8},{8,12},{12,0},{128,140},{132,128},{136,132},{140,136},... | collective-permute-start | bytes 1720328 | tf_op jit(solution)/shard_map/ppermute | solution.py:340
  92.4 3.2 collective-permute-start.7
  95.6 3.0 convolution_convert_fusion.2
  98.8 2.9 collective-permute-start
  104.5 4.4 %collective-permute-done.5 = bf16[80,3584]{1,0:T(8,128)(2,1)S(1)} collective-permute-done((bf16[80,3584]{1,0:T(8,128)(2,1)S(1)}, bf16[80,3584]{1,0:T(8,128)(2,1)S(1)}, u32[]{:S(2)}, u32[]{:S(2)}) %collective-permute-start.5) | collective-permute-done | bytes 573472 | tf_op jit(solution)/shard_map/ppermute | solution.py:340
  108.9 36.4 %collective-permute-done.7 = bf16[80,3584]{1,0:T(8,128)(2,1)S(1)} collective-permute-done((bf16[80,3584]{1,0:T(8,128)(2,1)S(1)}, bf16[80,3584]{1,0:T(8,128)(2,1)S(1)}, u32[]{:S(2)}, u32[]{:S(2)}) %collective-permute-start.7) | collective-permute-done | bytes 573472 | tf_op jit(solution)/shard_map/ppermute | solution.py:340
  145.6 9.9 %collective-permute-done.1 = bf16[80,3584]{1,0:T(8,128)(2,1)S(1)} collective-permute-done((bf16[80,3584]{1,0:T(8,128)(2,1)S(1)}, bf16[80,3584]{1,0:T(8,128)(2,1)S(1)}, u32[]{:S(2)}, u32[]{:S(2)}) %collective-permute-start.1) | collective-permute-done | bytes 573472 | tf_op jit(solution)/shard_map/ppermute | solution.py:340
  155.5 26.5 %collective-permute-done.2 = bf16[80,3584]{1,0:T(8,128)(2,1)S(1)} collective-permute-done((bf16[80,3584]{1,0:T(8,128)(2,1)S(1)}, bf16[80,3584]{1,0:T(8,128)(2,1)S(1)}, u32[]{:S(2)}, u32[]{:S(2)}) %collective-permute-start.2) | collective-permute-done | bytes 573472 | tf_op jit(solution)/shard_map/ppermute | solution.py:340
  186.5 4.8 %collective-permute-start.4 = (bf16[64,3584]{1,0:T(8,128)(2,1)}, bf16[64,3584]{1,0:T(8,128)(2,1)}, u32[]{:S(2)}, u32[]{:S(2)}) collective-permute-start(bf16[64,3584]{1,0:T(8,128)(2,1)} %get-tuple-element.30), channel_id=1, source_target_pairs={{0,8},{8,0},{1,9},{9,1},{2,10},{10,2},{3,11},{11,3},{4,12},{12,4},... | collective-permute-start | bytes 1376264 | tf_op jit(solution)/shard_map/ppermute | solution.py:30
  192.7 16.6 %shard_map.163 = (f32[320,3584]{1,0:T(8,128)}, bf16[320,3584]{1,0:T(8,128)(2,1)}, bf16[2,512,640]{2,1,0:T(8,128)(2,1)}) custom-call(bf16[320,3584]{1,0:T(8,128)(2,1)} %copy-done.4, bf16[320,3584]{1,0:T(8,128)(2,1)} %copy-done.12, bf16[320,3584]{1,0:T(8,128)(2,1)} %copy-done.5, bf16[320,3584]{1,0:T(8,128)(2,1)} %collective-permute-done.9.other_scaled_ref, ...), custom_call_target="tpu_custom_call" | custom-call | flops 7046430720 | bytes 36700160 | tf_op jit(solution)/shard_map/pallas_call | solution.py:205
  209.3 11.1 %shard_map.164 = bf16[8,128,3584]{2,1,0:T(8,128)(2,1)} custom-call(bf16[2,512,640]{2,1,0:T(8,128)(2,1)} %get-tuple-element.34.left_ref, bf16[320,3584]{1,0:T(8,128)(2,1)} %copy-done.4, bf16[320,3584]{1,0:T(8,128)(2,1)} %copy-done.12, bf16[320,3584]{1,0:T(8,128)(2,1)} %copy-done.5, bf16[320,3584]{1,0:T(8,128)(2,1)} %collective-permute-done.9.other_scaled_ref), custom_call_target="tpu_custom_call" | custom-call | bytes 1024 | tf_op jit(solution)/shard_map/pallas_call | solution.py:261
  220.5 8.7 %collective-permute-done.4 = bf16[64,3584]{1,0:T(8,128)(2,1)} collective-permute-done((bf16[64,3584]{1,0:T(8,128)(2,1)}, bf16[64,3584]{1,0:T(8,128)(2,1)}, u32[]{:S(2)}, u32[]{:S(2)}) %collective-permute-start.4) | collective-permute-done | bytes 458784 | tf_op jit(solution)/shard_map/ppermute | solution.py:30
  233.9 2.9 add_convert_fusion
  236.9 12.8 %collective-permute-done.12 = bf16[64,3584]{1,0:T(8,128)(2,1)S(1)} collective-permute-done((bf16[64,3584]{1,0:T(8,128)(2,1)S(1)}, bf16[64,3584]{1,0:T(8,128)(2,1)S(1)}, u32[]{:S(2)}, u32[]{:S(2)}) %collective-permute-start.12) | collective-permute-done | bytes 458784 | tf_op jit(solution)/shard_map/ppermute | solution.py:30
  250.0 3.9 %collective-permute-start.15 = (bf16[80,3584]{1,0:T(8,128)(2,1)S(1)}, bf16[80,3584]{1,0:T(8,128)(2,1)S(1)}, u32[]{:S(2)}, u32[]{:S(2)}) collective-permute-start(bf16[80,3584]{1,0:T(8,128)(2,1)S(1)} %get-tuple-element.58), channel_id=1, source_target_pairs={{140,0},{128,4},{132,8},{136,12},{4,128},{8,132},{12,136},{0,140},... | collective-permute-start | bytes 1720328 | tf_op jit(solution)/shard_map/ppermute | solution.py:340
  257.0 9.7 %collective-permute-done.14 = bf16[80,3584]{1,0:T(8,128)(2,1)S(1)} collective-permute-done((bf16[80,3584]{1,0:T(8,128)(2,1)S(1)}, bf16[80,3584]{1,0:T(8,128)(2,1)S(1)}, u32[]{:S(2)}, u32[]{:S(2)}) %collective-permute-start.14) | collective-permute-done | bytes 573472 | tf_op jit(solution)/shard_map/ppermute | solution.py:340
  266.7 13.2 %collective-permute-done.15 = bf16[80,3584]{1,0:T(8,128)(2,1)S(1)} collective-permute-done((bf16[80,3584]{1,0:T(8,128)(2,1)S(1)}, bf16[80,3584]{1,0:T(8,128)(2,1)S(1)}, u32[]{:S(2)}, u32[]{:S(2)}) %collective-permute-start.15) | collective-permute-done | bytes 573472 | tf_op jit(solution)/shard_map/ppermute | solution.py:340
  279.9 26.0 %collective-permute-done.16 = bf16[80,3584]{1,0:T(8,128)(2,1)S(1)} collective-permute-done((bf16[80,3584]{1,0:T(8,128)(2,1)S(1)}, bf16[80,3584]{1,0:T(8,128)(2,1)S(1)}, u32[]{:S(2)}, u32[]{:S(2)}) %collective-permute-start.16) | collective-permute-done | bytes 573472 | tf_op jit(solution)/shard_map/ppermute | solution.py:340
  306.1 2.8 convolution_convert_fusion
  308.9 5.9 %all-to-all-start.2 = ((bf16[4,80,3584]{2,1,0:T(8,128)(2,1)}), bf16[4,80,3584]{2,1,0:T(8,128)(2,1)}, u32[]{:S(2)}, u32[]{:S(2)}) async-start(bf16[4,80,3584]{2,1,0:T(8,128)(2,1)} %bitcast.87), calls=%async_computation.2 | async-start | bytes 4587520 | tf_op jit(solution)/shard_map/all_to_all | solution.py:324
  318.1 19.6 %collective-permute-done.17 = bf16[64,3584]{1,0:T(8,128)(2,1)} collective-permute-done((bf16[64,3584]{1,0:T(8,128)(2,1)}, bf16[64,3584]{1,0:T(8,128)(2,1)}, u32[]{:S(2)}, u32[]{:S(2)}) %collective-permute-start.17) | collective-permute-done | bytes 458784 | tf_op jit(solution)/shard_map/ppermute | solution.py:30
  337.7 3.7 all-to-all-done.2
  341.5 3.4 convolution_convert_fusion.3
  344.8 15.5 %collective-permute-done.18 = bf16[128,3584]{1,0:T(8,128)(2,1)} collective-permute-done((bf16[128,3584]{1,0:T(8,128)(2,1)}, bf16[128,3584]{1,0:T(8,128)(2,1)}, u32[]{:S(2)}, u32[]{:S(2)}) %collective-permute-start.18) | collective-permute-done | bytes 917536 | tf_op jit(solution)/shard_map/ppermute | solution.py:30
  361.8 4.3 %fusion.30 = (f32[1,64,3584]{2,1,0:T(8,128)}, bf16[1,64,3584]{2,1,0:T(8,128)(2,1)}, f32[1,64,3584]{2,1,0:T(8,128)}, f32[1,64,3584]{2,1,0:T(8,128)}, bf16[1,64,3584]{2,1,0:T(8,128)(2,1)}, /*index=5*/f32[1,64,3584]{2,1,0:T(8,128)}) fusion(f32[128,3584]{1,0:T(8,128)S(1)} %convert_add_fusion, f32[1,64,3584]{2,1,0:T(8,128)S(1)} %copy-done.9, ...), kind=kLoop, calls=%fused_computation.68 | loop fusion | flops 8257536 | bytes 12845057 | tf_op jit(solution)/shard_map/broadcast_in_dim | solution.py:412
  (74 shorter events, 34.9 us)
Async XLA Ops:
  7.2 10.2 %copy-start = (bf16[128,3584]{1,0:T(8,128)(2,1)S(1)}, bf16[128,3584]{1,0:T(8,128)(2,1)}, u32[]{:S(2)}) copy-start(bf16[128,3584]{1,0:T(8,128)(2,1)} %tokens_ref.1) | copy-start | bytes 2752516
  7.2 10.2 %copy-start.1 = (bf16[128,3584]{1,0:T(8,128)(2,1)S(1)}, bf16[128,3584]{1,0:T(8,128)(2,1)}, u32[]{:S(2)}) copy-start(bf16[128,3584]{1,0:T(8,128)(2,1)} %out_grad_ref.1) | copy-start | bytes 2752516
  9.5 46.2 %collective-permute-start.10 = (bf16[128,3584]{1,0:T(8,128)(2,1)}, bf16[128,3584]{1,0:T(8,128)(2,1)}, u32[]{:S(2)}, u32[]{:S(2)}) collective-permute-start(bf16[128,3584]{1,0:T(8,128)(2,1)} %pad_maximum_fusion.4), channel_id=1, source_target_pairs={{0,8},{8,0},{1,9},{9,1},{2,10},{10,2},{3,11},{11,3},{4,12},{12,4},... | collective-permute-start | bytes 2752520 | tf_op jit(solution)/shard_map/ppermute | solution.py:30
  22.3 34.8 %all-to-all-start.1 = ((bf16[4,80,3584]{2,1,0:T(8,128)(2,1)}), bf16[4,80,3584]{2,1,0:T(8,128)(2,1)S(1)}, u32[]{:S(2)}, u32[]{:S(2)}) async-start(bf16[4,80,3584]{2,1,0:T(8,128)(2,1)} %bitcast.9), calls=%async_computation.1 | async-start | bytes 4587520 | tf_op jit(solution)/shard_map/all_to_all | solution.py:324
  57.1 29.9 %all-to-all-start = ((bf16[4,80,3584]{2,1,0:T(8,128)(2,1)}), bf16[4,80,3584]{2,1,0:T(8,128)(2,1)}, u32[]{:S(2)}, u32[]{:S(2)}) async-start(bf16[4,80,3584]{2,1,0:T(8,128)(2,1)} %bitcast.7), calls=%async_computation | async-start | bytes 4587520 | tf_op jit(solution)/shard_map/all_to_all | solution.py:324
  62.3 129.0 %all-gather.3.cloned.1.call-start = ((), (), s32[]{:S(2)}) async-start(), calls=%async_computation.5 | async-start | bytes 9175040 | tf_op jit(solution)/shard_map/all_gather | solution.py:357
  63.7 21.9 %collective-permute-start.11 = (bf16[128,3584]{1,0:T(8,128)(2,1)S(1)}, bf16[128,3584]{1,0:T(8,128)(2,1)S(1)}, u32[]{:S(2)}, u32[]{:S(2)}) collective-permute-start(bf16[128,3584]{1,0:T(8,128)(2,1)S(1)} %broadcast_select_fusion), channel_id=1, source_target_pairs={{0,128},{128,0},{1,129},{129,1},{2,130},{130,2},{3,131},{131,3},{4... | collective-permute-start | bytes 2752520 | tf_op jit(solution)/shard_map/ppermute | solution.py:30
  67.3 19.7 %collective-permute-start.6 = (bf16[80,3584]{1,0:T(8,128)(2,1)}, bf16[80,3584]{1,0:T(8,128)(2,1)S(1)}, u32[]{:S(2)}, u32[]{:S(2)}) collective-permute-start(bf16[80,3584]{1,0:T(8,128)(2,1)} %get-tuple-element.62), channel_id=1, source_target_pairs={{0,140},{4,128},{8,132},{12,136},{128,4},{132,8},{136,12},{140,0},... | collective-permute-start | bytes 1720328 | tf_op jit(solution)/shard_map/ppermute | solution.py:340
  87.0 228.9 %reduce-scatter.2.cloned.1.call-start = ((), (), s32[]{:S(2)}) async-start(), calls=%async_computation.4 | async-start | bytes 9175040 | tf_op jit(solution)/shard_map/reduce_scatter | solution.py:389
  87.1 21.8 %collective-permute-start.5 = (bf16[80,3584]{1,0:T(8,128)(2,1)S(1)}, bf16[80,3584]{1,0:T(8,128)(2,1)S(1)}, u32[]{:S(2)}, u32[]{:S(2)}) collective-permute-start(bf16[80,3584]{1,0:T(8,128)(2,1)S(1)} %get-tuple-element.63), channel_id=1, source_target_pairs={{0,4},{4,8},{8,12},{12,0},{128,140},{132,128},{136,132},{140,136},... | collective-permute-start | bytes 1720328 | tf_op jit(solution)/shard_map/ppermute | solution.py:340
  92.4 52.9 %collective-permute-start.7 = (bf16[80,3584]{1,0:T(8,128)(2,1)S(1)}, bf16[80,3584]{1,0:T(8,128)(2,1)S(1)}, u32[]{:S(2)}, u32[]{:S(2)}) collective-permute-start(bf16[80,3584]{1,0:T(8,128)(2,1)S(1)} %get-tuple-element.61), channel_id=1, source_target_pairs={{0,136},{4,140},{8,128},{12,132},{128,8},{132,12},{136,0},{140,4},... | collective-permute-start | bytes 1720328 | tf_op jit(solution)/shard_map/ppermute | solution.py:340
  98.8 46.8 %collective-permute-start = (bf16[80,3584]{1,0:T(8,128)(2,1)S(1)}, bf16[80,3584]{1,0:T(8,128)(2,1)S(1)}, u32[]{:S(2)}, u32[]{:S(2)}) collective-permute-start(bf16[80,3584]{1,0:T(8,128)(2,1)S(1)} %get-tuple-element.67), channel_id=1, source_target_pairs={{0,4},{4,8},{8,12},{12,0},{128,140},{132,128},{136,132},{140,136},... | collective-permute-start | bytes 1720328 | tf_op jit(solution)/shard_map/ppermute | solution.py:340
  101.7 53.8 %collective-permute-start.1 = (bf16[80,3584]{1,0:T(8,128)(2,1)S(1)}, bf16[80,3584]{1,0:T(8,128)(2,1)S(1)}, u32[]{:S(2)}, u32[]{:S(2)}) collective-permute-start(bf16[80,3584]{1,0:T(8,128)(2,1)S(1)} %get-tuple-element.66), channel_id=1, source_target_pairs={{0,140},{4,128},{8,132},{12,136},{128,4},{132,8},{136,12},{140,0},... | collective-permute-start | bytes 1720328 | tf_op jit(solution)/shard_map/ppermute | solution.py:340
  101.7 80.4 %collective-permute-start.2 = (bf16[80,3584]{1,0:T(8,128)(2,1)S(1)}, bf16[80,3584]{1,0:T(8,128)(2,1)S(1)}, u32[]{:S(2)}, u32[]{:S(2)}) collective-permute-start(bf16[80,3584]{1,0:T(8,128)(2,1)S(1)} %get-tuple-element.65), channel_id=1, source_target_pairs={{0,136},{4,140},{8,128},{12,132},{128,8},{132,12},{136,0},{140,4},... | collective-permute-start | bytes 1720328 | tf_op jit(solution)/shard_map/ppermute | solution.py:340
  145.5 36.7 %copy-start.4 = (bf16[320,3584]{1,0:T(8,128)(2,1)}, bf16[320,3584]{1,0:T(8,128)(2,1)S(1)}, u32[]{:S(2)}) copy-start(bf16[320,3584]{1,0:T(8,128)(2,1)S(1)} %pad_maximum_fusion.1.mine_ref) | copy-start | bytes 6881284
  145.5 45.8 %collective-permute-start.8 = (bf16[320,3584]{1,0:T(8,128)(2,1)S(1)}, bf16[320,3584]{1,0:T(8,128)(2,1)S(1)}, u32[]{:S(2)}, u32[]{:S(2)}) collective-permute-start(bf16[320,3584]{1,0:T(8,128)(2,1)S(1)} %pad_maximum_fusion.1.mine_ref), channel_id=1, source_target_pairs={{0,16},{16,0},{1,17},{17,1},{2,18},{18,2},{3,19},{19,3},{4,20},{20... | collective-permute-start | bytes 6881288 | tf_op jit(solution)/shard_map/ppermute | solution.py:30
  182.2 9.1 %copy-start.5 = (bf16[320,3584]{1,0:T(8,128)(2,1)}, bf16[320,3584]{1,0:T(8,128)(2,1)S(1)}, u32[]{:S(2)}) copy-start(bf16[320,3584]{1,0:T(8,128)(2,1)S(1)} %pad_maximum_fusion.mine_scaled_ref) | copy-start | bytes 6881284
  182.2 9.1 %collective-permute-start.9 = (bf16[320,3584]{1,0:T(8,128)(2,1)S(1)}, bf16[320,3584]{1,0:T(8,128)(2,1)}, u32[]{:S(2)}, u32[]{:S(2)}) collective-permute-start(bf16[320,3584]{1,0:T(8,128)(2,1)S(1)} %pad_maximum_fusion.mine_scaled_ref), channel_id=1, source_target_pairs={{0,16},{16,0},{1,17},{17,1},{2,18},{18,2},{3,19},{19,3},{4,20},{20... | collective-permute-start | bytes 6881288 | tf_op jit(solution)/shard_map/ppermute | solution.py:30
  185.4 35.1 %collective-permute-start.3 = (bf16[64,3584]{1,0:T(8,128)(2,1)}, bf16[64,3584]{1,0:T(8,128)(2,1)}, u32[]{:S(2)}, u32[]{:S(2)}) collective-permute-start(bf16[64,3584]{1,0:T(8,128)(2,1)} %get-tuple-element.29), channel_id=1, source_target_pairs={{0,8},{8,0},{1,9},{9,1},{2,10},{10,2},{3,11},{11,3},{4,12},{12,4},... | collective-permute-start | bytes 1376264 | tf_op jit(solution)/shard_map/ppermute | solution.py:30
  186.5 42.6 %collective-permute-start.4 = (bf16[64,3584]{1,0:T(8,128)(2,1)}, bf16[64,3584]{1,0:T(8,128)(2,1)}, u32[]{:S(2)}, u32[]{:S(2)}) collective-permute-start(bf16[64,3584]{1,0:T(8,128)(2,1)} %get-tuple-element.30), channel_id=1, source_target_pairs={{0,8},{8,0},{1,9},{9,1},{2,10},{10,2},{3,11},{11,3},{4,12},{12,4},... | collective-permute-start | bytes 1376264 | tf_op jit(solution)/shard_map/ppermute | solution.py:30
  229.2 4.7 %collective-permute-start.13 = (bf16[320,3584]{1,0:T(8,128)(2,1)}, bf16[320,3584]{1,0:T(8,128)(2,1)S(1)}, u32[]{:S(2)}, u32[]{:S(2)}) collective-permute-start(bf16[320,3584]{1,0:T(8,128)(2,1)} %get-tuple-element.38), channel_id=1, source_target_pairs={{0,16},{16,0},{1,17},{17,1},{2,18},{18,2},{3,19},{19,3},{4,20},{20... | collective-permute-start | bytes 6881288 | tf_op jit(solution)/shard_map/ppermute | solution.py:30
  230.4 19.3 %collective-permute-start.12 = (bf16[64,3584]{1,0:T(8,128)(2,1)S(1)}, bf16[64,3584]{1,0:T(8,128)(2,1)S(1)}, u32[]{:S(2)}, u32[]{:S(2)}) collective-permute-start(bf16[64,3584]{1,0:T(8,128)(2,1)S(1)} %bitcast_convert_fusion.2), channel_id=1, source_target_pairs={{0,8},{8,0},{1,9},{9,1},{2,10},{10,2},{3,11},{11,3},{4,12},{12,4},... | collective-permute-start | bytes 1376264 | tf_op jit(solution)/shard_map/ppermute | solution.py:30
  236.9 19.3 %copy-start.7 = (f32[1,64,3584]{2,1,0:T(8,128)S(1)}, f32[1,64,3584]{2,1,0:T(8,128)}, u32[]{:S(2)}) copy-start(f32[1,64,3584]{2,1,0:T(8,128)} %param.21) | copy-start | bytes 2752516
  249.9 16.8 %collective-permute-start.14 = (bf16[80,3584]{1,0:T(8,128)(2,1)S(1)}, bf16[80,3584]{1,0:T(8,128)(2,1)S(1)}, u32[]{:S(2)}, u32[]{:S(2)}) collective-permute-start(bf16[80,3584]{1,0:T(8,128)(2,1)S(1)} %get-tuple-element.59), channel_id=1, source_target_pairs={{4,0},{8,4},{12,8},{0,12},{140,128},{128,132},{132,136},{136,140},... | collective-permute-start | bytes 1720328 | tf_op jit(solution)/shard_map/ppermute | solution.py:340
  250.0 29.9 %collective-permute-start.15 = (bf16[80,3584]{1,0:T(8,128)(2,1)S(1)}, bf16[80,3584]{1,0:T(8,128)(2,1)S(1)}, u32[]{:S(2)}, u32[]{:S(2)}) collective-permute-start(bf16[80,3584]{1,0:T(8,128)(2,1)S(1)} %get-tuple-element.58), channel_id=1, source_target_pairs={{140,0},{128,4},{132,8},{136,12},{4,128},{8,132},{12,136},{0,140},... | collective-permute-start | bytes 1720328 | tf_op jit(solution)/shard_map/ppermute | solution.py:340
  253.9 52.0 %collective-permute-start.16 = (bf16[80,3584]{1,0:T(8,128)(2,1)S(1)}, bf16[80,3584]{1,0:T(8,128)(2,1)S(1)}, u32[]{:S(2)}, u32[]{:S(2)}) collective-permute-start(bf16[80,3584]{1,0:T(8,128)(2,1)S(1)} %get-tuple-element.57), channel_id=1, source_target_pairs={{136,0},{140,4},{128,8},{132,12},{8,128},{12,132},{0,136},{4,140},... | collective-permute-start | bytes 1720328 | tf_op jit(solution)/shard_map/ppermute | solution.py:340
  308.9 32.6 %all-to-all-start.2 = ((bf16[4,80,3584]{2,1,0:T(8,128)(2,1)}), bf16[4,80,3584]{2,1,0:T(8,128)(2,1)}, u32[]{:S(2)}, u32[]{:S(2)}) async-start(bf16[4,80,3584]{2,1,0:T(8,128)(2,1)} %bitcast.87), calls=%async_computation.2 | async-start | bytes 4587520 | tf_op jit(solution)/shard_map/all_to_all | solution.py:324
  314.8 23.0 %collective-permute-start.17 = (bf16[64,3584]{1,0:T(8,128)(2,1)}, bf16[64,3584]{1,0:T(8,128)(2,1)}, u32[]{:S(2)}, u32[]{:S(2)}) collective-permute-start(bf16[64,3584]{1,0:T(8,128)(2,1)} %bitcast_convert_fusion.3), channel_id=1, source_target_pairs={{0,8},{8,0},{1,9},{9,1},{2,10},{10,2},{3,11},{11,3},{4,12},{12,4},... | collective-permute-start | bytes 1376264 | tf_op jit(solution)/shard_map/ppermute | solution.py:30
  337.7 22.6 %collective-permute-start.18 = (bf16[128,3584]{1,0:T(8,128)(2,1)}, bf16[128,3584]{1,0:T(8,128)(2,1)}, u32[]{:S(2)}, u32[]{:S(2)}) collective-permute-start(bf16[128,3584]{1,0:T(8,128)(2,1)} %slice_bitcast_fusion), channel_id=1, source_target_pairs={{0,128},{128,0},{1,129},{129,1},{2,130},{130,2},{3,131},{131,3},{4... | collective-permute-start | bytes 2752520 | tf_op jit(solution)/shard_map/ppermute | solution.py:30
  341.5 18.9 %copy-start.13 = (bf16[1,2,128,3584]{3,2,1,0:T(8,128)(2,1)S(1)}, bf16[1,2,128,3584]{3,2,1,0:T(8,128)(2,1)}, u32[]{:S(2)}) copy-start(bf16[1,2,128,3584]{3,2,1,0:T(8,128)(2,1)} %reduce-scatter.2.cloned.1.call-done) | copy-start | bytes 5505028
  344.8 16.9 %copy-start.9 = (f32[1,64,3584]{2,1,0:T(8,128)S(1)}, f32[1,64,3584]{2,1,0:T(8,128)}, u32[]{:S(2)}) copy-start(f32[1,64,3584]{2,1,0:T(8,128)} %param.19) | copy-start | bytes 2752516
  344.8 16.9 %copy-start.11 = (f32[1,64,3584]{2,1,0:T(8,128)S(1)}, f32[1,64,3584]{2,1,0:T(8,128)}, u32[]{:S(2)}) copy-start(f32[1,64,3584]{2,1,0:T(8,128)} %param.18) | copy-start | bytes 2752516
  (7 other events, 12.7 us)
Sparse Core Ops, SparseCore 0:
  87.2 79.8 all-gather.2
  229.3 72.0 reduce-scatter.1

commit v7 on v6

--- a/solution.py
+++ b/solution.py
@@ -56,7 +56,7 @@
 
 def dispatch_kernel(
     capacity,
-    flags_ref,
+    experts,
     routes_ref,
     probs_ref,
     tokens_ref,
@@ -66,18 +66,15 @@
     select_ref,
 ):
     tops, count = routes_ref.shape
-    experts = flags_ref.shape[0]
     rows, width = token_rows_ref.shape
     side = experts // HIGHS
-    half_axis = experts // 2
     my_high = lax.axis_index(FAR) * (HIGHS // 2) + lax.axis_index(STEP)
     my_near = lax.axis_index(NEAR)
     ids = lax.broadcasted_iota(jnp.int32, (experts, 1), 0)
-    slot = jnp.where(flags_ref[...] == 1, jnp.bitwise_xor(ids, half_axis), ids)
-    away = lax.shift_right_logical(slot, side.bit_length() - 1) - my_high
+    away = lax.shift_right_logical(ids, side.bit_length() - 1) - my_high
     away = jnp.bitwise_and(jnp.where(my_near == 0, away, -away), HIGHS - 1)
     block = jnp.where(away >= 2, 5 - away, away)
-    base = jnp.bitwise_and(slot, side - 1) * (HIGHS * capacity) + block * capacity
+    base = jnp.bitwise_and(ids, side - 1) * (HIGHS * capacity) + block * capacity
     base = base.astype(jnp.float32)
     expert_ids = lax.broadcasted_iota(jnp.int32, (experts, count), 0)
     before = (
@@ -111,13 +108,13 @@
             ).astype(jnp.bfloat16)
 
 
-def dispatch(swap_flags, routes, probs, tokens, out_grad, capacity):
+def dispatch(experts, routes, probs, tokens, out_grad, capacity):
     count, width = tokens.shape
-    rows = swap_flags.shape[0] * capacity
+    rows = experts * capacity
     whole = pl.BlockSpec(memory_space=pltpu.VMEM)
     return pl.pallas_call(
-        functools.partial(dispatch_kernel, capacity),
-        in_specs=[whole] * 5,
+        functools.partial(dispatch_kernel, capacity, experts),
+        in_specs=[whole] * 4,
         out_specs=[whole] * 3,
         out_shape=[
             jax.ShapeDtypeStruct((rows, width), jnp.bfloat16),
@@ -126,7 +123,7 @@
         ],
         compiler_params=pltpu.CompilerParams(vmem_limit_bytes=24 * 1024 * 1024),
         cost_estimate=pl.CostEstimate(flops=0, bytes_accessed=1024, transcendentals=0),
-    )(swap_flags.reshape(-1, 1), routes.T, probs.T, tokens, out_grad)
+    )(routes.T, probs.T, tokens, out_grad)
 
 
 def expert_kernel(
@@ -291,7 +288,6 @@
     ring = lax.axis_size(RING)
     near = lax.axis_size(NEAR)
     chips = ring * near
-    half_axis = experts // 2
     capacity = max(2, routes.size * 5 // (4 * experts))
     side_rows = high * capacity
     high_rows = side * capacity
@@ -307,10 +303,12 @@
     swapped = flag_mine == 1
 
     weights = jnp.concatenate((up_weight[0], down_weight[0]), axis=0)
-    weights_partner = partner(weights, FAR, 1)
+    moments = (up_first[0], up_second[0], down_first[0], down_second[0])
+    rounded = tuple(array.astype(jnp.bfloat16) for array in moments)
+    first_arrived = partner(rounded[0], FAR, 1)
 
     send_tokens, send_scaled, token_select = dispatch(
-        swap_flags, routes, probs, tokens, out_grad, capacity
+        experts, routes, probs, tokens, out_grad, capacity
     )
     buffer_ids = jnp.arange(buffer_rows, dtype=jnp.int32)
     other_order = (
@@ -342,30 +340,26 @@
             )
             for array, way in zip(blocks[1:], ways)
         ]
-        return jnp.concatenate(blocks[:1] + moved, axis=0), moved[1]
-
-    token_rows = pick(regroup, along_side(send_tokens))
+        return jnp.concatenate(blocks[:1] + moved, axis=0)
+
+    side_tokens = along_side(send_tokens)
+    token_rows = pick(regroup, side_tokens)
     side_scaled = along_side(send_scaled)
     scaled_rows = pick(regroup, side_scaled)
 
-    rows_mine, nearest = along_high(token_rows, False)
-
-    weights = jnp.where(swapped, weights_partner, weights)
-    weights, _ = lax.optimization_barrier((weights, token_rows))
+    rows_mine = along_high(token_rows, False)
+
     both = jnp.stack((weights, partner(weights, NEAR, 1)), axis=0)
-    both, _, _ = lax.optimization_barrier((both, side_scaled, nearest))
+    first_arrived, both, _ = lax.optimization_barrier((first_arrived, both, side_tokens))
     gathered = lax.all_gather(both, RING, axis=0).reshape(
         chips, 2 * local_hidden, model_width
     )
 
-    scaled_mine, _ = along_high(scaled_rows, False)
+    scaled_mine = along_high(scaled_rows, False)
     rows_other = partner(rows_mine, CORE, 1)
     scaled_other = partner(scaled_mine, CORE, 1)
-    moments = (up_first[0], up_second[0], down_first[0], down_second[0])
-
-    rounded = tuple(array.astype(jnp.bfloat16) for array in moments)
-    up_held, _ = lax.optimization_barrier((rounded[:2], scaled_mine))
-    up_arrived = tuple(partner(array, FAR, 1) for array in up_held)
+    down_held, _ = lax.optimization_barrier((rounded[2:], scaled_mine))
+    down_arrived = tuple(partner(array, FAR, 1) for array in down_held)
     pair_mine, for_other, left = expert_stage(
         rows_mine, rows_other, scaled_mine, scaled_other, gathered, inv_model, inv_hidden
     )
@@ -374,13 +368,13 @@
     )
     from_other = partner(for_other, CORE, 1)
     pair_grad = (pair_mine + from_other.astype(jnp.float32)).astype(jnp.bfloat16)
-    up_arrived, parts = lax.optimization_barrier((up_arrived, parts))
-    down_held, _ = lax.optimization_barrier((rounded[2], parts))
-    down_arrived = partner(down_held, FAR, 1)
-    down_arrived, pair_grad = lax.optimization_barrier((down_arrived, pair_grad))
-    back_rows, _ = along_high(pair_grad, True)
-    late_held, back_rows = lax.optimization_barrier((rounded[3], back_rows))
-    late_arrived = partner(late_held, FAR, 1)
+    down_arrived, parts = lax.optimization_barrier((down_arrived, parts))
+    held, _ = lax.optimization_barrier(((rounded[1], weights), parts))
+    second_arrived, weights_arrived = (partner(array, FAR, 1) for array in held)
+    second_arrived, weights_arrived, pair_grad = lax.optimization_barrier(
+        (second_arrived, weights_arrived, pair_grad)
+    )
+    back_rows = along_high(pair_grad, True)
     returned = along_side(pick(regroup, back_rows))
     token_grad = lax.dot_general(
         token_select, returned, (((0,), (0,)), ((), ())), preferred_element_type=jnp.float32
@@ -392,9 +386,11 @@
         scatter_dimension=0,
         tiled=False,
     )
-    late_arrived, beside = lax.optimization_barrier((late_arrived, beside))
-    arrived = (*up_arrived, down_arrived, late_arrived)
+    arrived = (first_arrived, second_arrived, *down_arrived)
     summed = own.astype(jnp.float32) + partner(beside, NEAR, 1).astype(jnp.float32)
+    summed_partner = partner(summed.astype(jnp.bfloat16), FAR, 1)
+    summed = jnp.where(swapped, summed_partner.astype(jnp.float32), summed)
+    weights = jnp.where(swapped, weights_arrived, weights)
     moments = tuple(
         jnp.where(swapped, new.astype(jnp.float32), old) for new, old in zip(arrived, moments)
     )

time: 374 us -> 395 us (1.056)
  the two profiles are of different devices: /device:TPU:8 before, /device:TPU:107 now
where the time goes in v7:
time: 395 us; the launch traced here: 394 us
  waiting for transfers between devices  228 us (58%)
  starting transfers between devices  80 us (20%)
  Pallas kernels  31.2 us (8%)
  other arithmetic  17.2 us (4%)
  between operations  15 us (4%)
  local copies, waits for them, and re-layouts  12.5 us (3%)
  matrix products  10.2 us (3%)
    ppermute x9, waiting for transfers between devices, along_high(): lax.ppermute(array, (NEAR, *HIGH), [(b, a) for a, b in way] if back else...  97.8 us
    ppermute x11, waiting for transfers between devices, partner(): lax.ppermute(array, axis, [(i, i ^ flip) for i in range(lax.axis_size(axi...  83.6 us
    ppermute x9, starting transfers between devices, along_high(): lax.ppermute(array, (NEAR, *HIGH), [(b, a) for a, b in way] if back else...  45 us
    all_to_all x3, waiting for transfers between devices, along_side(): lax.all_to_all(rows.reshape(side, side_rows, model_width), SIDE, split_ax...  37.7 us
    ppermute x11, starting transfers between devices, partner(): lax.ppermute(array, axis, [(i, i ^ flip) for i in range(lax.axis_size(axi...  21 us
    pallas_call x1, Pallas kernels, expert_stage(): pl.pallas_call(functools.partial(expert_kernel, steps, inv_model, inv_hid...  16.5 us
    all_to_all x3, starting transfers between devices, along_side(): lax.all_to_all(rows.reshape(side, side_rows, model_width), SIDE, split_ax...  14 us
    pallas_call x1, Pallas kernels, weight_stage(): pl.pallas_call(functools.partial(weight_kernel, inv_model, inv_hidden), g...  11.1 us
  transfers between devices with their start and end apart: 25, of which 12 were waited for; matrix products, arithmetic and copies ran while one was open for 7% of the time, Pallas kernels for 7%

profile of v7, /device:TPU:107, one launch (start us, length us, event | category | flops | bytes accessed | tf_op | source)
XLA Modules:
  0.0 394.0 jit_solution(6567520618499148022)
XLA Ops:
  10.9 3.6 shard_map.162
  14.5 4.4 %all-to-all-start.1 = ((bf16[4,80,3584]{2,1,0:T(8,128)(2,1)}), bf16[4,80,3584]{2,1,0:T(8,128)(2,1)S(1)}, u32[]{:S(2)}, u32[]{:S(2)}) async-start(bf16[4,80,3584]{2,1,0:T(8,128)(2,1)} %bitcast.9), calls=%async_computation.1 | async-start | bytes 4587520 | tf_op jit(solution)/shard_map/all_to_all | solution.py:322
  21.3 4.8 %collective-permute-start.10 = (bf16[64,3584]{1,0:T(8,128)(2,1)}, bf16[64,3584]{1,0:T(8,128)(2,1)S(1)}, u32[]{:S(2)}, u32[]{:S(2)}) collective-permute-start(bf16[64,3584]{1,0:T(8,128)(2,1)} %bitcast_convert_fusion), channel_id=1, source_target_pairs={{0,8},{8,0},{1,9},{9,1},{2,10},{10,2},{3,11},{11,3},{4,12},{12,4},... | collective-permute-start | bytes 1376264 | tf_op jit(solution)/shard_map/ppermute | solution.py:30
  26.1 15.8 %collective-permute-done.11 = bf16[128,3584]{1,0:T(8,128)(2,1)S(1)} collective-permute-done((bf16[128,3584]{1,0:T(8,128)(2,1)S(1)}, bf16[128,3584]{1,0:T(8,128)(2,1)S(1)}, u32[]{:S(2)}, u32[]{:S(2)}) %collective-permute-start.11) | collective-permute-done | bytes 917536 | tf_op jit(solution)/shard_map/ppermute | solution.py:30
  43.2 20.8 %collective-permute-done.10 = bf16[64,3584]{1,0:T(8,128)(2,1)S(1)} collective-permute-done((bf16[64,3584]{1,0:T(8,128)(2,1)}, bf16[64,3584]{1,0:T(8,128)(2,1)S(1)}, u32[]{:S(2)}, u32[]{:S(2)}) %collective-permute-start.10) | collective-permute-done | bytes 458784 | tf_op jit(solution)/shard_map/ppermute | solution.py:30
  64.8 4.7 %all-to-all-start = ((bf16[4,80,3584]{2,1,0:T(8,128)(2,1)}), bf16[4,80,3584]{2,1,0:T(8,128)(2,1)}, u32[]{:S(2)}, u32[]{:S(2)}) async-start(bf16[4,80,3584]{2,1,0:T(8,128)(2,1)} %bitcast.7), calls=%async_computation | async-start | bytes 4587520 | tf_op jit(solution)/shard_map/all_to_all | solution.py:322
  73.0 3.8 collective-permute-start.7
  76.7 18.3 %all-to-all-done = bf16[4,80,3584]{2,1,0:T(8,128)(2,1)} async-done(((bf16[4,80,3584]{2,1,0:T(8,128)(2,1)}), bf16[4,80,3584]{2,1,0:T(8,128)(2,1)}, u32[]{:S(2)}, u32[]{:S(2)}) %all-to-all-start) | async-done | bytes 2293792 | tf_op jit(solution)/shard_map/all_to_all | solution.py:322
  95.0 3.0 convolution_convert_fusion.2
  99.3 3.7 collective-permute-start.2
  103.1 25.5 %collective-permute-done.7 = bf16[80,3584]{1,0:T(8,128)(2,1)S(1)} collective-permute-done((bf16[80,3584]{1,0:T(8,128)(2,1)S(1)}, bf16[80,3584]{1,0:T(8,128)(2,1)S(1)}, u32[]{:S(2)}, u32[]{:S(2)}) %collective-permute-start.7) | collective-permute-done | bytes 573472 | tf_op jit(solution)/shard_map/ppermute | solution.py:338
  129.5 22.1 %collective-permute-done.1 = bf16[80,3584]{1,0:T(8,128)(2,1)S(1)} collective-permute-done((bf16[80,3584]{1,0:T(8,128)(2,1)S(1)}, bf16[80,3584]{1,0:T(8,128)(2,1)S(1)}, u32[]{:S(2)}, u32[]{:S(2)}) %collective-permute-start.1) | collective-permute-done | bytes 573472 | tf_op jit(solution)/shard_map/ppermute | solution.py:338
  151.6 13.1 %collective-permute-done.2 = bf16[80,3584]{1,0:T(8,128)(2,1)S(1)} collective-permute-done((bf16[80,3584]{1,0:T(8,128)(2,1)S(1)}, bf16[80,3584]{1,0:T(8,128)(2,1)S(1)}, u32[]{:S(2)}, u32[]{:S(2)}) %collective-permute-start.2) | collective-permute-done | bytes 573472 | tf_op jit(solution)/shard_map/ppermute | solution.py:338
  168.0 2.6 collective-permute-start.3
  170.6 2.7 collective-permute-start.4
  174.7 16.5 %shard_map.163 = (f32[320,3584]{1,0:T(8,128)}, bf16[320,3584]{1,0:T(8,128)(2,1)}, bf16[2,512,640]{2,1,0:T(8,128)(2,1)}) custom-call(bf16[320,3584]{1,0:T(8,128)(2,1)} %copy-done.4, bf16[320,3584]{1,0:T(8,128)(2,1)} %copy-done.15, bf16[320,3584]{1,0:T(8,128)(2,1)} %copy-done.5, bf16[320,3584]{1,0:T(8,128)(2,1)} %collective-permute-done.9.other_scaled_ref, ...), custom_call_target="tpu_custom_call" | custom-call | flops 7046430720 | bytes 36700160 | tf_op jit(solution)/shard_map/pallas_call | solution.py:202
  191.2 11.1 %shard_map.164 = bf16[8,128,3584]{2,1,0:T(8,128)(2,1)} custom-call(bf16[2,512,640]{2,1,0:T(8,128)(2,1)} %get-tuple-element.31.left_ref, bf16[320,3584]{1,0:T(8,128)(2,1)} %copy-done.4, bf16[320,3584]{1,0:T(8,128)(2,1)} %copy-done.15, bf16[320,3584]{1,0:T(8,128)(2,1)} %copy-done.5, bf16[320,3584]{1,0:T(8,128)(2,1)} %collective-permute-done.9.other_scaled_ref), custom_call_target="tpu_custom_call" | custom-call | bytes 1024 | tf_op jit(solution)/shard_map/pallas_call | solution.py:258
  204.4 3.0 collective-permute-start.13
  207.4 2.5 collective-permute-start.12
  209.9 2.9 add_convert_fusion
  212.9 35.1 %collective-permute-done.12 = bf16[64,3584]{1,0:T(8,128)(2,1)S(1)} collective-permute-done((bf16[64,3584]{1,0:T(8,128)(2,1)S(1)}, bf16[64,3584]{1,0:T(8,128)(2,1)S(1)}, u32[]{:S(2)}, u32[]{:S(2)}) %collective-permute-start.12) | collective-permute-done | bytes 458784 | tf_op jit(solution)/shard_map/ppermute | solution.py:30
  249.1 30.9 %collective-permute-start.15 = (bf16[80,3584]{1,0:T(8,128)(2,1)S(1)}, bf16[80,3584]{1,0:T(8,128)(2,1)}, u32[]{:S(2)}, u32[]{:S(2)}) collective-permute-start(bf16[80,3584]{1,0:T(8,128)(2,1)S(1)} %get-tuple-element.55), channel_id=1, source_target_pairs={{4,0},{8,4},{12,8},{0,12},{140,128},{128,132},{132,136},{136,140},... | collective-permute-start | bytes 1720328 | tf_op jit(solution)/shard_map/ppermute | solution.py:338
  284.5 8.8 %reduce-scatter.2.cloned.1.call-done = bf16[1,2,128,3584]{3,2,1,0:T(8,128)(2,1)} async-done(((bf16[4,2,128,3584]{3,2,1,0:T(8,128)(2,1)}), bf16[1,2,128,3584]{3,2,1,0:T(8,128)(2,1)}) %reduce-scatter.2.cloned.1.call-update) | async-done | bytes 1835024 | tf_op jit(solution)/shard_map/reduce_scatter | solution.py:383
  296.9 10.8 %collective-permute-done.16 = bf16[80,3584]{1,0:T(8,128)(2,1)} collective-permute-done((bf16[80,3584]{1,0:T(8,128)(2,1)S(1)}, bf16[80,3584]{1,0:T(8,128)(2,1)}, u32[]{:S(2)}, u32[]{:S(2)}) %collective-permute-start.16) | collective-permute-done | bytes 573472 | tf_op jit(solution)/shard_map/ppermute | solution.py:338
  307.7 26.3 %collective-permute-done.17 = bf16[80,3584]{1,0:T(8,128)(2,1)} collective-permute-done((bf16[80,3584]{1,0:T(8,128)(2,1)S(1)}, bf16[80,3584]{1,0:T(8,128)(2,1)}, u32[]{:S(2)}, u32[]{:S(2)}) %collective-permute-start.17) | collective-permute-done | bytes 573472 | tf_op jit(solution)/shard_map/ppermute | solution.py:338
  334.1 4.2 %convolution_convert_fusion = bf16[320,3584]{1,0:T(8,128)(2,1)} fusion(bf16[80,3584]{1,0:T(8,128)(2,1)} %collective-permute-done.17, bf16[80,3584]{1,0:T(8,128)(2,1)} %collective-permute-done.16, bf16[80,3584]{1,0:T(8,128)(2,1)} %collective-permute-done.15, bf16[80,3584]{1,0:T(8,128)(2,1)S(1)} %get-tuple-element.52, s32[320]{0:T(512)S(1)} %fusion.27), kind=kOutput, calls=%fused_computation | convolution fusion | flops 744427520 | bytes 4588800 | tf_op jit(solution)/shard_map/dot_general | solution.py:331
  338.3 4.9 %all-to-all-start.2 = ((bf16[4,80,3584]{2,1,0:T(8,128)(2,1)}), bf16[4,80,3584]{2,1,0:T(8,128)(2,1)S(1)}, u32[]{:S(2)}, u32[]{:S(2)}) async-start(bf16[4,80,3584]{2,1,0:T(8,128)(2,1)} %bitcast.88), calls=%async_computation.2 | async-start | bytes 4587520 | tf_op jit(solution)/shard_map/all_to_all | solution.py:322
  343.2 2.7 fusion.7
  345.9 2.5 collective-permute-start.19
  349.6 19.4 %all-to-all-done.2 = bf16[4,80,3584]{2,1,0:T(8,128)(2,1)S(1)} async-done(((bf16[4,80,3584]{2,1,0:T(8,128)(2,1)}), bf16[4,80,3584]{2,1,0:T(8,128)(2,1)S(1)}, u32[]{:S(2)}, u32[]{:S(2)}) %all-to-all-start.2) | async-done | bytes 2293792 | tf_op jit(solution)/shard_map/all_to_all | solution.py:322
  370.6 11.9 %collective-permute-done.19 = bf16[128,3584]{1,0:T(8,128)(2,1)} collective-permute-done((bf16[128,3584]{1,0:T(8,128)(2,1)}, bf16[128,3584]{1,0:T(8,128)(2,1)}, u32[]{:S(2)}, u32[]{:S(2)}) %collective-permute-start.19) | collective-permute-done | bytes 917536 | tf_op jit(solution)/shard_map/ppermute | solution.py:30
  384.3 2.9 fusion.39
  (107 shorter events, 33.6 us)
Async XLA Ops:
  14.5 49.6 %all-to-all-start.1 = ((bf16[4,80,3584]{2,1,0:T(8,128)(2,1)}), bf16[4,80,3584]{2,1,0:T(8,128)(2,1)S(1)}, u32[]{:S(2)}, u32[]{:S(2)}) async-start(bf16[4,80,3584]{2,1,0:T(8,128)(2,1)} %bitcast.9), calls=%async_computation.1 | async-start | bytes 4587520 | tf_op jit(solution)/shard_map/all_to_all | solution.py:322
  18.8 154.6 %all-gather.3.cloned.1.call-start = ((), (), s32[]{:S(2)}) async-start(), calls=%async_computation.5 | async-start | bytes 9175040 | tf_op jit(solution)/shard_map/all_gather | solution.py:354
  20.2 21.6 %copy-start.20 = (bf16[128,3584]{1,0:T(8,128)(2,1)}, bf16[128,3584]{1,0:T(8,128)(2,1)S(1)}, u32[]{:S(2)}) copy-start(bf16[128,3584]{1,0:T(8,128)(2,1)S(1)} %get-tuple-element.34) | copy-start | bytes 2752516
  20.2 21.6 %collective-permute-start.11 = (bf16[128,3584]{1,0:T(8,128)(2,1)S(1)}, bf16[128,3584]{1,0:T(8,128)(2,1)S(1)}, u32[]{:S(2)}, u32[]{:S(2)}) collective-permute-start(bf16[128,3584]{1,0:T(8,128)(2,1)S(1)} %get-tuple-element.34), channel_id=1, source_target_pairs={{0,128},{128,0},{1,129},{129,1},{2,130},{130,2},{3,131},{131,3},{4... | collective-permute-start | bytes 2752520 | tf_op jit(solution)/shard_map/ppermute | solution.py:30
  21.3 42.8 %collective-permute-start.10 = (bf16[64,3584]{1,0:T(8,128)(2,1)}, bf16[64,3584]{1,0:T(8,128)(2,1)S(1)}, u32[]{:S(2)}, u32[]{:S(2)}) collective-permute-start(bf16[64,3584]{1,0:T(8,128)(2,1)} %bitcast_convert_fusion), channel_id=1, source_target_pairs={{0,8},{8,0},{1,9},{9,1},{2,10},{10,2},{3,11},{11,3},{4,12},{12,4},... | collective-permute-start | bytes 1376264 | tf_op jit(solution)/shard_map/ppermute | solution.py:30
  64.8 30.2 %all-to-all-start = ((bf16[4,80,3584]{2,1,0:T(8,128)(2,1)}), bf16[4,80,3584]{2,1,0:T(8,128)(2,1)}, u32[]{:S(2)}, u32[]{:S(2)}) async-start(bf16[4,80,3584]{2,1,0:T(8,128)(2,1)} %bitcast.7), calls=%async_computation | async-start | bytes 4587520 | tf_op jit(solution)/shard_map/all_to_all | solution.py:322
  69.5 223.8 %reduce-scatter.2.cloned.1.call-start = ((), (), s32[]{:S(2)}) async-start(), calls=%async_computation.4 | async-start | bytes 9175040 | tf_op jit(solution)/shard_map/reduce_scatter | solution.py:383
  71.9 27.4 %collective-permute-start.5 = (bf16[80,3584]{1,0:T(8,128)(2,1)}, bf16[80,3584]{1,0:T(8,128)(2,1)S(1)}, u32[]{:S(2)}, u32[]{:S(2)}) collective-permute-start(bf16[80,3584]{1,0:T(8,128)(2,1)} %get-tuple-element.59), channel_id=1, source_target_pairs={{0,4},{4,8},{8,12},{12,0},{128,140},{132,128},{136,132},{140,136},... | collective-permute-start | bytes 1720328 | tf_op jit(solution)/shard_map/ppermute | solution.py:338
  72.0 31.1 %collective-permute-start.6 = (bf16[80,3584]{1,0:T(8,128)(2,1)S(1)}, bf16[80,3584]{1,0:T(8,128)(2,1)S(1)}, u32[]{:S(2)}, u32[]{:S(2)}) collective-permute-start(bf16[80,3584]{1,0:T(8,128)(2,1)S(1)} %get-tuple-element.58), channel_id=1, source_target_pairs={{0,140},{4,128},{8,132},{12,136},{128,4},{132,8},{136,12},{140,0},... | collective-permute-start | bytes 1720328 | tf_op jit(solution)/shard_map/ppermute | solution.py:338
  73.0 55.6 %collective-permute-start.7 = (bf16[80,3584]{1,0:T(8,128)(2,1)S(1)}, bf16[80,3584]{1,0:T(8,128)(2,1)S(1)}, u32[]{:S(2)}, u32[]{:S(2)}) collective-permute-start(bf16[80,3584]{1,0:T(8,128)(2,1)S(1)} %get-tuple-element.57), channel_id=1, source_target_pairs={{0,136},{4,140},{8,128},{12,132},{128,8},{132,12},{136,0},{140,4},... | collective-permute-start | bytes 1720328 | tf_op jit(solution)/shard_map/ppermute | solution.py:338
  98.2 31.3 %collective-permute-start = (bf16[80,3584]{1,0:T(8,128)(2,1)S(1)}, bf16[80,3584]{1,0:T(8,128)(2,1)S(1)}, u32[]{:S(2)}, u32[]{:S(2)}) collective-permute-start(bf16[80,3584]{1,0:T(8,128)(2,1)S(1)} %get-tuple-element.63), channel_id=1, source_target_pairs={{0,4},{4,8},{8,12},{12,0},{128,140},{132,128},{136,132},{140,136},... | collective-permute-start | bytes 1720328 | tf_op jit(solution)/shard_map/ppermute | solution.py:338
  98.3 53.3 %collective-permute-start.1 = (bf16[80,3584]{1,0:T(8,128)(2,1)S(1)}, bf16[80,3584]{1,0:T(8,128)(2,1)S(1)}, u32[]{:S(2)}, u32[]{:S(2)}) collective-permute-start(bf16[80,3584]{1,0:T(8,128)(2,1)S(1)} %get-tuple-element.62), channel_id=1, source_target_pairs={{0,140},{4,128},{8,132},{12,136},{128,4},{132,8},{136,12},{140,0},... | collective-permute-start | bytes 1720328 | tf_op jit(solution)/shard_map/ppermute | solution.py:338
  99.3 65.4 %collective-permute-start.2 = (bf16[80,3584]{1,0:T(8,128)(2,1)S(1)}, bf16[80,3584]{1,0:T(8,128)(2,1)S(1)}, u32[]{:S(2)}, u32[]{:S(2)}) collective-permute-start(bf16[80,3584]{1,0:T(8,128)(2,1)S(1)} %get-tuple-element.61), channel_id=1, source_target_pairs={{0,136},{4,140},{8,128},{12,132},{128,8},{132,12},{136,0},{140,4},... | collective-permute-start | bytes 1720328 | tf_op jit(solution)/shard_map/ppermute | solution.py:338
  128.7 36.1 %copy-start.4 = (bf16[320,3584]{1,0:T(8,128)(2,1)}, bf16[320,3584]{1,0:T(8,128)(2,1)S(1)}, u32[]{:S(2)}) copy-start(bf16[320,3584]{1,0:T(8,128)(2,1)S(1)} %pad_maximum_fusion.1.mine_ref) | copy-start | bytes 6881284
  128.7 44.6 %collective-permute-start.8 = (bf16[320,3584]{1,0:T(8,128)(2,1)S(1)}, bf16[320,3584]{1,0:T(8,128)(2,1)S(1)}, u32[]{:S(2)}, u32[]{:S(2)}) collective-permute-start(bf16[320,3584]{1,0:T(8,128)(2,1)S(1)} %pad_maximum_fusion.1.mine_ref), channel_id=1, source_target_pairs={{0,16},{16,0},{1,17},{17,1},{2,18},{18,2},{3,19},{19,3},{4,20},{20... | collective-permute-start | bytes 6881288 | tf_op jit(solution)/shard_map/ppermute | solution.py:30
  164.9 8.5 %collective-permute-start.9 = (bf16[320,3584]{1,0:T(8,128)(2,1)S(1)}, bf16[320,3584]{1,0:T(8,128)(2,1)}, u32[]{:S(2)}, u32[]{:S(2)}) collective-permute-start(bf16[320,3584]{1,0:T(8,128)(2,1)S(1)} %pad_maximum_fusion.mine_scaled_ref), channel_id=1, source_target_pairs={{0,16},{16,0},{1,17},{17,1},{2,18},{18,2},{3,19},{19,3},{4,20},{20... | collective-permute-start | bytes 6881288 | tf_op jit(solution)/shard_map/ppermute | solution.py:30
  168.0 34.3 %collective-permute-start.3 = (bf16[64,3584]{1,0:T(8,128)(2,1)}, bf16[64,3584]{1,0:T(8,128)(2,1)S(1)}, u32[]{:S(2)}, u32[]{:S(2)}) collective-permute-start(bf16[64,3584]{1,0:T(8,128)(2,1)} %get-tuple-element.27), channel_id=1, source_target_pairs={{0,8},{8,0},{1,9},{9,1},{2,10},{10,2},{3,11},{11,3},{4,12},{12,4},... | collective-permute-start | bytes 1376264 | tf_op jit(solution)/shard_map/ppermute | solution.py:30
  170.6 31.7 %collective-permute-start.4 = (bf16[64,3584]{1,0:T(8,128)(2,1)}, bf16[64,3584]{1,0:T(8,128)(2,1)S(1)}, u32[]{:S(2)}, u32[]{:S(2)}) collective-permute-start(bf16[64,3584]{1,0:T(8,128)(2,1)} %get-tuple-element.28), channel_id=1, source_target_pairs={{0,8},{8,0},{1,9},{9,1},{2,10},{10,2},{3,11},{11,3},{4,12},{12,4},... | collective-permute-start | bytes 1376264 | tf_op jit(solution)/shard_map/ppermute | solution.py:30
  203.2 6.7 %collective-permute-start.14 = (bf16[320,3584]{1,0:T(8,128)(2,1)}, bf16[320,3584]{1,0:T(8,128)(2,1)S(1)}, u32[]{:S(2)}, u32[]{:S(2)}) collective-permute-start(bf16[320,3584]{1,0:T(8,128)(2,1)} %get-tuple-element.36), channel_id=1, source_target_pairs={{0,16},{16,0},{1,17},{17,1},{2,18},{18,2},{3,19},{19,3},{4,20},{20... | collective-permute-start | bytes 6881288 | tf_op jit(solution)/shard_map/ppermute | solution.py:30
  204.4 43.6 %collective-permute-start.13 = (bf16[128,3584]{1,0:T(8,128)(2,1)S(1)}, bf16[128,3584]{1,0:T(8,128)(2,1)S(1)}, u32[]{:S(2)}, u32[]{:S(2)}) collective-permute-start(bf16[128,3584]{1,0:T(8,128)(2,1)S(1)} %copy-done.21), channel_id=1, source_target_pairs={{0,8},{8,0},{1,9},{9,1},{2,10},{10,2},{3,11},{11,3},{4,12},{12,4},... | collective-permute-start | bytes 2752520 | tf_op jit(solution)/shard_map/ppermute | solution.py:30
  207.4 40.6 %collective-permute-start.12 = (bf16[64,3584]{1,0:T(8,128)(2,1)S(1)}, bf16[64,3584]{1,0:T(8,128)(2,1)S(1)}, u32[]{:S(2)}, u32[]{:S(2)}) collective-permute-start(bf16[64,3584]{1,0:T(8,128)(2,1)S(1)} %bitcast_convert_fusion.3), channel_id=1, source_target_pairs={{0,8},{8,0},{1,9},{9,1},{2,10},{10,2},{3,11},{11,3},{4,12},{12,4},... | collective-permute-start | bytes 1376264 | tf_op jit(solution)/shard_map/ppermute | solution.py:30
  212.8 82.8 %copy-start.30 = (s32[16]{0:T(128)S(1)}, s32[16]{0:T(128)}, u32[]{:S(2)}) copy-start(s32[16]{0:T(128)} %param.15) | copy-start | bytes 196
  249.1 47.9 %collective-permute-start.15 = (bf16[80,3584]{1,0:T(8,128)(2,1)S(1)}, bf16[80,3584]{1,0:T(8,128)(2,1)}, u32[]{:S(2)}, u32[]{:S(2)}) collective-permute-start(bf16[80,3584]{1,0:T(8,128)(2,1)S(1)} %get-tuple-element.55), channel_id=1, source_target_pairs={{4,0},{8,4},{12,8},{0,12},{140,128},{128,132},{132,136},{136,140},... | collective-permute-start | bytes 1720328 | tf_op jit(solution)/shard_map/ppermute | solution.py:338
  280.0 27.7 %collective-permute-start.16 = (bf16[80,3584]{1,0:T(8,128)(2,1)S(1)}, bf16[80,3584]{1,0:T(8,128)(2,1)}, u32[]{:S(2)}, u32[]{:S(2)}) collective-permute-start(bf16[80,3584]{1,0:T(8,128)(2,1)S(1)} %get-tuple-element.54), channel_id=1, source_target_pairs={{140,0},{128,4},{132,8},{136,12},{4,128},{8,132},{12,136},{0,140},... | collective-permute-start | bytes 1720328 | tf_op jit(solution)/shard_map/ppermute | solution.py:338
  282.4 51.6 %collective-permute-start.17 = (bf16[80,3584]{1,0:T(8,128)(2,1)S(1)}, bf16[80,3584]{1,0:T(8,128)(2,1)}, u32[]{:S(2)}, u32[]{:S(2)}) collective-permute-start(bf16[80,3584]{1,0:T(8,128)(2,1)S(1)} %get-tuple-element.53), channel_id=1, source_target_pairs={{136,0},{140,4},{128,8},{132,12},{8,128},{12,132},{0,136},{4,140},... | collective-permute-start | bytes 1720328 | tf_op jit(solution)/shard_map/ppermute | solution.py:338
  295.5 47.7 %collective-permute-start.18 = (bf16[128,3584]{1,0:T(8,128)(2,1)}, bf16[128,3584]{1,0:T(8,128)(2,1)}, u32[]{:S(2)}, u32[]{:S(2)}) collective-permute-start(bf16[128,3584]{1,0:T(8,128)(2,1)} %slice_bitcast_fusion), channel_id=1, source_target_pairs={{0,128},{128,0},{1,129},{129,1},{2,130},{130,2},{3,131},{131,3},{4... | collective-permute-start | bytes 2752520 | tf_op jit(solution)/shard_map/ppermute | solution.py:30
  338.3 30.7 %all-to-all-start.2 = ((bf16[4,80,3584]{2,1,0:T(8,128)(2,1)}), bf16[4,80,3584]{2,1,0:T(8,128)(2,1)S(1)}, u32[]{:S(2)}, u32[]{:S(2)}) async-start(bf16[4,80,3584]{2,1,0:T(8,128)(2,1)} %bitcast.88), calls=%async_computation.2 | async-start | bytes 4587520 | tf_op jit(solution)/shard_map/all_to_all | solution.py:322
  345.9 36.5 %collective-permute-start.19 = (bf16[128,3584]{1,0:T(8,128)(2,1)}, bf16[128,3584]{1,0:T(8,128)(2,1)}, u32[]{:S(2)}, u32[]{:S(2)}) collective-permute-start(bf16[128,3584]{1,0:T(8,128)(2,1)} %fusion.7), channel_id=1, source_target_pairs={{0,8},{8,0},{1,9},{9,1},{2,10},{10,2},{3,11},{11,3},{4,12},{12,4},... | collective-permute-start | bytes 2752520 | tf_op jit(solution)/shard_map/ppermute | solution.py:30
  368.9 15.3 %copy-start.27 = (bf16[64,3584]{1,0:T(8,128)(2,1)S(1)}, bf16[64,3584]{1,0:T(8,128)(2,1)}, u32[]{:S(2)}) copy-start(bf16[64,3584]{1,0:T(8,128)(2,1)} %copy-done.26) | copy-start | bytes 1376260
  368.9 15.3 %copy-start.29 = (bf16[64,3584]{1,0:T(8,128)(2,1)S(1)}, bf16[64,3584]{1,0:T(8,128)(2,1)}, u32[]{:S(2)}) copy-start(bf16[64,3584]{1,0:T(8,128)(2,1)} %copy-done.28) | copy-start | bytes 1376260
  370.5 13.7 %copy-start.23 = (bf16[64,3584]{1,0:T(8,128)(2,1)S(1)}, bf16[64,3584]{1,0:T(8,128)(2,1)}, u32[]{:S(2)}) copy-start(bf16[64,3584]{1,0:T(8,128)(2,1)} %copy-done.22) | copy-start | bytes 1376260
  370.6 13.7 %copy-start.25 = (bf16[64,3584]{1,0:T(8,128)(2,1)S(1)}, bf16[64,3584]{1,0:T(8,128)(2,1)}, u32[]{:S(2)}) copy-start(bf16[64,3584]{1,0:T(8,128)(2,1)} %copy-done.24) | copy-start | bytes 1376260
  (24 other events, 111.1 us)
Sparse Core Ops, SparseCore 0:
  64.2 77.3 all-gather.2
  202.5 90.7 reduce-scatter.1

commit v8 on v6

--- a/solution.py
+++ b/solution.py
@@ -382,6 +382,7 @@
     late_held, back_rows = lax.optimization_barrier((rounded[3], back_rows))
     late_arrived = partner(late_held, FAR, 1)
     returned = along_side(pick(regroup, back_rows))
+    late_arrived, returned = lax.optimization_barrier((late_arrived, returned))
     token_grad = lax.dot_general(
         token_select, returned, (((0,), (0,)), ((), ())), preferred_element_type=jnp.float32
     ).astype(jnp.bfloat16)
@@ -392,7 +393,6 @@
         scatter_dimension=0,
         tiled=False,
     )
-    late_arrived, beside = lax.optimization_barrier((late_arrived, beside))
     arrived = (*up_arrived, down_arrived, late_arrived)
     summed = own.astype(jnp.float32) + partner(beside, NEAR, 1).astype(jnp.float32)
     moments = tuple(

time: 374 us -> 374 us (level)
  waiting for transfers between devices: 230 us -> 226 us
  transfers between devices with their start and end apart: 24 -> 24, of which waited for: 15 -> 13; matrix products, arithmetic and copies ran while one was open for 6% -> 6% of each run, Pallas kernels for 8% -> 8%
where the time goes in v8:
time: 374 us; the launch traced here: 369 us
  waiting for transfers between devices  226 us (60%)
  starting transfers between devices  59.5 us (16%)
  Pallas kernels  31.3 us (8%)
  other arithmetic  16.8 us (4%)
  between operations  14.9 us (4%)
  matrix products  10.6 us (3%)
  local copies, waits for them, and re-layouts  10.2 us (3%)
    ppermute x9, waiting for transfers between devices, along_high(): lax.ppermute(array, (NEAR, *HIGH), [(b, a) for a, b in way] if back else...  126 us
    ppermute x10, waiting for transfers between devices, partner(): lax.ppermute(array, axis, [(i, i ^ flip) for i in range(lax.axis_size(axi...  99.8 us
    ppermute x9, starting transfers between devices, along_high(): lax.ppermute(array, (NEAR, *HIGH), [(b, a) for a, b in way] if back else...  24.3 us
    ppermute x10, starting transfers between devices, partner(): lax.ppermute(array, axis, [(i, i ^ flip) for i in range(lax.axis_size(axi...  19 us
    pallas_call x1, Pallas kernels, expert_stage(): pl.pallas_call(functools.partial(expert_kernel, steps, inv_model, inv_hid...  16.6 us
    all_to_all x3, starting transfers between devices, along_side(): lax.all_to_all(rows.reshape(side, side_rows, model_width), SIDE, split_ax...  16.2 us
    pallas_call x1, Pallas kernels, weight_stage(): pl.pallas_call(functools.partial(weight_kernel, inv_model, inv_hidden), g...  11.1 us
  transfers between devices with their start and end apart: 24, of which 13 were waited for; matrix products, arithmetic and copies ran while one was open for 6% of the time, Pallas kernels for 8%

profile of v8, /device:TPU:8, one launch (start us, length us, event | category | flops | bytes accessed | tf_op | source)
XLA Modules:
  0.0 369.3 jit_solution(108182783515845096)
XLA Ops:
  9.5 7.2 %collective-permute-start.10 = (bf16[128,3584]{1,0:T(8,128)(2,1)}, bf16[128,3584]{1,0:T(8,128)(2,1)}, u32[]{:S(2)}, u32[]{:S(2)}) collective-permute-start(bf16[128,3584]{1,0:T(8,128)(2,1)} %pad_maximum_fusion.4), channel_id=1, source_target_pairs={{0,8},{8,0},{1,9},{9,1},{2,10},{10,2},{3,11},{11,3},{4,12},{12,4},... | collective-permute-start | bytes 2752520 | tf_op jit(solution)/shard_map/ppermute | solution.py:30
  18.7 3.6 shard_map.162
  22.3 5.0 %all-to-all-start.1 = ((bf16[4,80,3584]{2,1,0:T(8,128)(2,1)}), bf16[4,80,3584]{2,1,0:T(8,128)(2,1)S(1)}, u32[]{:S(2)}, u32[]{:S(2)}) async-start(bf16[4,80,3584]{2,1,0:T(8,128)(2,1)} %bitcast.9), calls=%async_computation.1 | async-start | bytes 4587520 | tf_op jit(solution)/shard_map/all_to_all | solution.py:324
  28.7 27.0 %collective-permute-done.10 = bf16[128,3584]{1,0:T(8,128)(2,1)} collective-permute-done((bf16[128,3584]{1,0:T(8,128)(2,1)}, bf16[128,3584]{1,0:T(8,128)(2,1)}, u32[]{:S(2)}, u32[]{:S(2)}) %collective-permute-start.10) | collective-permute-done | bytes 917536 | tf_op jit(solution)/shard_map/ppermute | solution.py:30
  57.1 5.2 %all-to-all-start = ((bf16[4,80,3584]{2,1,0:T(8,128)(2,1)}), bf16[4,80,3584]{2,1,0:T(8,128)(2,1)}, u32[]{:S(2)}, u32[]{:S(2)}) async-start(bf16[4,80,3584]{2,1,0:T(8,128)(2,1)} %bitcast.7), calls=%async_computation | async-start | bytes 4587520 | tf_op jit(solution)/shard_map/all_to_all | solution.py:324
  63.7 2.6 collective-permute-start.11
  67.3 3.8 %collective-permute-start.6 = (bf16[80,3584]{1,0:T(8,128)(2,1)}, bf16[80,3584]{1,0:T(8,128)(2,1)S(1)}, u32[]{:S(2)}, u32[]{:S(2)}) collective-permute-start(bf16[80,3584]{1,0:T(8,128)(2,1)} %get-tuple-element.62), channel_id=1, source_target_pairs={{0,140},{4,128},{8,132},{12,136},{128,4},{132,8},{136,12},{140,0},... | collective-permute-start | bytes 1720328 | tf_op jit(solution)/shard_map/ppermute | solution.py:340
  71.1 14.5 %collective-permute-done.11 = bf16[128,3584]{1,0:T(8,128)(2,1)S(1)} collective-permute-done((bf16[128,3584]{1,0:T(8,128)(2,1)S(1)}, bf16[128,3584]{1,0:T(8,128)(2,1)S(1)}, u32[]{:S(2)}, u32[]{:S(2)}) %collective-permute-start.11) | collective-permute-done | bytes 917536 | tf_op jit(solution)/shard_map/ppermute | solution.py:30
  87.1 5.3 %collective-permute-start.5 = (bf16[80,3584]{1,0:T(8,128)(2,1)S(1)}, bf16[80,3584]{1,0:T(8,128)(2,1)S(1)}, u32[]{:S(2)}, u32[]{:S(2)}) collective-permute-start(bf16[80,3584]{1,0:T(8,128)(2,1)S(1)} %get-tuple-element.63), channel_id=1, source_target_pairs={{0,4},{4,8},{8,12},{12,0},{128,140},{132,128},{136,132},{140,136},... | collective-permute-start | bytes 1720328 | tf_op jit(solution)/shard_map/ppermute | solution.py:340
  92.4 3.2 collective-permute-start.7
  95.6 3.0 convolution_convert_fusion.2
  98.8 2.9 collective-permute-start
  101.7 2.8 collective-permute-start.2
  104.5 4.4 %collective-permute-done.5 = bf16[80,3584]{1,0:T(8,128)(2,1)S(1)} collective-permute-done((bf16[80,3584]{1,0:T(8,128)(2,1)S(1)}, bf16[80,3584]{1,0:T(8,128)(2,1)S(1)}, u32[]{:S(2)}, u32[]{:S(2)}) %collective-permute-start.5) | collective-permute-done | bytes 573472 | tf_op jit(solution)/shard_map/ppermute | solution.py:340
  108.9 36.4 %collective-permute-done.7 = bf16[80,3584]{1,0:T(8,128)(2,1)S(1)} collective-permute-done((bf16[80,3584]{1,0:T(8,128)(2,1)S(1)}, bf16[80,3584]{1,0:T(8,128)(2,1)S(1)}, u32[]{:S(2)}, u32[]{:S(2)}) %collective-permute-start.7) | collective-permute-done | bytes 573472 | tf_op jit(solution)/shard_map/ppermute | solution.py:340
  145.6 9.9 %collective-permute-done.1 = bf16[80,3584]{1,0:T(8,128)(2,1)S(1)} collective-permute-done((bf16[80,3584]{1,0:T(8,128)(2,1)S(1)}, bf16[80,3584]{1,0:T(8,128)(2,1)S(1)}, u32[]{:S(2)}, u32[]{:S(2)}) %collective-permute-start.1) | collective-permute-done | bytes 573472 | tf_op jit(solution)/shard_map/ppermute | solution.py:340
  155.5 26.5 %collective-permute-done.2 = bf16[80,3584]{1,0:T(8,128)(2,1)S(1)} collective-permute-done((bf16[80,3584]{1,0:T(8,128)(2,1)S(1)}, bf16[80,3584]{1,0:T(8,128)(2,1)S(1)}, u32[]{:S(2)}, u32[]{:S(2)}) %collective-permute-start.2) | collective-permute-done | bytes 573472 | tf_op jit(solution)/shard_map/ppermute | solution.py:340
  186.5 4.8 %collective-permute-start.4 = (bf16[64,3584]{1,0:T(8,128)(2,1)}, bf16[64,3584]{1,0:T(8,128)(2,1)}, u32[]{:S(2)}, u32[]{:S(2)}) collective-permute-start(bf16[64,3584]{1,0:T(8,128)(2,1)} %get-tuple-element.30), channel_id=1, source_target_pairs={{0,8},{8,0},{1,9},{9,1},{2,10},{10,2},{3,11},{11,3},{4,12},{12,4},... | collective-permute-start | bytes 1376264 | tf_op jit(solution)/shard_map/ppermute | solution.py:30
  192.7 16.6 %shard_map.163 = (f32[320,3584]{1,0:T(8,128)}, bf16[320,3584]{1,0:T(8,128)(2,1)}, bf16[2,512,640]{2,1,0:T(8,128)(2,1)}) custom-call(bf16[320,3584]{1,0:T(8,128)(2,1)} %copy-done.4, bf16[320,3584]{1,0:T(8,128)(2,1)} %copy-done.12, bf16[320,3584]{1,0:T(8,128)(2,1)} %copy-done.5, bf16[320,3584]{1,0:T(8,128)(2,1)} %collective-permute-done.9.other_scaled_ref, ...), custom_call_target="tpu_custom_call" | custom-call | flops 7046430720 | bytes 36700160 | tf_op jit(solution)/shard_map/pallas_call | solution.py:205
  209.3 11.1 %shard_map.164 = bf16[8,128,3584]{2,1,0:T(8,128)(2,1)} custom-call(bf16[2,512,640]{2,1,0:T(8,128)(2,1)} %get-tuple-element.34.left_ref, bf16[320,3584]{1,0:T(8,128)(2,1)} %copy-done.4, bf16[320,3584]{1,0:T(8,128)(2,1)} %copy-done.12, bf16[320,3584]{1,0:T(8,128)(2,1)} %copy-done.5, bf16[320,3584]{1,0:T(8,128)(2,1)} %collective-permute-done.9.other_scaled_ref), custom_call_target="tpu_custom_call" | custom-call | bytes 1024 | tf_op jit(solution)/shard_map/pallas_call | solution.py:261
  220.5 8.7 %collective-permute-done.4 = bf16[64,3584]{1,0:T(8,128)(2,1)} collective-permute-done((bf16[64,3584]{1,0:T(8,128)(2,1)}, bf16[64,3584]{1,0:T(8,128)(2,1)}, u32[]{:S(2)}, u32[]{:S(2)}) %collective-permute-start.4) | collective-permute-done | bytes 458784 | tf_op jit(solution)/shard_map/ppermute | solution.py:30
  233.9 2.9 add_convert_fusion
  236.9 12.8 %collective-permute-done.12 = bf16[64,3584]{1,0:T(8,128)(2,1)S(1)} collective-permute-done((bf16[64,3584]{1,0:T(8,128)(2,1)S(1)}, bf16[64,3584]{1,0:T(8,128)(2,1)S(1)}, u32[]{:S(2)}, u32[]{:S(2)}) %collective-permute-start.12) | collective-permute-done | bytes 458784 | tf_op jit(solution)/shard_map/ppermute | solution.py:30
  250.0 3.9 %collective-permute-start.15 = (bf16[80,3584]{1,0:T(8,128)(2,1)S(1)}, bf16[80,3584]{1,0:T(8,128)(2,1)S(1)}, u32[]{:S(2)}, u32[]{:S(2)}) collective-permute-start(bf16[80,3584]{1,0:T(8,128)(2,1)S(1)} %get-tuple-element.58), channel_id=1, source_target_pairs={{140,0},{128,4},{132,8},{136,12},{4,128},{8,132},{12,136},{0,140},... | collective-permute-start | bytes 1720328 | tf_op jit(solution)/shard_map/ppermute | solution.py:340
  257.0 9.7 %collective-permute-done.14 = bf16[80,3584]{1,0:T(8,128)(2,1)S(1)} collective-permute-done((bf16[80,3584]{1,0:T(8,128)(2,1)S(1)}, bf16[80,3584]{1,0:T(8,128)(2,1)S(1)}, u32[]{:S(2)}, u32[]{:S(2)}) %collective-permute-start.14) | collective-permute-done | bytes 573472 | tf_op jit(solution)/shard_map/ppermute | solution.py:340
  266.7 13.2 %collective-permute-done.15 = bf16[80,3584]{1,0:T(8,128)(2,1)S(1)} collective-permute-done((bf16[80,3584]{1,0:T(8,128)(2,1)S(1)}, bf16[80,3584]{1,0:T(8,128)(2,1)S(1)}, u32[]{:S(2)}, u32[]{:S(2)}) %collective-permute-start.15) | collective-permute-done | bytes 573472 | tf_op jit(solution)/shard_map/ppermute | solution.py:340
  279.9 26.0 %collective-permute-done.16 = bf16[80,3584]{1,0:T(8,128)(2,1)S(1)} collective-permute-done((bf16[80,3584]{1,0:T(8,128)(2,1)S(1)}, bf16[80,3584]{1,0:T(8,128)(2,1)S(1)}, u32[]{:S(2)}, u32[]{:S(2)}) %collective-permute-start.16) | collective-permute-done | bytes 573472 | tf_op jit(solution)/shard_map/ppermute | solution.py:340
  306.1 2.8 convolution_convert_fusion
  308.9 5.9 %all-to-all-start.2 = ((bf16[4,80,3584]{2,1,0:T(8,128)(2,1)}), bf16[4,80,3584]{2,1,0:T(8,128)(2,1)}, u32[]{:S(2)}, u32[]{:S(2)}) async-start(bf16[4,80,3584]{2,1,0:T(8,128)(2,1)} %bitcast.87), calls=%async_computation.2 | async-start | bytes 4587520 | tf_op jit(solution)/shard_map/all_to_all | solution.py:324
  318.1 35.0 %collective-permute-done.17 = bf16[64,3584]{1,0:T(8,128)(2,1)} collective-permute-done((bf16[64,3584]{1,0:T(8,128)(2,1)}, bf16[64,3584]{1,0:T(8,128)(2,1)}, u32[]{:S(2)}, u32[]{:S(2)}) %collective-permute-start.17) | collective-permute-done | bytes 458784 | tf_op jit(solution)/shard_map/ppermute | solution.py:30
  353.1 3.4 convolution_convert_fusion.3
  358.2 4.3 %fusion.30 = (f32[1,64,3584]{2,1,0:T(8,128)}, bf16[1,64,3584]{2,1,0:T(8,128)(2,1)}, f32[1,64,3584]{2,1,0:T(8,128)}, f32[1,64,3584]{2,1,0:T(8,128)}, bf16[1,64,3584]{2,1,0:T(8,128)(2,1)}, /*index=5*/f32[1,64,3584]{2,1,0:T(8,128)}) fusion(f32[128,3584]{1,0:T(8,128)S(1)} %convert_add_fusion, f32[1,64,3584]{2,1,0:T(8,128)S(1)} %copy-done.9, ...), kind=kLoop, calls=%fused_computation.68 | loop fusion | flops 8257536 | bytes 12845057 | tf_op jit(solution)/shard_map/broadcast_in_dim | solution.py:412
  (74 shorter events, 29.8 us)
Async XLA Ops:
  7.2 10.2 %copy-start = (bf16[128,3584]{1,0:T(8,128)(2,1)S(1)}, bf16[128,3584]{1,0:T(8,128)(2,1)}, u32[]{:S(2)}) copy-start(bf16[128,3584]{1,0:T(8,128)(2,1)} %tokens_ref.1) | copy-start | bytes 2752516
  7.2 10.2 %copy-start.1 = (bf16[128,3584]{1,0:T(8,128)(2,1)S(1)}, bf16[128,3584]{1,0:T(8,128)(2,1)}, u32[]{:S(2)}) copy-start(bf16[128,3584]{1,0:T(8,128)(2,1)} %out_grad_ref.1) | copy-start | bytes 2752516
  9.5 46.2 %collective-permute-start.10 = (bf16[128,3584]{1,0:T(8,128)(2,1)}, bf16[128,3584]{1,0:T(8,128)(2,1)}, u32[]{:S(2)}, u32[]{:S(2)}) collective-permute-start(bf16[128,3584]{1,0:T(8,128)(2,1)} %pad_maximum_fusion.4), channel_id=1, source_target_pairs={{0,8},{8,0},{1,9},{9,1},{2,10},{10,2},{3,11},{11,3},{4,12},{12,4},... | collective-permute-start | bytes 2752520 | tf_op jit(solution)/shard_map/ppermute | solution.py:30
  22.3 5.0 %copy-start.14 = (s32[16]{0:T(128)S(1)}, s32[16]{0:T(128)}, u32[]{:S(2)}) copy-start(s32[16]{0:T(128)} %param.15) | copy-start | bytes 196
  22.3 34.8 %all-to-all-start.1 = ((bf16[4,80,3584]{2,1,0:T(8,128)(2,1)}), bf16[4,80,3584]{2,1,0:T(8,128)(2,1)S(1)}, u32[]{:S(2)}, u32[]{:S(2)}) async-start(bf16[4,80,3584]{2,1,0:T(8,128)(2,1)} %bitcast.9), calls=%async_computation.1 | async-start | bytes 4587520 | tf_op jit(solution)/shard_map/all_to_all | solution.py:324
  57.1 29.9 %all-to-all-start = ((bf16[4,80,3584]{2,1,0:T(8,128)(2,1)}), bf16[4,80,3584]{2,1,0:T(8,128)(2,1)}, u32[]{:S(2)}, u32[]{:S(2)}) async-start(bf16[4,80,3584]{2,1,0:T(8,128)(2,1)} %bitcast.7), calls=%async_computation | async-start | bytes 4587520 | tf_op jit(solution)/shard_map/all_to_all | solution.py:324
  62.3 129.0 %all-gather.3.cloned.1.call-start = ((), (), s32[]{:S(2)}) async-start(), calls=%async_computation.5 | async-start | bytes 9175040 | tf_op jit(solution)/shard_map/all_gather | solution.py:357
  63.7 21.9 %collective-permute-start.11 = (bf16[128,3584]{1,0:T(8,128)(2,1)S(1)}, bf16[128,3584]{1,0:T(8,128)(2,1)S(1)}, u32[]{:S(2)}, u32[]{:S(2)}) collective-permute-start(bf16[128,3584]{1,0:T(8,128)(2,1)S(1)} %broadcast_select_fusion), channel_id=1, source_target_pairs={{0,128},{128,0},{1,129},{129,1},{2,130},{130,2},{3,131},{131,3},{4... | collective-permute-start | bytes 2752520 | tf_op jit(solution)/shard_map/ppermute | solution.py:30
  67.3 19.7 %collective-permute-start.6 = (bf16[80,3584]{1,0:T(8,128)(2,1)}, bf16[80,3584]{1,0:T(8,128)(2,1)S(1)}, u32[]{:S(2)}, u32[]{:S(2)}) collective-permute-start(bf16[80,3584]{1,0:T(8,128)(2,1)} %get-tuple-element.62), channel_id=1, source_target_pairs={{0,140},{4,128},{8,132},{12,136},{128,4},{132,8},{136,12},{140,0},... | collective-permute-start | bytes 1720328 | tf_op jit(solution)/shard_map/ppermute | solution.py:340
  87.0 227.7 %reduce-scatter.2.cloned.1.call-start = ((), (), s32[]{:S(2)}) async-start(), calls=%async_computation.4 | async-start | bytes 9175040 | tf_op jit(solution)/shard_map/reduce_scatter | solution.py:390
  87.1 21.8 %collective-permute-start.5 = (bf16[80,3584]{1,0:T(8,128)(2,1)S(1)}, bf16[80,3584]{1,0:T(8,128)(2,1)S(1)}, u32[]{:S(2)}, u32[]{:S(2)}) collective-permute-start(bf16[80,3584]{1,0:T(8,128)(2,1)S(1)} %get-tuple-element.63), channel_id=1, source_target_pairs={{0,4},{4,8},{8,12},{12,0},{128,140},{132,128},{136,132},{140,136},... | collective-permute-start | bytes 1720328 | tf_op jit(solution)/shard_map/ppermute | solution.py:340
  92.4 52.9 %collective-permute-start.7 = (bf16[80,3584]{1,0:T(8,128)(2,1)S(1)}, bf16[80,3584]{1,0:T(8,128)(2,1)S(1)}, u32[]{:S(2)}, u32[]{:S(2)}) collective-permute-start(bf16[80,3584]{1,0:T(8,128)(2,1)S(1)} %get-tuple-element.61), channel_id=1, source_target_pairs={{0,136},{4,140},{8,128},{12,132},{128,8},{132,12},{136,0},{140,4},... | collective-permute-start | bytes 1720328 | tf_op jit(solution)/shard_map/ppermute | solution.py:340
  98.8 46.8 %collective-permute-start = (bf16[80,3584]{1,0:T(8,128)(2,1)S(1)}, bf16[80,3584]{1,0:T(8,128)(2,1)S(1)}, u32[]{:S(2)}, u32[]{:S(2)}) collective-permute-start(bf16[80,3584]{1,0:T(8,128)(2,1)S(1)} %get-tuple-element.67), channel_id=1, source_target_pairs={{0,4},{4,8},{8,12},{12,0},{128,140},{132,128},{136,132},{140,136},... | collective-permute-start | bytes 1720328 | tf_op jit(solution)/shard_map/ppermute | solution.py:340
  101.7 53.8 %collective-permute-start.1 = (bf16[80,3584]{1,0:T(8,128)(2,1)S(1)}, bf16[80,3584]{1,0:T(8,128)(2,1)S(1)}, u32[]{:S(2)}, u32[]{:S(2)}) collective-permute-start(bf16[80,3584]{1,0:T(8,128)(2,1)S(1)} %get-tuple-element.66), channel_id=1, source_target_pairs={{0,140},{4,128},{8,132},{12,136},{128,4},{132,8},{136,12},{140,0},... | collective-permute-start | bytes 1720328 | tf_op jit(solution)/shard_map/ppermute | solution.py:340
  101.7 80.4 %collective-permute-start.2 = (bf16[80,3584]{1,0:T(8,128)(2,1)S(1)}, bf16[80,3584]{1,0:T(8,128)(2,1)S(1)}, u32[]{:S(2)}, u32[]{:S(2)}) collective-permute-start(bf16[80,3584]{1,0:T(8,128)(2,1)S(1)} %get-tuple-element.65), channel_id=1, source_target_pairs={{0,136},{4,140},{8,128},{12,132},{128,8},{132,12},{136,0},{140,4},... | collective-permute-start | bytes 1720328 | tf_op jit(solution)/shard_map/ppermute | solution.py:340
  145.5 36.7 %copy-start.4 = (bf16[320,3584]{1,0:T(8,128)(2,1)}, bf16[320,3584]{1,0:T(8,128)(2,1)S(1)}, u32[]{:S(2)}) copy-start(bf16[320,3584]{1,0:T(8,128)(2,1)S(1)} %pad_maximum_fusion.1.mine_ref) | copy-start | bytes 6881284
  145.5 45.8 %collective-permute-start.8 = (bf16[320,3584]{1,0:T(8,128)(2,1)S(1)}, bf16[320,3584]{1,0:T(8,128)(2,1)S(1)}, u32[]{:S(2)}, u32[]{:S(2)}) collective-permute-start(bf16[320,3584]{1,0:T(8,128)(2,1)S(1)} %pad_maximum_fusion.1.mine_ref), channel_id=1, source_target_pairs={{0,16},{16,0},{1,17},{17,1},{2,18},{18,2},{3,19},{19,3},{4,20},{20... | collective-permute-start | bytes 6881288 | tf_op jit(solution)/shard_map/ppermute | solution.py:30
  182.1 2.3 copy-start.10
  182.2 9.1 %copy-start.5 = (bf16[320,3584]{1,0:T(8,128)(2,1)}, bf16[320,3584]{1,0:T(8,128)(2,1)S(1)}, u32[]{:S(2)}) copy-start(bf16[320,3584]{1,0:T(8,128)(2,1)S(1)} %pad_maximum_fusion.mine_scaled_ref) | copy-start | bytes 6881284
  182.2 9.1 %collective-permute-start.9 = (bf16[320,3584]{1,0:T(8,128)(2,1)S(1)}, bf16[320,3584]{1,0:T(8,128)(2,1)}, u32[]{:S(2)}, u32[]{:S(2)}) collective-permute-start(bf16[320,3584]{1,0:T(8,128)(2,1)S(1)} %pad_maximum_fusion.mine_scaled_ref), channel_id=1, source_target_pairs={{0,16},{16,0},{1,17},{17,1},{2,18},{18,2},{3,19},{19,3},{4,20},{20... | collective-permute-start | bytes 6881288 | tf_op jit(solution)/shard_map/ppermute | solution.py:30
  185.4 35.1 %collective-permute-start.3 = (bf16[64,3584]{1,0:T(8,128)(2,1)}, bf16[64,3584]{1,0:T(8,128)(2,1)}, u32[]{:S(2)}, u32[]{:S(2)}) collective-permute-start(bf16[64,3584]{1,0:T(8,128)(2,1)} %get-tuple-element.29), channel_id=1, source_target_pairs={{0,8},{8,0},{1,9},{9,1},{2,10},{10,2},{3,11},{11,3},{4,12},{12,4},... | collective-permute-start | bytes 1376264 | tf_op jit(solution)/shard_map/ppermute | solution.py:30
  186.5 42.6 %collective-permute-start.4 = (bf16[64,3584]{1,0:T(8,128)(2,1)}, bf16[64,3584]{1,0:T(8,128)(2,1)}, u32[]{:S(2)}, u32[]{:S(2)}) collective-permute-start(bf16[64,3584]{1,0:T(8,128)(2,1)} %get-tuple-element.30), channel_id=1, source_target_pairs={{0,8},{8,0},{1,9},{9,1},{2,10},{10,2},{3,11},{11,3},{4,12},{12,4},... | collective-permute-start | bytes 1376264 | tf_op jit(solution)/shard_map/ppermute | solution.py:30
  229.2 4.7 %collective-permute-start.13 = (bf16[320,3584]{1,0:T(8,128)(2,1)}, bf16[320,3584]{1,0:T(8,128)(2,1)S(1)}, u32[]{:S(2)}, u32[]{:S(2)}) collective-permute-start(bf16[320,3584]{1,0:T(8,128)(2,1)} %get-tuple-element.38), channel_id=1, source_target_pairs={{0,16},{16,0},{1,17},{17,1},{2,18},{18,2},{3,19},{19,3},{4,20},{20... | collective-permute-start | bytes 6881288 | tf_op jit(solution)/shard_map/ppermute | solution.py:30
  230.4 19.3 %collective-permute-start.12 = (bf16[64,3584]{1,0:T(8,128)(2,1)S(1)}, bf16[64,3584]{1,0:T(8,128)(2,1)S(1)}, u32[]{:S(2)}, u32[]{:S(2)}) collective-permute-start(bf16[64,3584]{1,0:T(8,128)(2,1)S(1)} %bitcast_convert_fusion.2), channel_id=1, source_target_pairs={{0,8},{8,0},{1,9},{9,1},{2,10},{10,2},{3,11},{11,3},{4,12},{12,4},... | collective-permute-start | bytes 1376264 | tf_op jit(solution)/shard_map/ppermute | solution.py:30
  236.9 19.3 %copy-start.7 = (f32[1,64,3584]{2,1,0:T(8,128)S(1)}, f32[1,64,3584]{2,1,0:T(8,128)}, u32[]{:S(2)}) copy-start(f32[1,64,3584]{2,1,0:T(8,128)} %param.21) | copy-start | bytes 2752516
  249.9 16.8 %collective-permute-start.14 = (bf16[80,3584]{1,0:T(8,128)(2,1)S(1)}, bf16[80,3584]{1,0:T(8,128)(2,1)S(1)}, u32[]{:S(2)}, u32[]{:S(2)}) collective-permute-start(bf16[80,3584]{1,0:T(8,128)(2,1)S(1)} %get-tuple-element.59), channel_id=1, source_target_pairs={{4,0},{8,4},{12,8},{0,12},{140,128},{128,132},{132,136},{136,140},... | collective-permute-start | bytes 1720328 | tf_op jit(solution)/shard_map/ppermute | solution.py:340
  250.0 29.9 %collective-permute-start.15 = (bf16[80,3584]{1,0:T(8,128)(2,1)S(1)}, bf16[80,3584]{1,0:T(8,128)(2,1)S(1)}, u32[]{:S(2)}, u32[]{:S(2)}) collective-permute-start(bf16[80,3584]{1,0:T(8,128)(2,1)S(1)} %get-tuple-element.58), channel_id=1, source_target_pairs={{140,0},{128,4},{132,8},{136,12},{4,128},{8,132},{12,136},{0,140},... | collective-permute-start | bytes 1720328 | tf_op jit(solution)/shard_map/ppermute | solution.py:340
  253.9 52.0 %collective-permute-start.16 = (bf16[80,3584]{1,0:T(8,128)(2,1)S(1)}, bf16[80,3584]{1,0:T(8,128)(2,1)S(1)}, u32[]{:S(2)}, u32[]{:S(2)}) collective-permute-start(bf16[80,3584]{1,0:T(8,128)(2,1)S(1)} %get-tuple-element.57), channel_id=1, source_target_pairs={{136,0},{140,4},{128,8},{132,12},{8,128},{12,132},{0,136},{4,140},... | collective-permute-start | bytes 1720328 | tf_op jit(solution)/shard_map/ppermute | solution.py:340
  308.9 44.2 %all-to-all-start.2 = ((bf16[4,80,3584]{2,1,0:T(8,128)(2,1)}), bf16[4,80,3584]{2,1,0:T(8,128)(2,1)}, u32[]{:S(2)}, u32[]{:S(2)}) async-start(bf16[4,80,3584]{2,1,0:T(8,128)(2,1)} %bitcast.87), calls=%async_computation.2 | async-start | bytes 4587520 | tf_op jit(solution)/shard_map/all_to_all | solution.py:324
  316.9 39.6 %collective-permute-start.18 = (bf16[128,3584]{1,0:T(8,128)(2,1)}, bf16[128,3584]{1,0:T(8,128)(2,1)}, u32[]{:S(2)}, u32[]{:S(2)}) collective-permute-start(bf16[128,3584]{1,0:T(8,128)(2,1)} %slice_bitcast_fusion), channel_id=1, source_target_pairs={{0,128},{128,0},{1,129},{129,1},{2,130},{130,2},{3,131},{131,3},{4... | collective-permute-start | bytes 2752520 | tf_op jit(solution)/shard_map/ppermute | solution.py:30
  316.9 36.2 %collective-permute-start.17 = (bf16[64,3584]{1,0:T(8,128)(2,1)}, bf16[64,3584]{1,0:T(8,128)(2,1)}, u32[]{:S(2)}, u32[]{:S(2)}) collective-permute-start(bf16[64,3584]{1,0:T(8,128)(2,1)} %bitcast_convert_fusion.3), channel_id=1, source_target_pairs={{0,8},{8,0},{1,9},{9,1},{2,10},{10,2},{3,11},{11,3},{4,12},{12,4},... | collective-permute-start | bytes 1376264 | tf_op jit(solution)/shard_map/ppermute | solution.py:30
  353.1 3.4 copy-start.13
  (7 other events, 8.6 us)
Sparse Core Ops, SparseCore 0:
  87.2 79.8 all-gather.2
  229.3 72.0 reduce-scatter.1

commit v9 on v4

--- a/solution.py
+++ b/solution.py
@@ -377,8 +377,8 @@
     up_arrived, parts = lax.optimization_barrier((up_arrived, parts))
     down_held, _ = lax.optimization_barrier((rounded[2], parts))
     down_arrived = partner(down_held, FAR, 1)
-    down_arrived, pair_grad = lax.optimization_barrier((down_arrived, pair_grad))
     back_rows, _ = along_high(pair_grad, True)
+    down_arrived, back_rows = lax.optimization_barrier((down_arrived, back_rows))
     late_held, back_rows = lax.optimization_barrier((rounded[3], back_rows))
     late_arrived = partner(late_held, FAR, 1)
     returned = along_side(pick(regroup, back_rows))

time: 374 us -> 378 us (1.011)
  waiting for transfers between devices: 212 us -> 220 us
    ppermute x9, waiting for transfers between devices: 108 us -> 124 us  [along_high(): lax.ppermute(array, (NEAR, *HIGH), [(b, a) for a, b in way] if back else...]
    ppermute x10, waiting for transfers between devices: 104 us -> 96 us  [partner(): lax.ppermute(array, axis, [(i, i ^ flip) for i in range(lax.axis_size(axi...]
    ppermute x9, starting transfers between devices: 32 us -> 26.8 us  [along_high(): lax.ppermute(array, (NEAR, *HIGH), [(b, a) for a, b in way] if back else...]
  transfers between devices with their start and end apart: 24 -> 24, of which waited for: 12 -> 11; matrix products, arithmetic and copies ran while one was open for 6% -> 6% of each run, Pallas kernels for 10% -> 10%
where the time goes in v9:
time: 378 us; the launch traced here: 377 us
  waiting for transfers between devices  220 us (58%)
  starting transfers between devices  68.7 us (18%)
  Pallas kernels  36.1 us (10%)
  other arithmetic  16.8 us (4%)
  between operations  14.9 us (4%)
  matrix products  10.6 us (3%)
  local copies, waits for them, and re-layouts  10.2 us (3%)
    ppermute x9, waiting for transfers between devices, along_high(): lax.ppermute(array, (NEAR, *HIGH), [(b, a) for a, b in way] if back else...  124 us
    ppermute x10, waiting for transfers between devices, partner(): lax.ppermute(array, axis, [(i, i ^ flip) for i in range(lax.axis_size(axi...  96 us
    ppermute x9, starting transfers between devices, along_high(): lax.ppermute(array, (NEAR, *HIGH), [(b, a) for a, b in way] if back else...  26.8 us
    ppermute x10, starting transfers between devices, partner(): lax.ppermute(array, axis, [(i, i ^ flip) for i in range(lax.axis_size(axi...  26.4 us
    pallas_call x1, Pallas kernels, expert_stage(): pl.pallas_call(functools.partial(expert_kernel, steps, inv_model, inv_hid...  20.6 us
    all_to_all x3, starting transfers between devices, along_side(): lax.all_to_all(rows.reshape(side, side_rows, model_width), SIDE, split_ax...  15.4 us
    pallas_call x1, Pallas kernels, weight_stage(): pl.pallas_call(functools.partial(weight_kernel, inv_model, inv_hidden), g...  11.9 us
  transfers between devices with their start and end apart: 24, of which 11 were waited for; matrix products, arithmetic and copies ran while one was open for 6% of the time, Pallas kernels for 10%

profile of v9, /device:TPU:8, one launch (start us, length us, event | category | flops | bytes accessed | tf_op | source)
XLA Modules:
  0.0 377.0 jit_solution(827796356839516396)
XLA Ops:
  9.5 7.2 %collective-permute-start.10 = (bf16[128,3584]{1,0:T(8,128)(2,1)}, bf16[128,3584]{1,0:T(8,128)(2,1)}, u32[]{:S(2)}, u32[]{:S(2)}) collective-permute-start(bf16[128,3584]{1,0:T(8,128)(2,1)} %pad_maximum_fusion.4), channel_id=1, source_target_pairs={{0,8},{8,0},{1,9},{9,1},{2,10},{10,2},{3,11},{11,3},{4,12},{12,4},... | collective-permute-start | bytes 2752520 | tf_op jit(solution)/shard_map/ppermute | solution.py:30
  18.7 3.6 shard_map.162
  22.3 5.0 %all-to-all-start.1 = ((bf16[4,80,3584]{2,1,0:T(8,128)(2,1)}), bf16[4,80,3584]{2,1,0:T(8,128)(2,1)S(1)}, u32[]{:S(2)}, u32[]{:S(2)}) async-start(bf16[4,80,3584]{2,1,0:T(8,128)(2,1)} %bitcast.9), calls=%async_computation.1 | async-start | bytes 4587520 | tf_op jit(solution)/shard_map/all_to_all | solution.py:324
  28.7 27.0 %collective-permute-done.10 = bf16[128,3584]{1,0:T(8,128)(2,1)} collective-permute-done((bf16[128,3584]{1,0:T(8,128)(2,1)}, bf16[128,3584]{1,0:T(8,128)(2,1)}, u32[]{:S(2)}, u32[]{:S(2)}) %collective-permute-start.10) | collective-permute-done | bytes 917536 | tf_op jit(solution)/shard_map/ppermute | solution.py:30
  57.1 5.2 %all-to-all-start = ((bf16[4,80,3584]{2,1,0:T(8,128)(2,1)}), bf16[4,80,3584]{2,1,0:T(8,128)(2,1)}, u32[]{:S(2)}, u32[]{:S(2)}) async-start(bf16[4,80,3584]{2,1,0:T(8,128)(2,1)} %bitcast.7), calls=%async_computation | async-start | bytes 4587520 | tf_op jit(solution)/shard_map/all_to_all | solution.py:324
  63.7 2.6 collective-permute-start.11
  67.3 4.5 %collective-permute-start.7 = (bf16[80,3584]{1,0:T(8,128)(2,1)}, bf16[80,3584]{1,0:T(8,128)(2,1)S(1)}, u32[]{:S(2)}, u32[]{:S(2)}) collective-permute-start(bf16[80,3584]{1,0:T(8,128)(2,1)} %get-tuple-element.61), channel_id=1, source_target_pairs={{0,136},{4,140},{8,128},{12,132},{128,8},{132,12},{136,0},{140,4},... | collective-permute-start | bytes 1720328 | tf_op jit(solution)/shard_map/ppermute | solution.py:340
  71.8 26.1 %collective-permute-done.11 = bf16[128,3584]{1,0:T(8,128)(2,1)S(1)} collective-permute-done((bf16[128,3584]{1,0:T(8,128)(2,1)S(1)}, bf16[128,3584]{1,0:T(8,128)(2,1)S(1)}, u32[]{:S(2)}, u32[]{:S(2)}) %collective-permute-start.11) | collective-permute-done | bytes 917536 | tf_op jit(solution)/shard_map/ppermute | solution.py:30
  99.4 2.6 collective-permute-start.5
  102.0 3.6 collective-permute-start.6
  105.6 3.0 convolution_convert_fusion.2
  109.9 4.6 %collective-permute-start.2 = (bf16[80,3584]{1,0:T(8,128)(2,1)S(1)}, bf16[80,3584]{1,0:T(8,128)(2,1)S(1)}, u32[]{:S(2)}, u32[]{:S(2)}) collective-permute-start(bf16[80,3584]{1,0:T(8,128)(2,1)S(1)} %get-tuple-element.65), channel_id=1, source_target_pairs={{0,136},{4,140},{8,128},{12,132},{128,8},{132,12},{136,0},{140,4},... | collective-permute-start | bytes 1720328 | tf_op jit(solution)/shard_map/ppermute | solution.py:340
  114.5 3.9 %collective-permute-done.5 = bf16[80,3584]{1,0:T(8,128)(2,1)S(1)} collective-permute-done((bf16[80,3584]{1,0:T(8,128)(2,1)S(1)}, bf16[80,3584]{1,0:T(8,128)(2,1)S(1)}, u32[]{:S(2)}, u32[]{:S(2)}) %collective-permute-start.5) | collective-permute-done | bytes 573472 | tf_op jit(solution)/shard_map/ppermute | solution.py:340
  118.5 21.8 %collective-permute-done.6 = bf16[80,3584]{1,0:T(8,128)(2,1)S(1)} collective-permute-done((bf16[80,3584]{1,0:T(8,128)(2,1)S(1)}, bf16[80,3584]{1,0:T(8,128)(2,1)S(1)}, u32[]{:S(2)}, u32[]{:S(2)}) %collective-permute-start.6) | collective-permute-done | bytes 573472 | tf_op jit(solution)/shard_map/ppermute | solution.py:340
  140.5 14.9 %collective-permute-done.1 = bf16[80,3584]{1,0:T(8,128)(2,1)S(1)} collective-permute-done((bf16[80,3584]{1,0:T(8,128)(2,1)S(1)}, bf16[80,3584]{1,0:T(8,128)(2,1)S(1)}, u32[]{:S(2)}, u32[]{:S(2)}) %collective-permute-start.1) | collective-permute-done | bytes 573472 | tf_op jit(solution)/shard_map/ppermute | solution.py:340
  155.4 20.9 %collective-permute-done.2 = bf16[80,3584]{1,0:T(8,128)(2,1)S(1)} collective-permute-done((bf16[80,3584]{1,0:T(8,128)(2,1)S(1)}, bf16[80,3584]{1,0:T(8,128)(2,1)S(1)}, u32[]{:S(2)}, u32[]{:S(2)}) %collective-permute-start.2) | collective-permute-done | bytes 573472 | tf_op jit(solution)/shard_map/ppermute | solution.py:340
  181.1 4.4 %collective-permute-start.4 = (bf16[64,3584]{1,0:T(8,128)(2,1)}, bf16[64,3584]{1,0:T(8,128)(2,1)}, u32[]{:S(2)}, u32[]{:S(2)}) collective-permute-start(bf16[64,3584]{1,0:T(8,128)(2,1)} %get-tuple-element.30), channel_id=1, source_target_pairs={{0,8},{8,0},{1,9},{9,1},{2,10},{10,2},{3,11},{11,3},{4,12},{12,4},... | collective-permute-start | bytes 1376264 | tf_op jit(solution)/shard_map/ppermute | solution.py:30
  186.9 20.6 %shard_map.163 = (f32[320,3584]{1,0:T(8,128)}, bf16[320,3584]{1,0:T(8,128)(2,1)}, bf16[2,512,640]{2,1,0:T(8,128)(2,1)}) custom-call(bf16[320,3584]{1,0:T(8,128)(2,1)} %copy-done.4, bf16[320,3584]{1,0:T(8,128)(2,1)} %copy-done.12, bf16[320,3584]{1,0:T(8,128)(2,1)} %copy-done.5, bf16[320,3584]{1,0:T(8,128)(2,1)} %collective-permute-done.9.other_scaled_ref, ...), custom_call_target="tpu_custom_call" | custom-call | flops 7046430720 | bytes 36700160 | tf_op jit(solution)/shard_map/pallas_call | solution.py:205
  207.5 11.9 %shard_map.164 = bf16[8,128,3584]{2,1,0:T(8,128)(2,1)} custom-call(bf16[2,512,640]{2,1,0:T(8,128)(2,1)} %get-tuple-element.34.left_ref, bf16[320,3584]{1,0:T(8,128)(2,1)} %copy-done.4, bf16[320,3584]{1,0:T(8,128)(2,1)} %copy-done.12, bf16[320,3584]{1,0:T(8,128)(2,1)} %copy-done.5, bf16[320,3584]{1,0:T(8,128)(2,1)} %collective-permute-done.9.other_scaled_ref), custom_call_target="tpu_custom_call" | custom-call | bytes 1024 | tf_op jit(solution)/shard_map/pallas_call | solution.py:261
  220.7 3.5 collective-permute-done.13
  224.2 2.9 add_convert_fusion
  227.4 7.9 %collective-permute-start.14 = (bf16[80,3584]{1,0:T(8,128)(2,1)S(1)}, bf16[80,3584]{1,0:T(8,128)(2,1)S(1)}, u32[]{:S(2)}, u32[]{:S(2)}) collective-permute-start(bf16[80,3584]{1,0:T(8,128)(2,1)S(1)} %get-tuple-element.59), channel_id=1, source_target_pairs={{4,0},{8,4},{12,8},{0,12},{140,128},{128,132},{132,136},{136,140},... | collective-permute-start | bytes 1720328 | tf_op jit(solution)/shard_map/ppermute | solution.py:340
  238.6 3.4 collective-permute-start.12
  242.0 8.1 %collective-permute-done.14 = bf16[80,3584]{1,0:T(8,128)(2,1)S(1)} collective-permute-done((bf16[80,3584]{1,0:T(8,128)(2,1)S(1)}, bf16[80,3584]{1,0:T(8,128)(2,1)S(1)}, u32[]{:S(2)}, u32[]{:S(2)}) %collective-permute-start.14) | collective-permute-done | bytes 573472 | tf_op jit(solution)/shard_map/ppermute | solution.py:340
  250.1 45.7 %collective-permute-done.15 = bf16[80,3584]{1,0:T(8,128)(2,1)S(1)} collective-permute-done((bf16[80,3584]{1,0:T(8,128)(2,1)S(1)}, bf16[80,3584]{1,0:T(8,128)(2,1)S(1)}, u32[]{:S(2)}, u32[]{:S(2)}) %collective-permute-start.15) | collective-permute-done | bytes 573472 | tf_op jit(solution)/shard_map/ppermute | solution.py:340
  295.8 8.5 %collective-permute-done.16 = bf16[80,3584]{1,0:T(8,128)(2,1)S(1)} collective-permute-done((bf16[80,3584]{1,0:T(8,128)(2,1)S(1)}, bf16[80,3584]{1,0:T(8,128)(2,1)S(1)}, u32[]{:S(2)}, u32[]{:S(2)}) %collective-permute-start.16) | collective-permute-done | bytes 573472 | tf_op jit(solution)/shard_map/ppermute | solution.py:340
  304.5 2.8 convolution_convert_fusion
  307.3 5.1 %all-to-all-start.2 = ((bf16[4,80,3584]{2,1,0:T(8,128)(2,1)}), bf16[4,80,3584]{2,1,0:T(8,128)(2,1)}, u32[]{:S(2)}, u32[]{:S(2)}) async-start(bf16[4,80,3584]{2,1,0:T(8,128)(2,1)} %bitcast.87), calls=%async_computation.2 | async-start | bytes 4587520 | tf_op jit(solution)/shard_map/all_to_all | solution.py:324
  314.6 5.4 %collective-permute-start.18 = (bf16[128,3584]{1,0:T(8,128)(2,1)}, bf16[128,3584]{1,0:T(8,128)(2,1)}, u32[]{:S(2)}, u32[]{:S(2)}) collective-permute-start(bf16[128,3584]{1,0:T(8,128)(2,1)} %slice_bitcast_fusion), channel_id=1, source_target_pairs={{0,128},{128,0},{1,129},{129,1},{2,130},{130,2},{3,131},{131,3},{4... | collective-permute-start | bytes 2752520 | tf_op jit(solution)/shard_map/ppermute | solution.py:30
  321.6 39.2 %collective-permute-done.17 = bf16[64,3584]{1,0:T(8,128)(2,1)} collective-permute-done((bf16[64,3584]{1,0:T(8,128)(2,1)}, bf16[64,3584]{1,0:T(8,128)(2,1)}, u32[]{:S(2)}, u32[]{:S(2)}) %collective-permute-start.17) | collective-permute-done | bytes 458784 | tf_op jit(solution)/shard_map/ppermute | solution.py:30
  360.8 3.4 convolution_convert_fusion.3
  365.9 4.3 %fusion.30 = (f32[1,64,3584]{2,1,0:T(8,128)}, bf16[1,64,3584]{2,1,0:T(8,128)(2,1)}, f32[1,64,3584]{2,1,0:T(8,128)}, f32[1,64,3584]{2,1,0:T(8,128)}, bf16[1,64,3584]{2,1,0:T(8,128)(2,1)}, /*index=5*/f32[1,64,3584]{2,1,0:T(8,128)}) fusion(f32[128,3584]{1,0:T(8,128)S(1)} %convert_add_fusion, f32[1,64,3584]{2,1,0:T(8,128)S(1)} %copy-done.9, ...), kind=kLoop, calls=%fused_computation.68 | loop fusion | flops 8257536 | bytes 12845057 | tf_op jit(solution)/shard_map/broadcast_in_dim | solution.py:412
  (74 shorter events, 28.2 us)
Async XLA Ops:
  7.2 10.2 %copy-start = (bf16[128,3584]{1,0:T(8,128)(2,1)S(1)}, bf16[128,3584]{1,0:T(8,128)(2,1)}, u32[]{:S(2)}) copy-start(bf16[128,3584]{1,0:T(8,128)(2,1)} %tokens_ref.1) | copy-start | bytes 2752516
  7.2 10.2 %copy-start.1 = (bf16[128,3584]{1,0:T(8,128)(2,1)S(1)}, bf16[128,3584]{1,0:T(8,128)(2,1)}, u32[]{:S(2)}) copy-start(bf16[128,3584]{1,0:T(8,128)(2,1)} %out_grad_ref.1) | copy-start | bytes 2752516
  9.5 46.2 %collective-permute-start.10 = (bf16[128,3584]{1,0:T(8,128)(2,1)}, bf16[128,3584]{1,0:T(8,128)(2,1)}, u32[]{:S(2)}, u32[]{:S(2)}) collective-permute-start(bf16[128,3584]{1,0:T(8,128)(2,1)} %pad_maximum_fusion.4), channel_id=1, source_target_pairs={{0,8},{8,0},{1,9},{9,1},{2,10},{10,2},{3,11},{11,3},{4,12},{12,4},... | collective-permute-start | bytes 2752520 | tf_op jit(solution)/shard_map/ppermute | solution.py:30
  22.3 5.0 %copy-start.14 = (s32[16]{0:T(128)S(1)}, s32[16]{0:T(128)}, u32[]{:S(2)}) copy-start(s32[16]{0:T(128)} %param.15) | copy-start | bytes 196
  22.3 34.8 %all-to-all-start.1 = ((bf16[4,80,3584]{2,1,0:T(8,128)(2,1)}), bf16[4,80,3584]{2,1,0:T(8,128)(2,1)S(1)}, u32[]{:S(2)}, u32[]{:S(2)}) async-start(bf16[4,80,3584]{2,1,0:T(8,128)(2,1)} %bitcast.9), calls=%async_computation.1 | async-start | bytes 4587520 | tf_op jit(solution)/shard_map/all_to_all | solution.py:324
  57.1 42.2 %all-to-all-start = ((bf16[4,80,3584]{2,1,0:T(8,128)(2,1)}), bf16[4,80,3584]{2,1,0:T(8,128)(2,1)}, u32[]{:S(2)}, u32[]{:S(2)}) async-start(bf16[4,80,3584]{2,1,0:T(8,128)(2,1)} %bitcast.7), calls=%async_computation | async-start | bytes 4587520 | tf_op jit(solution)/shard_map/all_to_all | solution.py:324
  62.3 123.2 %all-gather.3.cloned.1.call-start = ((), (), s32[]{:S(2)}) async-start(), calls=%async_computation.5 | async-start | bytes 9175040 | tf_op jit(solution)/shard_map/all_gather | solution.py:357
  63.7 34.2 %collective-permute-start.11 = (bf16[128,3584]{1,0:T(8,128)(2,1)S(1)}, bf16[128,3584]{1,0:T(8,128)(2,1)S(1)}, u32[]{:S(2)}, u32[]{:S(2)}) collective-permute-start(bf16[128,3584]{1,0:T(8,128)(2,1)S(1)} %broadcast_select_fusion), channel_id=1, source_target_pairs={{0,128},{128,0},{1,129},{129,1},{2,130},{130,2},{3,131},{131,3},{4... | collective-permute-start | bytes 2752520 | tf_op jit(solution)/shard_map/ppermute | solution.py:30
  67.3 32.0 %collective-permute-start.7 = (bf16[80,3584]{1,0:T(8,128)(2,1)}, bf16[80,3584]{1,0:T(8,128)(2,1)S(1)}, u32[]{:S(2)}, u32[]{:S(2)}) collective-permute-start(bf16[80,3584]{1,0:T(8,128)(2,1)} %get-tuple-element.61), channel_id=1, source_target_pairs={{0,136},{4,140},{8,128},{12,132},{128,8},{132,12},{136,0},{140,4},... | collective-permute-start | bytes 1720328 | tf_op jit(solution)/shard_map/ppermute | solution.py:340
  99.3 213.1 %reduce-scatter.2.cloned.1.call-start = ((), (), s32[]{:S(2)}) async-start(), calls=%async_computation.4 | async-start | bytes 9175040 | tf_op jit(solution)/shard_map/reduce_scatter | solution.py:390
  99.4 19.1 %collective-permute-start.5 = (bf16[80,3584]{1,0:T(8,128)(2,1)S(1)}, bf16[80,3584]{1,0:T(8,128)(2,1)S(1)}, u32[]{:S(2)}, u32[]{:S(2)}) collective-permute-start(bf16[80,3584]{1,0:T(8,128)(2,1)S(1)} %get-tuple-element.63), channel_id=1, source_target_pairs={{0,4},{4,8},{8,12},{12,0},{128,140},{132,128},{136,132},{140,136},... | collective-permute-start | bytes 1720328 | tf_op jit(solution)/shard_map/ppermute | solution.py:340
  102.0 38.2 %collective-permute-start.6 = (bf16[80,3584]{1,0:T(8,128)(2,1)S(1)}, bf16[80,3584]{1,0:T(8,128)(2,1)S(1)}, u32[]{:S(2)}, u32[]{:S(2)}) collective-permute-start(bf16[80,3584]{1,0:T(8,128)(2,1)S(1)} %get-tuple-element.62), channel_id=1, source_target_pairs={{0,140},{4,128},{8,132},{12,136},{128,4},{132,8},{136,12},{140,0},... | collective-permute-start | bytes 1720328 | tf_op jit(solution)/shard_map/ppermute | solution.py:340
  108.9 31.7 %collective-permute-start = (bf16[80,3584]{1,0:T(8,128)(2,1)S(1)}, bf16[80,3584]{1,0:T(8,128)(2,1)S(1)}, u32[]{:S(2)}, u32[]{:S(2)}) collective-permute-start(bf16[80,3584]{1,0:T(8,128)(2,1)S(1)} %get-tuple-element.67), channel_id=1, source_target_pairs={{0,4},{4,8},{8,12},{12,0},{128,140},{132,128},{136,132},{140,136},... | collective-permute-start | bytes 1720328 | tf_op jit(solution)/shard_map/ppermute | solution.py:340
  109.6 45.8 %collective-permute-start.1 = (bf16[80,3584]{1,0:T(8,128)(2,1)S(1)}, bf16[80,3584]{1,0:T(8,128)(2,1)S(1)}, u32[]{:S(2)}, u32[]{:S(2)}) collective-permute-start(bf16[80,3584]{1,0:T(8,128)(2,1)S(1)} %get-tuple-element.66), channel_id=1, source_target_pairs={{0,140},{4,128},{8,132},{12,136},{128,4},{132,8},{136,12},{140,0},... | collective-permute-start | bytes 1720328 | tf_op jit(solution)/shard_map/ppermute | solution.py:340
  109.9 66.3 %collective-permute-start.2 = (bf16[80,3584]{1,0:T(8,128)(2,1)S(1)}, bf16[80,3584]{1,0:T(8,128)(2,1)S(1)}, u32[]{:S(2)}, u32[]{:S(2)}) collective-permute-start(bf16[80,3584]{1,0:T(8,128)(2,1)S(1)} %get-tuple-element.65), channel_id=1, source_target_pairs={{0,136},{4,140},{8,128},{12,132},{128,8},{132,12},{136,0},{140,4},... | collective-permute-start | bytes 1720328 | tf_op jit(solution)/shard_map/ppermute | solution.py:340
  140.4 36.0 %copy-start.4 = (bf16[320,3584]{1,0:T(8,128)(2,1)}, bf16[320,3584]{1,0:T(8,128)(2,1)S(1)}, u32[]{:S(2)}) copy-start(bf16[320,3584]{1,0:T(8,128)(2,1)S(1)} %pad_maximum_fusion.1.mine_ref) | copy-start | bytes 6881284
  140.4 45.1 %collective-permute-start.8 = (bf16[320,3584]{1,0:T(8,128)(2,1)S(1)}, bf16[320,3584]{1,0:T(8,128)(2,1)S(1)}, u32[]{:S(2)}, u32[]{:S(2)}) collective-permute-start(bf16[320,3584]{1,0:T(8,128)(2,1)S(1)} %pad_maximum_fusion.1.mine_ref), channel_id=1, source_target_pairs={{0,16},{16,0},{1,17},{17,1},{2,18},{18,2},{3,19},{19,3},{4,20},{20... | collective-permute-start | bytes 6881288 | tf_op jit(solution)/shard_map/ppermute | solution.py:30
  176.3 2.3 copy-start.10
  176.4 9.1 %copy-start.5 = (bf16[320,3584]{1,0:T(8,128)(2,1)}, bf16[320,3584]{1,0:T(8,128)(2,1)S(1)}, u32[]{:S(2)}) copy-start(bf16[320,3584]{1,0:T(8,128)(2,1)S(1)} %pad_maximum_fusion.mine_scaled_ref) | copy-start | bytes 6881284
  176.5 9.1 %collective-permute-start.9 = (bf16[320,3584]{1,0:T(8,128)(2,1)S(1)}, bf16[320,3584]{1,0:T(8,128)(2,1)}, u32[]{:S(2)}, u32[]{:S(2)}) collective-permute-start(bf16[320,3584]{1,0:T(8,128)(2,1)S(1)} %pad_maximum_fusion.mine_scaled_ref), channel_id=1, source_target_pairs={{0,16},{16,0},{1,17},{17,1},{2,18},{18,2},{3,19},{19,3},{4,20},{20... | collective-permute-start | bytes 6881288 | tf_op jit(solution)/shard_map/ppermute | solution.py:30
  179.6 39.9 %collective-permute-start.3 = (bf16[64,3584]{1,0:T(8,128)(2,1)}, bf16[64,3584]{1,0:T(8,128)(2,1)}, u32[]{:S(2)}, u32[]{:S(2)}) collective-permute-start(bf16[64,3584]{1,0:T(8,128)(2,1)} %get-tuple-element.29), channel_id=1, source_target_pairs={{0,8},{8,0},{1,9},{9,1},{2,10},{10,2},{3,11},{11,3},{4,12},{12,4},... | collective-permute-start | bytes 1376264 | tf_op jit(solution)/shard_map/ppermute | solution.py:30
  181.1 38.3 %collective-permute-start.4 = (bf16[64,3584]{1,0:T(8,128)(2,1)}, bf16[64,3584]{1,0:T(8,128)(2,1)}, u32[]{:S(2)}, u32[]{:S(2)}) collective-permute-start(bf16[64,3584]{1,0:T(8,128)(2,1)} %get-tuple-element.30), channel_id=1, source_target_pairs={{0,8},{8,0},{1,9},{9,1},{2,10},{10,2},{3,11},{11,3},{4,12},{12,4},... | collective-permute-start | bytes 1376264 | tf_op jit(solution)/shard_map/ppermute | solution.py:30
  219.5 4.7 %collective-permute-start.13 = (bf16[320,3584]{1,0:T(8,128)(2,1)}, bf16[320,3584]{1,0:T(8,128)(2,1)S(1)}, u32[]{:S(2)}, u32[]{:S(2)}) collective-permute-start(bf16[320,3584]{1,0:T(8,128)(2,1)} %get-tuple-element.38), channel_id=1, source_target_pairs={{0,16},{16,0},{1,17},{17,1},{2,18},{18,2},{3,19},{19,3},{4,20},{20... | collective-permute-start | bytes 6881288 | tf_op jit(solution)/shard_map/ppermute | solution.py:30
  227.2 10.6 %copy-start.7 = (f32[1,64,3584]{2,1,0:T(8,128)S(1)}, f32[1,64,3584]{2,1,0:T(8,128)}, u32[]{:S(2)}) copy-start(f32[1,64,3584]{2,1,0:T(8,128)} %param.21) | copy-start | bytes 2752516
  227.4 22.7 %collective-permute-start.14 = (bf16[80,3584]{1,0:T(8,128)(2,1)S(1)}, bf16[80,3584]{1,0:T(8,128)(2,1)S(1)}, u32[]{:S(2)}, u32[]{:S(2)}) collective-permute-start(bf16[80,3584]{1,0:T(8,128)(2,1)S(1)} %get-tuple-element.59), channel_id=1, source_target_pairs={{4,0},{8,4},{12,8},{0,12},{140,128},{128,132},{132,136},{136,140},... | collective-permute-start | bytes 1720328 | tf_op jit(solution)/shard_map/ppermute | solution.py:340
  235.3 60.5 %collective-permute-start.15 = (bf16[80,3584]{1,0:T(8,128)(2,1)S(1)}, bf16[80,3584]{1,0:T(8,128)(2,1)S(1)}, u32[]{:S(2)}, u32[]{:S(2)}) collective-permute-start(bf16[80,3584]{1,0:T(8,128)(2,1)S(1)} %get-tuple-element.58), channel_id=1, source_target_pairs={{140,0},{128,4},{132,8},{136,12},{4,128},{8,132},{12,136},{0,140},... | collective-permute-start | bytes 1720328 | tf_op jit(solution)/shard_map/ppermute | solution.py:340
  237.8 66.6 %collective-permute-start.16 = (bf16[80,3584]{1,0:T(8,128)(2,1)S(1)}, bf16[80,3584]{1,0:T(8,128)(2,1)S(1)}, u32[]{:S(2)}, u32[]{:S(2)}) collective-permute-start(bf16[80,3584]{1,0:T(8,128)(2,1)S(1)} %get-tuple-element.57), channel_id=1, source_target_pairs={{136,0},{140,4},{128,8},{132,12},{8,128},{12,132},{0,136},{4,140},... | collective-permute-start | bytes 1720328 | tf_op jit(solution)/shard_map/ppermute | solution.py:340
  238.6 65.9 %collective-permute-start.12 = (bf16[64,3584]{1,0:T(8,128)(2,1)S(1)}, bf16[64,3584]{1,0:T(8,128)(2,1)S(1)}, u32[]{:S(2)}, u32[]{:S(2)}) collective-permute-start(bf16[64,3584]{1,0:T(8,128)(2,1)S(1)} %bitcast_convert_fusion.2), channel_id=1, source_target_pairs={{0,8},{8,0},{1,9},{9,1},{2,10},{10,2},{3,11},{11,3},{4,12},{12,4},... | collective-permute-start | bytes 1376264 | tf_op jit(solution)/shard_map/ppermute | solution.py:30
  307.3 53.5 %all-to-all-start.2 = ((bf16[4,80,3584]{2,1,0:T(8,128)(2,1)}), bf16[4,80,3584]{2,1,0:T(8,128)(2,1)}, u32[]{:S(2)}, u32[]{:S(2)}) async-start(bf16[4,80,3584]{2,1,0:T(8,128)(2,1)} %bitcast.87), calls=%async_computation.2 | async-start | bytes 4587520 | tf_op jit(solution)/shard_map/all_to_all | solution.py:324
  314.6 49.6 %collective-permute-start.18 = (bf16[128,3584]{1,0:T(8,128)(2,1)}, bf16[128,3584]{1,0:T(8,128)(2,1)}, u32[]{:S(2)}, u32[]{:S(2)}) collective-permute-start(bf16[128,3584]{1,0:T(8,128)(2,1)} %slice_bitcast_fusion), channel_id=1, source_target_pairs={{0,128},{128,0},{1,129},{129,1},{2,130},{130,2},{3,131},{131,3},{4... | collective-permute-start | bytes 2752520 | tf_op jit(solution)/shard_map/ppermute | solution.py:30
  320.0 40.8 %collective-permute-start.17 = (bf16[64,3584]{1,0:T(8,128)(2,1)}, bf16[64,3584]{1,0:T(8,128)(2,1)}, u32[]{:S(2)}, u32[]{:S(2)}) collective-permute-start(bf16[64,3584]{1,0:T(8,128)(2,1)} %bitcast_convert_fusion.3), channel_id=1, source_target_pairs={{0,8},{8,0},{1,9},{9,1},{2,10},{10,2},{3,11},{11,3},{4,12},{12,4},... | collective-permute-start | bytes 1376264 | tf_op jit(solution)/shard_map/ppermute | solution.py:30
  360.8 3.4 copy-start.13
  (7 other events, 8.6 us)
Sparse Core Ops, SparseCore 0:
  99.5 78.1 all-gather.2
  219.6 79.2 reduce-scatter.1
